TPU v7x, 512 devices: a whole 4x8x8 slice. The times are simulated.
512 devices in a mesh: vec: 32 (over z_hi, y), space: 16 (over x, z_lo, core).
Axes of the slice: x: 4, y: 8, z: 8 (z_hi: 4, z_lo: 2; z = z_hi * 2 + z_lo), core: 2. Of those that a mesh axis runs over, the one named last changes fastest.
Arguments:
- perturbation: float32 [32, 6, 384, 512], P('vec', None, 'space'), may hold values from -40 to 40
- trajectory: bfloat16 [32, 3, 6, 384, 512], P('vec', None, None, 'space'), may hold values from -1.796875 to 1.796875
- step_order: int32 [32], replicated, may hold values from 0 to 31, each once
Outputs:
- ortho_vectors: float32 [32, 6, 384, 512], P('vec', None, 'space')
- upper_factor: float32 [32, 32], replicated
Inputs may be any that keep to these rules, and one draw needn't show every extreme that they name: `step_order`: each number appears once.
All inputs are finite; a program needn't handle non-finite values.
Results may differ from a plain program's by a relative error of at most 0.0003.
Values may be sent and summed in bfloat16 or wider, within the bound.
No kernel may reach another device: no remote copies, remote signals or barrier semaphores. Data moves between devices by JAX's collectives and lax.ppermute only.
A program may use at most 64 MiB of HBM per device.

v0:
```python
import jax
import jax.numpy as jnp
from jax import lax
from jax.sharding import PartitionSpec as P

STEPS = 2


GRAVITY_TOP = 1.0
GRAVITY_LOW = 0.5
DEPTH_TOP = 1.0
DEPTH_LOW = 1.0
CORIOLIS = 0.3
TIME_STEP = 0.25


def from_root(block, axis, source):
    block = jnp.where(lax.axis_index(axis) == source, block, jnp.zeros_like(block))
    return lax.psum(block, axis)


def with_halo(block, sides, width):
    for axis, dim in sides:
        count = lax.axis_size(axis)
        forward = [(i, i + 1) for i in range(count - 1)]
        forward.append((count - 1, 0))
        backward = [(target, source) for source, target in forward]
        low = lax.ppermute(
            lax.slice_in_dim(block, block.shape[dim] - width, None, axis=dim), axis, forward
        )
        high = lax.ppermute(lax.slice_in_dim(block, 0, width, axis=dim), axis, backward)
        block = jnp.concatenate([low, block, high], axis=dim)
    return block


def diff_x(field):
    return 0.5 * (field[..., 2:, :] - field[..., :-2, :])


def diff_y(field):
    return 0.5 * (jnp.roll(field, -1, -1) - jnp.roll(field, 1, -1))


def trimmed(field, amount):
    return field[..., amount : field.shape[-2] - amount, :]


def tangent(base_state, tangent_state):
    dp_top = GRAVITY_TOP * (tangent_state[..., 0, :, :] + tangent_state[..., 3, :, :])
    dp_low = dp_top + GRAVITY_LOW * tangent_state[..., 3, :, :]
    results = []
    for layer_num, (mean_depth, pressure) in enumerate(((DEPTH_TOP, dp_top), (DEPTH_LOW, dp_low))):
        offset = 3 * layer_num
        base_depth = base_state[offset] + mean_depth
        base_xvel = base_state[offset + 1]
        base_yvel = base_state[offset + 2]
        pert_depth = tangent_state[..., offset, :, :]
        pert_xvel = tangent_state[..., offset + 1, :, :]
        pert_yvel = tangent_state[..., offset + 2, :, :]
        depth_rate = -diff_x(base_depth * pert_xvel + pert_depth * base_xvel) - trimmed(
            diff_y(base_depth * pert_yvel + pert_depth * base_yvel), 1
        )
        xvel_rate = (
            -(trimmed(base_xvel, 1) * diff_x(pert_xvel) + trimmed(pert_xvel, 1) * diff_x(base_xvel))
            - trimmed(base_yvel * diff_y(pert_xvel) + pert_yvel * diff_y(base_xvel), 1)
            + CORIOLIS * trimmed(pert_yvel, 1)
            - diff_x(pressure)
        )
        yvel_rate = (
            -(trimmed(base_xvel, 1) * diff_x(pert_yvel) + trimmed(pert_xvel, 1) * diff_x(base_yvel))
            - trimmed(base_yvel * diff_y(pert_yvel) + pert_yvel * diff_y(base_yvel), 1)
            - CORIOLIS * trimmed(pert_xvel, 1)
            - trimmed(diff_y(pressure), 1)
        )
        results += [depth_rate, xvel_rate, yvel_rate]
    return jnp.stack(results, axis=-3)


def combine(section_num, anchor, current, change):
    if section_num == 0:
        return current + TIME_STEP * change
    if section_num == 1:
        return 0.75 * anchor + 0.25 * (current + TIME_STEP * change)
    return anchor / 3.0 + 2.0 / 3.0 * (current + TIME_STEP * change)


def body(perturbation, trajectory, step_order):
    vectors = perturbation.shape[0]
    rim_width = 1
    state = perturbation
    for step_num in range(STEPS):
        owner_index = step_order[step_num]
        shared = from_root(trajectory[0], "vec", owner_index)
        sections = with_halo(shared, (("space", 2),), rim_width).astype(jnp.float32)
        current = state
        for section_num in range(3):
            padded = with_halo(current, (("space", 2),), 1)
            change = tangent(sections[section_num], padded)
            current = combine(section_num, state, current, change)
        state = current
    entries = 6 * state.shape[2] * state.shape[3] * lax.axis_size("space")
    flat_cells = state.reshape(vectors, -1)
    columns = lax.all_to_all(flat_cells, "vec", split_axis=1, concat_axis=0, tiled=True)
    partial_value = lax.dot_general(
        columns,
        columns,
        (((1,), (1,)), ((), ())),
        precision=lax.Precision.HIGHEST,
        preferred_element_type=jnp.float32,
    )
    gram_matrix = lax.psum(partial_value, ("vec", "space")) / entries
    lower_factor = jnp.linalg.cholesky(gram_matrix)
    ortho = jax.scipy.linalg.solve_triangular(lower_factor, columns, lower=True)
    back_rows = lax.all_to_all(ortho, "vec", split_axis=0, concat_axis=1, tiled=True)
    return (back_rows.reshape(state.shape), jnp.transpose(lower_factor))


def solution(mesh):
    in_specs = (P("vec", None, "space", None), P("vec", None, None, "space", None), P())
    out_specs = (P("vec", None, "space", None), P())
    return jax.shard_map(body, mesh=mesh, in_specs=in_specs, out_specs=out_specs, check_vma=False)
```

profile of v0, /device:TPU:8, one launch (start us, length us, event | category | flops | bytes accessed | tf_op | source)
XLA Modules:
  0.0 569.7 jit_solution(5685851224571037565)
XLA Ops:
  7.2 1.0 fusion.591
  8.2 1.9 collective-permute-start.2
  10.1 5.9 %collective-permute-start.3 = (f32[1,6,1,512]{3,2,1,0:T(1,128)S(1)}, f32[1,6,1,512]{3,2,1,0:T(1,128)S(1)}, u32[]{:S(2)}, u32[]{:S(2)}) collective-permute-start(f32[1,6,1,512]{3,2,1,0:T(1,128)S(1)} %get-tuple-element.135), channel_id=1, source_target_pairs={{1,0},{2,1},{3,2},{4,3},{5,4},{6,5},{7,6},{8,7},{9,8},{10,9},{11,1... | collective-permute-start | bytes 36872 | tf_op jit(solution)/shard_map/ppermute | solution.py:31
  16.1 1.3 fusion.688
  18.7 2.0 select_bitcast_fusion.1
  21.2 313.1 %all-reduce.3.cloned.1.call-done = (bf16[3,6,24,512]{3,2,1,0:T(8,128)(2,1)}, bf16[3,6,24,512]{3,2,1,0:T(8,128)(2,1)}) async-done(((bf16[3,6,24,512]{3,2,1,0:T(8,128)(2,1)}, bf16[3,6,24,512]{3,2,1,0:T(8,128)(2,1)}), (bf16[3,6,24,512]{3,2,1,0:T(8,128)(2,1)}, bf16[3,6,24,512]{3,2,1,0:T(8,128)(2,1)})) %all-reduce.3.cloned.1.call-update) | async-done | bytes 884752 | tf_op jit(solution)/shard_map/psum | solution.py:19
  334.3 1.0 fusion.584
  335.4 1.9 collective-permute-start
  337.3 5.8 %collective-permute-start.1 = (bf16[3,6,1,512]{3,2,1,0:T(2,128)(2,1)S(1)}, bf16[3,6,1,512]{3,2,1,0:T(2,128)(2,1)S(1)}, u32[]{:S(2)}, u32[]{:S(2)}) collective-permute-start(bf16[3,6,1,512]{3,2,1,0:T(2,128)(2,1)S(1)} %get-tuple-element.83), channel_id=1, source_target_pairs={{1,0},{2,1},{3,2},{4,3},{5,4},{6,5},{7,6},{8,7},{9,8},{10,9},{11,1... | collective-permute-start | bytes 55304 | tf_op jit(solution)/shard_map/ppermute | solution.py:31
  343.1 1.0 fusion.585
  344.1 1.9 collective-permute-start.8
  346.0 5.8 %collective-permute-start.9 = (bf16[3,6,1,512]{3,2,1,0:T(2,128)(2,1)S(1)}, bf16[3,6,1,512]{3,2,1,0:T(2,128)(2,1)S(1)}, u32[]{:S(2)}, u32[]{:S(2)}) collective-permute-start(bf16[3,6,1,512]{3,2,1,0:T(2,128)(2,1)S(1)} %get-tuple-element.85), channel_id=1, source_target_pairs={{1,0},{2,1},{3,2},{4,3},{5,4},{6,5},{7,6},{8,7},{9,8},{10,9},{11,1... | collective-permute-start | bytes 55304 | tf_op jit(solution)/shard_map/ppermute | solution.py:31
  351.8 1.2 maximum_convert_fusion
  353.3 0.1 slice_bitcast_fusion.102
  354.8 0.4 copy-done.1
  355.2 0.2 maximum_convert_fusion.1
  355.4 0.1 slice_bitcast_fusion.84
  356.5 1.9 collective-permute-start.4
  358.4 5.8 %collective-permute-start.5 = (f32[1,6,1,512]{3,2,1,0:T(1,128)S(1)}, f32[1,6,1,512]{3,2,1,0:T(1,128)S(1)}, u32[]{:S(2)}, u32[]{:S(2)}) collective-permute-start(f32[1,6,1,512]{3,2,1,0:T(1,128)S(1)} %get-tuple-element.133), channel_id=1, source_target_pairs={{1,0},{2,1},{3,2},{4,3},{5,4},{6,5},{7,6},{8,7},{9,8},{10,9},{11,1... | collective-permute-start | bytes 36872 | tf_op jit(solution)/shard_map/ppermute | solution.py:31
  364.8 0.8 collective-permute-done.5
  367.9 1.9 collective-permute-start.6
  369.8 5.8 %collective-permute-start.7 = (f32[1,6,1,512]{3,2,1,0:T(1,128)S(1)}, f32[1,6,1,512]{3,2,1,0:T(1,128)S(1)}, u32[]{:S(2)}, u32[]{:S(2)}) collective-permute-start(f32[1,6,1,512]{3,2,1,0:T(1,128)S(1)} %get-tuple-element.131), channel_id=1, source_target_pairs={{1,0},{2,1},{3,2},{4,3},{5,4},{6,5},{7,6},{8,7},{9,8},{10,9},{11,1... | collective-permute-start | bytes 36872 | tf_op jit(solution)/shard_map/ppermute | solution.py:31
  375.7 1.3 collective-permute-done.7
  379.3 1.9 collective-permute-start.10
  381.2 5.8 %collective-permute-start.11 = (f32[1,6,1,512]{3,2,1,0:T(1,128)S(1)}, f32[1,6,1,512]{3,2,1,0:T(1,128)S(1)}, u32[]{:S(2)}, u32[]{:S(2)}) collective-permute-start(f32[1,6,1,512]{3,2,1,0:T(1,128)S(1)} %get-tuple-element.129), channel_id=1, source_target_pairs={{1,0},{2,1},{3,2},{4,3},{5,4},{6,5},{7,6},{8,7},{9,8},{10,9},{11,1... | collective-permute-start | bytes 36872 | tf_op jit(solution)/shard_map/ppermute | solution.py:31
  387.1 1.3 collective-permute-done.11
  390.0 0.1 constant_dynamic-update-slice_fusion.21
  390.6 1.9 collective-permute-start.12
  392.6 5.8 %collective-permute-start.13 = (f32[1,6,1,512]{3,2,1,0:T(1,128)S(1)}, f32[1,6,1,512]{3,2,1,0:T(1,128)S(1)}, u32[]{:S(2)}, u32[]{:S(2)}) collective-permute-start(f32[1,6,1,512]{3,2,1,0:T(1,128)S(1)} %get-tuple-element.127), channel_id=1, source_target_pairs={{1,0},{2,1},{3,2},{4,3},{5,4},{6,5},{7,6},{8,7},{9,8},{10,9},{11,1... | collective-permute-start | bytes 36872 | tf_op jit(solution)/shard_map/ppermute | solution.py:31
  398.4 1.3 collective-permute-done.13
  402.0 1.9 collective-permute-start.14
  403.9 5.8 %collective-permute-start.15 = (f32[1,6,1,512]{3,2,1,0:T(1,128)S(1)}, f32[1,6,1,512]{3,2,1,0:T(1,128)S(1)}, u32[]{:S(2)}, u32[]{:S(2)}) collective-permute-start(f32[1,6,1,512]{3,2,1,0:T(1,128)S(1)} %get-tuple-element.125), channel_id=1, source_target_pairs={{1,0},{2,1},{3,2},{4,3},{5,4},{6,5},{7,6},{8,7},{9,8},{10,9},{11,1... | collective-permute-start | bytes 36872 | tf_op jit(solution)/shard_map/ppermute | solution.py:31
  409.8 1.3 collective-permute-done.15
  413.4 0.3 all_to_all.22
  413.7 20.6 %all_to_all.29 = f32[1,32,2304]{2,0,1:T(1,128)S(1)} all-to-all(f32[1,32,2304]{2,0,1:T(1,128)S(1)} %all_to_all.22), channel_id=1, replica_groups=mesh['vec'=32,'space'=16] {'vec'}, dimensions={1} | all-to-all | bytes 589824 | tf_op jit(solution)/shard_map/all_to_all | solution.py:103
  434.4 0.4 fusion.1
  434.7 93.6 %psum.23 = f32[32,32]{0,1:T(8,128)S(1)} all-reduce(f32[32,32]{0,1:T(8,128)S(1)} %fusion.1), channel_id=1, replica_groups=mesh['vec'=32,'space'=16] {'vec','space'}, use_global_device_ids=true, to_apply=%region_2.3 | all-reduce | flops 1024 | bytes 8192 | tf_op jit(solution)/shard_map/psum | solution.py:111
  528.5 2.9 cholesky.16
  531.4 0.6 compare_reduce_fusion
  532.1 0.7 fusion.577
  532.7 2.4 custom-call.7
  535.2 0.5 convolution_bitcast_fusion
  535.6 1.0 copy.157
  536.6 9.3 %all-to-all-start.1 = ((f32[32,1,2304]{2,1,0:T(1,128)}), f32[32,1,2304]{2,1,0:T(1,128)S(1)}, u32[]{:S(2)}, u32[]{:S(2)}) async-start(f32[32,1,2304]{2,1,0:T(1,128)} %copy.157), calls=%async_computation.1 | async-start | bytes 589824 | tf_op jit(solution)/shard_map/all_to_all | solution.py:114
  545.9 0.7 copy.158
  546.6 14.8 %all-to-all-done.1 = f32[32,1,2304]{2,1,0:T(1,128)S(1)} async-done(((f32[32,1,2304]{2,1,0:T(1,128)}), f32[32,1,2304]{2,1,0:T(1,128)S(1)}, u32[]{:S(2)}, u32[]{:S(2)}) %all-to-all-start.1) | async-done | bytes 294944 | tf_op jit(solution)/shard_map/all_to_all | solution.py:114
  561.4 0.7 reduce.6
  562.1 0.8 reshape.7406
  (196 shorter events, 15.0 us)
Async XLA Ops:
  7.2 13.6 %copy-start = (f32[1,6,24,512]{3,2,1,0:T(8,128)S(1)}, f32[1,6,24,512]{3,2,1,0:T(8,128)}, u32[]{:S(2)}) copy-start(f32[1,6,24,512]{3,2,1,0:T(8,128)} %param.3) | copy-start | bytes 884740
  7.2 327.2 %all-reduce.3.cloned.1.call-start = ((), (), s32[]{:S(2)}) async-start(), calls=%async_computation.2 | async-start | bytes 1769472 | tf_op jit(solution)/shard_map/psum | solution.py:19
  8.2 12.5 %collective-permute-start.2 = (f32[1,6,1,512]{3,2,1,0:T(1,128)S(1)}, f32[1,6,1,512]{3,2,1,0:T(1,128)S(1)}, u32[]{:S(2)}, u32[]{:S(2)}) collective-permute-start(f32[1,6,1,512]{3,2,1,0:T(1,128)S(1)} %get-tuple-element.134), channel_id=1, source_target_pairs={{0,1},{1,2},{2,3},{3,4},{4,5},{5,6},{6,7},{7,8},{8,9},{9,10},{10,1... | collective-permute-start | bytes 36872 | tf_op jit(solution)/shard_map/ppermute | solution.py:28
  10.1 10.6 %collective-permute-start.3 = (f32[1,6,1,512]{3,2,1,0:T(1,128)S(1)}, f32[1,6,1,512]{3,2,1,0:T(1,128)S(1)}, u32[]{:S(2)}, u32[]{:S(2)}) collective-permute-start(f32[1,6,1,512]{3,2,1,0:T(1,128)S(1)} %get-tuple-element.135), channel_id=1, source_target_pairs={{1,0},{2,1},{3,2},{4,3},{5,4},{6,5},{7,6},{8,7},{9,8},{10,9},{11,1... | collective-permute-start | bytes 36872 | tf_op jit(solution)/shard_map/ppermute | solution.py:31
  335.4 16.4 %collective-permute-start = (bf16[3,6,1,512]{3,2,1,0:T(2,128)(2,1)S(1)}, bf16[3,6,1,512]{3,2,1,0:T(2,128)(2,1)S(1)}, u32[]{:S(2)}, u32[]{:S(2)}) collective-permute-start(bf16[3,6,1,512]{3,2,1,0:T(2,128)(2,1)S(1)} %get-tuple-element.82), channel_id=1, source_target_pairs={{0,1},{1,2},{2,3},{3,4},{4,5},{5,6},{6,7},{7,8},{8,9},{9,10},{10,1... | collective-permute-start | bytes 55304 | tf_op jit(solution)/shard_map/ppermute | solution.py:28
  337.3 14.5 %collective-permute-start.1 = (bf16[3,6,1,512]{3,2,1,0:T(2,128)(2,1)S(1)}, bf16[3,6,1,512]{3,2,1,0:T(2,128)(2,1)S(1)}, u32[]{:S(2)}, u32[]{:S(2)}) collective-permute-start(bf16[3,6,1,512]{3,2,1,0:T(2,128)(2,1)S(1)} %get-tuple-element.83), channel_id=1, source_target_pairs={{1,0},{2,1},{3,2},{4,3},{5,4},{6,5},{7,6},{8,7},{9,8},{10,9},{11,1... | collective-permute-start | bytes 55304 | tf_op jit(solution)/shard_map/ppermute | solution.py:31
  344.1 10.7 %collective-permute-start.8 = (bf16[3,6,1,512]{3,2,1,0:T(2,128)(2,1)S(1)}, bf16[3,6,1,512]{3,2,1,0:T(2,128)(2,1)S(1)}, u32[]{:S(2)}, u32[]{:S(2)}) collective-permute-start(bf16[3,6,1,512]{3,2,1,0:T(2,128)(2,1)S(1)} %get-tuple-element.84), channel_id=1, source_target_pairs={{0,1},{1,2},{2,3},{3,4},{4,5},{5,6},{6,7},{7,8},{8,9},{9,10},{10,1... | collective-permute-start | bytes 55304 | tf_op jit(solution)/shard_map/ppermute | solution.py:28
  346.0 8.7 %collective-permute-start.9 = (bf16[3,6,1,512]{3,2,1,0:T(2,128)(2,1)S(1)}, bf16[3,6,1,512]{3,2,1,0:T(2,128)(2,1)S(1)}, u32[]{:S(2)}, u32[]{:S(2)}) collective-permute-start(bf16[3,6,1,512]{3,2,1,0:T(2,128)(2,1)S(1)} %get-tuple-element.85), channel_id=1, source_target_pairs={{1,0},{2,1},{3,2},{4,3},{5,4},{6,5},{7,6},{8,7},{9,8},{10,9},{11,1... | collective-permute-start | bytes 55304 | tf_op jit(solution)/shard_map/ppermute | solution.py:31
  354.1 1.0 copy-start.1
  356.5 8.3 %collective-permute-start.4 = (f32[1,6,1,512]{3,2,1,0:T(1,128)S(1)}, f32[1,6,1,512]{3,2,1,0:T(1,128)S(1)}, u32[]{:S(2)}, u32[]{:S(2)}) collective-permute-start(f32[1,6,1,512]{3,2,1,0:T(1,128)S(1)} %get-tuple-element.132), channel_id=1, source_target_pairs={{0,1},{1,2},{2,3},{3,4},{4,5},{5,6},{6,7},{7,8},{8,9},{9,10},{10,1... | collective-permute-start | bytes 36872 | tf_op jit(solution)/shard_map/ppermute | solution.py:28
  358.4 7.1 %collective-permute-start.5 = (f32[1,6,1,512]{3,2,1,0:T(1,128)S(1)}, f32[1,6,1,512]{3,2,1,0:T(1,128)S(1)}, u32[]{:S(2)}, u32[]{:S(2)}) collective-permute-start(f32[1,6,1,512]{3,2,1,0:T(1,128)S(1)} %get-tuple-element.133), channel_id=1, source_target_pairs={{1,0},{2,1},{3,2},{4,3},{5,4},{6,5},{7,6},{8,7},{9,8},{10,9},{11,1... | collective-permute-start | bytes 36872 | tf_op jit(solution)/shard_map/ppermute | solution.py:31
  367.9 7.8 %collective-permute-start.6 = (f32[1,6,1,512]{3,2,1,0:T(1,128)S(1)}, f32[1,6,1,512]{3,2,1,0:T(1,128)S(1)}, u32[]{:S(2)}, u32[]{:S(2)}) collective-permute-start(f32[1,6,1,512]{3,2,1,0:T(1,128)S(1)} %get-tuple-element.130), channel_id=1, source_target_pairs={{0,1},{1,2},{2,3},{3,4},{4,5},{5,6},{6,7},{7,8},{8,9},{9,10},{10,1... | collective-permute-start | bytes 36872 | tf_op jit(solution)/shard_map/ppermute | solution.py:28
  369.8 7.1 %collective-permute-start.7 = (f32[1,6,1,512]{3,2,1,0:T(1,128)S(1)}, f32[1,6,1,512]{3,2,1,0:T(1,128)S(1)}, u32[]{:S(2)}, u32[]{:S(2)}) collective-permute-start(f32[1,6,1,512]{3,2,1,0:T(1,128)S(1)} %get-tuple-element.131), channel_id=1, source_target_pairs={{1,0},{2,1},{3,2},{4,3},{5,4},{6,5},{7,6},{8,7},{9,8},{10,9},{11,1... | collective-permute-start | bytes 36872 | tf_op jit(solution)/shard_map/ppermute | solution.py:31
  379.3 7.8 %collective-permute-start.10 = (f32[1,6,1,512]{3,2,1,0:T(1,128)S(1)}, f32[1,6,1,512]{3,2,1,0:T(1,128)S(1)}, u32[]{:S(2)}, u32[]{:S(2)}) collective-permute-start(f32[1,6,1,512]{3,2,1,0:T(1,128)S(1)} %get-tuple-element.128), channel_id=1, source_target_pairs={{0,1},{1,2},{2,3},{3,4},{4,5},{5,6},{6,7},{7,8},{8,9},{9,10},{10,1... | collective-permute-start | bytes 36872 | tf_op jit(solution)/shard_map/ppermute | solution.py:28
  381.2 7.1 %collective-permute-start.11 = (f32[1,6,1,512]{3,2,1,0:T(1,128)S(1)}, f32[1,6,1,512]{3,2,1,0:T(1,128)S(1)}, u32[]{:S(2)}, u32[]{:S(2)}) collective-permute-start(f32[1,6,1,512]{3,2,1,0:T(1,128)S(1)} %get-tuple-element.129), channel_id=1, source_target_pairs={{1,0},{2,1},{3,2},{4,3},{5,4},{6,5},{7,6},{8,7},{9,8},{10,9},{11,1... | collective-permute-start | bytes 36872 | tf_op jit(solution)/shard_map/ppermute | solution.py:31
  390.6 7.8 %collective-permute-start.12 = (f32[1,6,1,512]{3,2,1,0:T(1,128)S(1)}, f32[1,6,1,512]{3,2,1,0:T(1,128)S(1)}, u32[]{:S(2)}, u32[]{:S(2)}) collective-permute-start(f32[1,6,1,512]{3,2,1,0:T(1,128)S(1)} %get-tuple-element.126), channel_id=1, source_target_pairs={{0,1},{1,2},{2,3},{3,4},{4,5},{5,6},{6,7},{7,8},{8,9},{9,10},{10,1... | collective-permute-start | bytes 36872 | tf_op jit(solution)/shard_map/ppermute | solution.py:28
  392.6 7.1 %collective-permute-start.13 = (f32[1,6,1,512]{3,2,1,0:T(1,128)S(1)}, f32[1,6,1,512]{3,2,1,0:T(1,128)S(1)}, u32[]{:S(2)}, u32[]{:S(2)}) collective-permute-start(f32[1,6,1,512]{3,2,1,0:T(1,128)S(1)} %get-tuple-element.127), channel_id=1, source_target_pairs={{1,0},{2,1},{3,2},{4,3},{5,4},{6,5},{7,6},{8,7},{9,8},{10,9},{11,1... | collective-permute-start | bytes 36872 | tf_op jit(solution)/shard_map/ppermute | solution.py:31
  402.0 7.8 %collective-permute-start.14 = (f32[1,6,1,512]{3,2,1,0:T(1,128)S(1)}, f32[1,6,1,512]{3,2,1,0:T(1,128)S(1)}, u32[]{:S(2)}, u32[]{:S(2)}) collective-permute-start(f32[1,6,1,512]{3,2,1,0:T(1,128)S(1)} %get-tuple-element.124), channel_id=1, source_target_pairs={{0,1},{1,2},{2,3},{3,4},{4,5},{5,6},{6,7},{7,8},{8,9},{9,10},{10,1... | collective-permute-start | bytes 36872 | tf_op jit(solution)/shard_map/ppermute | solution.py:28
  403.9 7.1 %collective-permute-start.15 = (f32[1,6,1,512]{3,2,1,0:T(1,128)S(1)}, f32[1,6,1,512]{3,2,1,0:T(1,128)S(1)}, u32[]{:S(2)}, u32[]{:S(2)}) collective-permute-start(f32[1,6,1,512]{3,2,1,0:T(1,128)S(1)} %get-tuple-element.125), channel_id=1, source_target_pairs={{1,0},{2,1},{3,2},{4,3},{5,4},{6,5},{7,6},{8,7},{9,8},{10,9},{11,1... | collective-permute-start | bytes 36872 | tf_op jit(solution)/shard_map/ppermute | solution.py:31
  536.6 24.7 %all-to-all-start.1 = ((f32[32,1,2304]{2,1,0:T(1,128)}), f32[32,1,2304]{2,1,0:T(1,128)S(1)}, u32[]{:S(2)}, u32[]{:S(2)}) async-start(f32[32,1,2304]{2,1,0:T(1,128)} %copy.157), calls=%async_computation.1 | async-start | bytes 589824 | tf_op jit(solution)/shard_map/all_to_all | solution.py:114
Sparse Core Ops, SparseCore 0:
  20.8 313.4 all-reduce.2
where the time goes:
time: 571 us; the launch traced here: 570 us
  waiting for transfers between devices  334 us (58%)
  blocking collectives  114 us (20%)
  starting transfers between devices  70.9 us (12%)
  local copies, waits for them, and re-layouts  17.3 us (3%)
  other arithmetic  16.4 us (3%)
  between operations  16.1 us (3%)
    psum x1, waiting for transfers between devices, from_root(): return lax.psum(block, axis)  313 us
    psum x1, blocking collectives, body(): gram_matrix = lax.psum(partial_value, ('vec', 'space')) / entries  93.6 us
    ppermute x8, starting transfers between devices, with_halo(): lax.ppermute(lax.slice_in_dim(block, 0, width, axis=dim), axis, backward)  46.2 us
    all_to_all x1, blocking collectives, body(): lax.all_to_all(flat_cells, 'vec', split_axis=1, concat_axis=0, tiled=True)  20.6 us
    ppermute x8, starting transfers between devices, with_halo(): lax.ppermute(lax.slice_in_dim(block, block.shape[dim] - width, None, axis...  15.4 us
    all_to_all x1, waiting for transfers between devices, body(): lax.all_to_all(ortho, 'vec', split_axis=0, concat_axis=1, tiled=True)  14.8 us
  transfers between devices with their start and end apart: 18, of which 7 were waited for; matrix products, arithmetic and copies ran while one was open for 2% of the time, Pallas kernels for 0%

commit v1 on v0

v1 whole, which is shorter than its diff:
```python
import jax
import jax.numpy as jnp
from jax import lax
from jax.experimental import pallas as pl
from jax.experimental.pallas import tpu as pltpu
from jax.sharding import PartitionSpec as P

GRAVITY_TOP = 1.0
GRAVITY_LOW = 0.5
DEPTH = 1.0
CORIOLIS = 0.3
TIME_STEP = 0.25

ROWS = 24
HALO = 6
PAD = ROWS + 2 * HALO
PERT_TILES = 9
BASE_TILES = 14
TILES = PERT_TILES + BASE_TILES
STEP_ROWS = tuple(HALO - section for section in range(6))
BASE_HALO_ROWS = 6 * sum(STEP_ROWS)
STATE_HALO_ROWS = 6 * HALO * 8
HALO_ROWS = STATE_HALO_ROWS + BASE_HALO_ROWS + 2
COEF = 14
LIMIT = pltpu.CompilerParams(vmem_limit_bytes=40 * 1024 * 1024)


def roll_lanes(value, shift):
    shift %= value.shape[-1]
    return pltpu.roll(value, shift, 1) if shift else value


def roll_rows(value, shift):
    shift %= value.shape[0]
    return pltpu.roll(value, shift, 0) if shift else value


def lane_group(shape, size):
    return lax.broadcasted_iota(jnp.int32, shape, 1) // size


def quad_transpose(items, group):
    odd = (group % 2) == 1
    upper = group >= 2
    a, b, c, d = items
    a, b = jnp.where(odd, roll_lanes(b, 32), a), jnp.where(odd, b, roll_lanes(a, -32))
    c, d = jnp.where(odd, roll_lanes(d, 32), c), jnp.where(odd, d, roll_lanes(c, -32))
    a, c = jnp.where(upper, roll_lanes(c, 64), a), jnp.where(upper, c, roll_lanes(a, 64))
    b, d = jnp.where(upper, roll_lanes(d, 64), b), jnp.where(upper, d, roll_lanes(b, 64))
    return a, b, c, d


def pack_kernel(pert_ref, traj_ref, out_ref):
    group = lane_group((8, 128), 32)
    for parity in range(2):
        shift = 8 if parity == 0 else -8
        units = []
        for field in range(6):
            value = roll_lanes(pert_ref[field], shift)
            high = value.astype(jnp.bfloat16).astype(jnp.float32)
            low = value - high
            for tile in range(3):
                rows = slice(8 * tile, 8 * tile + 8)
                units += [high[rows], low[rows]]
        base = []
        for field in range(18):
            base.append(roll_lanes(traj_ref[field].astype(jnp.float32), shift))
        for tile in range(3):
            for field in range(18):
                units.append(base[field][8 * tile : 8 * tile + 8])
        while len(units) < 4 * TILES:
            units.append(jnp.zeros((8, 512), jnp.float32))
        for part in range(4):
            columns = slice(128 * part, 128 * part + 128)
            blocks = [[], [], [], []]
            for quad in range(TILES):
                four = [units[4 * quad + i][:, columns] for i in range(4)]
                for block, item in zip(blocks, quad_transpose(four, group)):
                    block.append(item)
            for position, block in enumerate(blocks):
                target = 2 * (4 * part + position) + parity
                out_ref[target] = jnp.concatenate(block, axis=0).astype(jnp.bfloat16)


def unpack_kernel(order_ref, in_ref, state_ref, base_ref, up_ref, down_ref, held_ref):
    rows = 8 * PERT_TILES
    group = lane_group((8, 128), 32)
    for vector in range(32):
        value = in_ref[vector, 0:80].astype(jnp.float32)[:rows]
        held_ref[rows * vector : rows * vector + rows] = value + roll_lanes(value, -32)
    for quad in range(PERT_TILES):
        for row in range(8):
            a, b, c, d = [
                held_ref[pl.ds(8 * rows * i + 8 * quad + row, 8, stride=rows), :] for i in range(4)
            ]
            first = jnp.where(
                group < 2,
                jnp.where(group == 0, a, roll_lanes(b, 32)),
                jnp.where(group == 2, roll_lanes(c, 64), roll_lanes(d, 96)),
            )
            second = jnp.where(
                group < 2,
                jnp.where(group == 0, roll_lanes(a, 64), roll_lanes(b, 96)),
                jnp.where(group == 2, c, roll_lanes(d, 32)),
            )
            for unit, item in ((2 * quad, first), (2 * quad + 1, second)):
                field, line = unit // 3, 8 * (unit % 3) + row
                state_ref[field, line] = item
                if line < HALO:
                    up_ref[pl.ds(8 * (HALO * field + line), 8)] = item
                if line >= ROWS - HALO:
                    down_ref[pl.ds(8 * (HALO * field + line - ROWS + HALO), 8)] = item
    source = lax.broadcasted_iota(jnp.int32, (128, 512), 0)
    target = lax.broadcasted_iota(jnp.int32, (128, 512), 1)
    spread = ((source % 32 == target % 32) & (source // 32 == target // 128)).astype(jnp.float32)
    spread = spread.astype(jnp.bfloat16)
    place = STATE_HALO_ROWS
    for step in range(2):
        block = in_ref[order_ref[step]].astype(jnp.float32)[8 * PERT_TILES :]
        wide = jnp.dot(block.astype(jnp.bfloat16), spread, preferred_element_type=jnp.float32)
        for unit in range(54):
            tile, field = unit // 18, unit % 18
            item = wide[8 * (unit // 4) : 8 * (unit // 4) + 8, 128 * (unit % 4) : 128 * (unit % 4) + 128]
            base_ref[18 * step + field, 8 * tile : 8 * tile + 8] = item
    for index in range(36):
        width = STEP_ROWS[index // 6]
        up_ref[place : place + width] = base_ref[index, 0:width]
        down_ref[place : place + width] = base_ref[index, ROWS - width : ROWS]
        place += width
    up_ref[place : place + 2] = jnp.zeros((2, 128), jnp.float32)
    down_ref[place : place + 2] = jnp.zeros((2, 128), jnp.float32)


def coefficients(fields, scale):
    results = []
    for layer in range(2):
        depth, xvel, yvel = fields[3 * layer : 3 * layer + 3]
        dx = lambda f: roll_rows(f, -1) - roll_rows(f, 1)
        dy = lambda f: roll_lanes(f, -1) - roll_lanes(f, 1)
        results += [
            scale * (depth + DEPTH),
            scale * xvel,
            scale * yvel,
            scale * dx(xvel),
            scale * dy(xvel) - TIME_STEP * CORIOLIS,
            scale * dx(yvel) + TIME_STEP * CORIOLIS,
            scale * dy(yvel),
        ]
    return results


def section_rows(cur_ref, anchor_ref, new_ref, coef_ref, first, section):
    scale = 0.5 * TIME_STEP
    kind = section % 3

    def coef(index, row):
        return coef_ref[first + index, row]

    def flux(layer, row):
        at = COEF // 2 * layer
        return (
            coef(at, row) * cur_ref[3 * layer + 1, row] + cur_ref[3 * layer, row] * coef(at + 1, row)
        )

    def pressure(row):
        low = cur_ref[3, row]
        top = (scale * GRAVITY_TOP) * (cur_ref[0, row] + low)
        return top, top + (scale * GRAVITY_LOW) * low

    def dy(value):
        return roll_lanes(value, -1) - roll_lanes(value, 1)

    def line(row):
        here, after, before = pressure(row), pressure(row + 1), pressure(row - 1)
        for layer in range(2):
            at = COEF // 2 * layer
            h, u, v = [cur_ref[3 * layer + i, row] for i in range(3)]
            depth, xvel, yvel, xvel_dx, xvel_dy, yvel_dx, yvel_dy = [coef(at + i, row) for i in range(7)]
            du = cur_ref[3 * layer + 1, row + 1] - cur_ref[3 * layer + 1, row - 1]
            dv = cur_ref[3 * layer + 2, row + 1] - cur_ref[3 * layer + 2, row - 1]
            h_new = h - (flux(layer, row + 1) - flux(layer, row - 1)) - dy(depth * v + h * yvel)
            u_new = u - (
                xvel * du + u * xvel_dx + yvel * dy(u) + v * xvel_dy + (after[layer] - before[layer])
            )
            v_new = v - (xvel * dv + u * yvel_dx + yvel * dy(v) + v * yvel_dy + dy(here[layer]))
            for i, value in enumerate((h_new, u_new, v_new)):
                if kind == 1:
                    value = 0.75 * anchor_ref[3 * layer + i, row] + 0.25 * value
                if kind == 2:
                    value = (1.0 / 3.0) * anchor_ref[3 * layer + i, row] + (2.0 / 3.0) * value
                new_ref[3 * layer + i, row] = value

    low, high = section + 1, PAD - 1 - section

    def pair(index, carry):
        line(low + 2 * index)
        line(low + 2 * index + 1)
        return carry

    lax.fori_loop(0, (high - low) // 2, pair, 0)


def step_kernel(
    state_ref, base_ref, top_ref, bottom_ref, cells_ref, gram_ref, start_ref, one_ref, two_ref, coef_ref
):
    for field in range(6):
        start_ref[field, HALO : HALO + ROWS] = state_ref[field]
        for line in range(HALO):
            at = 8 * (HALO * field + line)
            start_ref[field, line] = top_ref[at : at + 8]
            start_ref[field, HALO + ROWS + line] = bottom_ref[at : at + 8]
    place = STATE_HALO_ROWS
    for section in range(6):
        width = STEP_ROWS[section]
        fields = []
        for field in range(6):
            value = base_ref[6 * section + field]
            low = top_ref[place : place + width]
            high = bottom_ref[place : place + width]
            place += width
            fields.append(
                jnp.concatenate(
                    [value, high, jnp.zeros((16 - 2 * width, 128), jnp.float32), low], axis=0
                )
            )
        for index, value in enumerate(coefficients(fields, 0.5 * TIME_STEP)):
            for row in range(-width, ROWS + width):
                at = row % 40
                coef_ref[COEF * (section % 3) + index, HALO + row] = jnp.broadcast_to(
                    value[at : at + 1], (8, 128)
                )
        if section % 3 == 2:
            anchor = start_ref
            begin = section - 2
            section_rows(anchor, anchor, one_ref, coef_ref, 0, begin)
            section_rows(one_ref, anchor, two_ref, coef_ref, COEF, begin + 1)
            section_rows(two_ref, anchor, start_ref, coef_ref, 2 * COEF, begin + 2)
    block = lane_group((8, 128), 16)
    for unit in range(18):
        field, tile = unit // 3, unit % 3
        lines = [start_ref[field, HALO + 8 * tile + row] for row in range(8)]
        for quarter in range(4):
            total = None
            for row in range(8):
                moved = roll_lanes(lines[row], 16 * row - 32 * quarter - 8)
                total = moved if total is None else jnp.where(block == row, moved, total)
            cells_ref[8 * quarter : 8 * quarter + 8, 128 * unit : 128 * unit + 128] = total
    cells = cells_ref[...]
    gram = lax.dot_general(
        cells,
        cells,
        (((1,), (1,)), ((), ())),
        precision=lax.Precision.HIGHEST,
        preferred_element_type=jnp.float32,
    )
    compact = jnp.concatenate([gram[8 * i : 8 * i + 8] for i in range(4)], axis=1)
    for peer in range(gram_ref.shape[0]):
        gram_ref[peer] = compact


def sum_kernel(in_ref, out_ref):
    total = in_ref[0]
    for peer in range(1, in_ref.shape[0]):
        total = total + in_ref[peer]
    for peer in range(out_ref.shape[0]):
        out_ref[peer] = total


def solve_kernel(entries, parts_ref, cells_ref, ortho_ref, upper_ref):
    total = parts_ref[0]
    for peer in range(1, parts_ref.shape[0]):
        total = total + parts_ref[peer]
    total = total / entries
    lane = lax.broadcasted_iota(jnp.int32, (32, 128), 1)
    line = lax.broadcasted_iota(jnp.int32, (32, 128), 0)
    wide = jnp.concatenate([roll_lanes(total, -32 * i) for i in range(4)], axis=0)
    work = jnp.where(lane < 32, wide, jnp.where(lane == line + 32, 1.0, 0.0))
    roots = jnp.zeros((32, 128), jnp.float32)
    for k in range(32):
        row = work[k : k + 1]
        pivot = row[:, k : k + 1]
        factor = jnp.where(line[:, :1] > k, work[:, k : k + 1] / pivot, 0.0)
        roots = jnp.where(line == k, jnp.broadcast_to(pivot, (32, 128)), roots)
        work = work - factor * row
    work = work / jnp.sqrt(roots)
    upper_ref[...] = jnp.where(lane >= line, work, 0.0)[:, :32]
    inverse = roll_lanes(work, -32)[:, :32]
    ortho = jnp.dot(
        inverse, cells_ref[...], precision=lax.Precision.HIGHEST, preferred_element_type=jnp.float32
    )
    ortho_ref[...] = ortho.reshape(ortho_ref.shape)


def place_kernel(in_ref, out_ref):
    block = lane_group((8, 128), 16)
    line = lax.broadcasted_iota(jnp.int32, (8, 128), 0)
    distance = (block - line) % 8
    for unit in range(18):
        field, tile = unit // 3, unit % 3
        for part in range(4):
            value = in_ref[8 * part : 8 * part + 8, 0, 128 * unit : 128 * unit + 128]
            total = value
            for k in range(1, 8):
                moved = roll_rows(roll_lanes(value, 16 * k), -k)
                total = jnp.where(distance == k, moved, total)
            out_ref[field, 8 * tile : 8 * tile + 8, 128 * part : 128 * part + 128] = total


def call(kernel, out_shape, name, scratch=(), smem=0):
    specs = {}
    if smem:
        specs = dict(
            in_specs=[pl.BlockSpec(memory_space=pltpu.SMEM)] * smem
            + [pl.BlockSpec(memory_space=pltpu.VMEM)]
        )
    return pl.pallas_call(
        kernel, out_shape=out_shape, scratch_shapes=list(scratch), compiler_params=LIMIT, name=name, **specs
    )


def f32(*shape):
    return jax.ShapeDtypeStruct(shape, jnp.float32)


def body(perturbation, trajectory, step_order):
    vectors, tiles = lax.axis_size("vec"), lax.axis_size("space")
    sent = call(pack_kernel, jax.ShapeDtypeStruct((32, 8 * TILES, 128), jnp.bfloat16), "pack")(
        perturbation[0], trajectory[0].reshape(18, ROWS, 512)
    )
    held = lax.all_to_all(sent, "vec", split_axis=0, concat_axis=0, tiled=True)
    state, base, up, down = call(
        unpack_kernel,
        (f32(6, ROWS, 8, 128), f32(36, ROWS, 128), f32(HALO_ROWS, 128), f32(HALO_ROWS, 128)),
        "unpack",
        [pltpu.VMEM((32 * 8 * PERT_TILES, 128), jnp.float32)],
        smem=1,
    )(step_order, held)
    top = lax.ppermute(down, "space", [(i, (i + 1) % tiles) for i in range(tiles)])
    bottom = lax.ppermute(up, "space", [(i, (i - 1) % tiles) for i in range(tiles)])
    padded = pltpu.VMEM((6, PAD, 8, 128), jnp.float32)
    cells, gram = call(
        step_kernel,
        (f32(32, 2304), f32(tiles, 8, 128)),
        "steps",
        [padded, padded, padded, pltpu.VMEM((3 * COEF, PAD, 8, 128), jnp.float32)],
    )(state, base, top, bottom)
    gram = lax.all_to_all(gram, "space", split_axis=0, concat_axis=0, tiled=True)
    gram = call(sum_kernel, f32(vectors, 8, 128), "sums")(gram)
    gram = lax.all_to_all(gram, "vec", split_axis=0, concat_axis=0, tiled=True)
    entries = float(6 * ROWS * 512 * tiles)
    ortho, upper = call(
        lambda *refs: solve_kernel(entries, *refs), (f32(32, 1, 2304), f32(32, 32)), "solve"
    )(gram, cells)
    ortho = lax.all_to_all(ortho, "vec", split_axis=0, concat_axis=0, tiled=True)
    placed = call(place_kernel, f32(6, ROWS, 512), "place")(ortho)
    return placed[None], upper


def solution(mesh):
    in_specs = (P("vec", None, "space", None), P("vec", None, None, "space", None), P())
    out_specs = (P("vec", None, "space", None), P())
    return jax.shard_map(body, mesh=mesh, in_specs=in_specs, out_specs=out_specs, check_vma=False)
```

time: 571 us -> 149 us (0.26)
  waiting for transfers between devices: 334 us -> 3.34 us
  starting transfers between devices: 70.9 us -> 7.67 us
  Pallas kernels: 0 us -> 29.9 us
  other arithmetic: 16.4 us -> 0 us
  between operations: 16.1 us -> 0.68 us
  local copies, waits for them, and re-layouts: 17.3 us -> 1.97 us
  blocking collectives: 114 us -> 105 us
    psum x1 -> x0, waiting for transfers between devices: 313 us -> none  [from_root(): return lax.psum(block, axis)]
    psum x1 -> x0, blocking collectives: 93.6 us -> none  [body(): gram_matrix = lax.psum(partial_value, ('vec', 'space')) / entries]
    all_to_all x1 -> x4, blocking collectives: 20.6 us -> 105 us  [the longest x1 57.3 us: body(): held = lax.all_to_all(sent, 'vec', split_axis=0, concat_axis=0, tiled=True)]
    ppermute x16 -> x2, starting transfers between devices: 61.5 us -> 7.67 us  [the longest x1 5.75 us: body(): lax.ppermute(up, 'space', [(i, (i - 1) % tiles) for i in range(tiles)])]
    pallas_call x0 -> x6, Pallas kernels: none -> 29.9 us  [the longest x1 13 us: body(): call(pack_kernel, jax.ShapeDtypeStruct((32, 8 * TILES, 128), jnp.bfloat16...]
    all_to_all x1 -> x0, waiting for transfers between devices: 14.8 us -> none  [body(): lax.all_to_all(ortho, 'vec', split_axis=0, concat_axis=1, tiled=True)]
    slice x97 -> x0, local copies, waits for them, and re-layouts: 11.5 us -> none  [the longest x88 7 us: diff_y(): return 0.5 * (jnp.roll(field, -1, -1) - jnp.roll(field, 1, -1))]
    all_to_all x1 -> x0, starting transfers between devices: 9.28 us -> none  [body(): lax.all_to_all(ortho, 'vec', split_axis=0, concat_axis=1, tiled=True)]
  transfers between devices with their start and end apart: 18 -> 2, of which waited for: 7 -> 2; matrix products, arithmetic and copies ran while one was open for 2% -> 0% of each run, Pallas kernels for 0% -> 0%
where the time goes in v1:
time: 149 us
  blocking collectives  105 us (70%)
  Pallas kernels  29.9 us (20%)
  starting transfers between devices  7.67 us (5%)
  waiting for transfers between devices  3.34 us (2%)
  local copies, waits for them, and re-layouts  1.97 us (1%)
    all_to_all x1, blocking collectives, body(): held = lax.all_to_all(sent, 'vec', split_axis=0, concat_axis=0, tiled=True)  57.3 us
    all_to_all x1, blocking collectives, body(): lax.all_to_all(ortho, 'vec', split_axis=0, concat_axis=0, tiled=True)  18.5 us
    all_to_all x1, blocking collectives, body(): gram = lax.all_to_all(gram, 'vec', split_axis=0, concat_axis=0, tiled=True)  17.8 us
    pallas_call x1, Pallas kernels, body(): call(pack_kernel, jax.ShapeDtypeStruct((32, 8 * TILES, 128), jnp.bfloat16...  13 us
    all_to_all x1, blocking collectives, body(): lax.all_to_all(gram, 'space', split_axis=0, concat_axis=0, tiled=True)  11.4 us
    pallas_call x1, Pallas kernels, body(): call(step_kernel, (f32(32, 2304), f32(tiles, 8, 128)), 'steps', [padded,...  10.9 us
    ppermute x1, starting transfers between devices, body(): lax.ppermute(up, 'space', [(i, (i - 1) % tiles) for i in range(tiles)])  5.75 us
    pallas_call x1, Pallas kernels, body(): call(lambda *refs: solve_kernel(entries, *refs), (f32(32, 1, 2304), f32(3...  3.31 us
  transfers between devices with their start and end apart: 2, of which 2 were waited for; matrix products, arithmetic and copies ran while one was open for 0% of the time, Pallas kernels for 0%

profile of v1, /device:TPU:8, one launch (start us, length us, event | category | flops | bytes accessed | tf_op | source)
XLA Modules:
  0.0 148.6 jit_solution(9836502356815742806)
XLA Ops:
  0.6 0.0 copy-start
  0.6 1.0 copy-done
  1.6 0.0 copy-start.1
  1.6 1.0 copy-done.1
  2.6 13.0 %pack.1 = bf16[32,184,128]{2,1,0:T(8,128)(2,1)S(1)} custom-call(f32[6,24,512]{2,1,0:T(8,128)S(1)} %bitcast.4, bf16[18,24,512]{2,1,0:T(8,128)(2,1)S(1)} %bitcast.3), custom_call_target="tpu_custom_call" | custom-call | tf_op jit(solution)/shard_map/pack/pallas_call | solution.py:327
  15.6 0.0 copy-start.2
  15.6 57.3 %all_to_all.20.in_ref = bf16[32,184,128]{2,1,0:T(8,128)(2,1)S(1)} all-to-all(bf16[32,184,128]{2,1,0:T(8,128)(2,1)S(1)} %pack.1), channel_id=1, replica_groups=mesh['vec'=32,'space'=16] {'vec'}, dimensions={0} | all-to-all | bytes 3014656 | tf_op jit(solution)/shard_map/all_to_all | solution.py:330
  72.9 0.0 copy-done.2
  73.0 1.3 unpack.1
  74.3 1.9 %collective-permute-start = (f32[416,128]{1,0:T(8,128)S(1)}, f32[416,128]{1,0:T(8,128)S(1)}, u32[]{:S(2)}, u32[]{:S(2)}) collective-permute-start(f32[416,128]{1,0:T(8,128)S(1)} %get-tuple-element.12), channel_id=1, source_target_pairs={{0,1},{1,2},{2,3},{3,4},{4,5},{5,6},{6,7},{7,8},{8,9},{9,10},{10,1... | collective-permute-start | bytes 638984 | tf_op jit(solution)/shard_map/ppermute | solution.py:338
  76.2 5.8 %collective-permute-start.1 = (f32[416,128]{1,0:T(8,128)S(1)}, f32[416,128]{1,0:T(8,128)S(1)}, u32[]{:S(2)}, u32[]{:S(2)}) collective-permute-start(f32[416,128]{1,0:T(8,128)S(1)} %get-tuple-element.13), channel_id=1, source_target_pairs={{0,15},{1,0},{2,1},{3,2},{4,3},{5,4},{6,5},{7,6},{8,7},{9,8},{10,9... | collective-permute-start | bytes 638984 | tf_op jit(solution)/shard_map/ppermute | solution.py:339
  82.0 1.6 %collective-permute-done.top_ref = f32[416,128]{1,0:T(8,128)S(1)} collective-permute-done((f32[416,128]{1,0:T(8,128)S(1)}, f32[416,128]{1,0:T(8,128)S(1)}, u32[]{:S(2)}, u32[]{:S(2)}) %collective-permute-start) | collective-permute-done | bytes 213024 | tf_op jit(solution)/shard_map/ppermute | solution.py:338
  83.6 1.8 %collective-permute-done.1.bottom_ref = f32[416,128]{1,0:T(8,128)S(1)} collective-permute-done((f32[416,128]{1,0:T(8,128)S(1)}, f32[416,128]{1,0:T(8,128)S(1)}, u32[]{:S(2)}, u32[]{:S(2)}) %collective-permute-start.1) | collective-permute-done | bytes 213024 | tf_op jit(solution)/shard_map/ppermute | solution.py:339
  85.3 10.9 %steps.1 = (f32[32,2304]{1,0:T(8,128)S(1)}, f32[16,8,128]{2,1,0:T(8,128)S(1)}) custom-call(f32[6,24,8,128]{3,2,1,0:T(8,128)S(1)} %get-tuple-element.10.state_ref, f32[36,24,128]{2,1,0:T(8,128)S(1)} %get-tuple-element.11.base_ref, f32[416,128]{1,0:T(8,128)S(1)} %collective-permute-done.top_ref, f32[416,128]{1,0:T(8,128)S(1)} %collective-permute-done.1.bottom_ref), custom_call_target="tpu_custom_call" | custom-call | tf_op jit(solution)/shard_map/steps/pallas_call | solution.py:341
  96.2 11.4 %all_to_all.21.in_ref = f32[16,8,128]{2,1,0:T(8,128)S(1)} all-to-all(f32[16,8,128]{2,1,0:T(8,128)S(1)} %get-tuple-element.14), channel_id=1, replica_groups=mesh['vec'=32,'space'=16] {'space'}, dimensions={0} | all-to-all | bytes 131072 | tf_op jit(solution)/shard_map/all_to_all | solution.py:347
  107.6 17.8 %all_to_all.22.refs_0_ = f32[32,8,128]{2,1,0:T(8,128)S(1)} all-to-all(f32[32,8,128]{2,1,0:T(8,128)S(1)} %sums.1), channel_id=1, replica_groups=mesh['vec'=32,'space'=16] {'vec'}, dimensions={0} | all-to-all | bytes 262144 | tf_op jit(solution)/shard_map/all_to_all | solution.py:349
  125.4 3.3 %solve.1 = (f32[32,1,2304]{2,1,0:T(1,128)S(1)}, f32[32,32]{1,0:T(8,128)}) custom-call(f32[32,8,128]{2,1,0:T(8,128)S(1)} %all_to_all.22.refs_0_, f32[32,2304]{1,0:T(8,128)S(1)} %get-tuple-element.15.refs_1_), custom_call_target="tpu_custom_call" | custom-call | tf_op jit(solution)/shard_map/solve/pallas_call | solution.py:351
  128.8 18.5 %all_to_all.23.in_ref = f32[32,1,2304]{2,1,0:T(1,128)S(1)} all-to-all(f32[32,1,2304]{2,1,0:T(1,128)S(1)} %get-tuple-element.16), channel_id=1, replica_groups=mesh['vec'=32,'space'=16] {'vec'}, dimensions={0} | all-to-all | bytes 589824 | tf_op jit(solution)/shard_map/all_to_all | solution.py:354
  147.3 1.3 place.1
  (1 shorter events, 0.0 us)
Async XLA Ops:
  0.6 1.0 copy-start
  1.6 1.0 copy-start.1
  15.6 57.3 %copy-start.2 = (s32[32]{0:T(128)S(1)}, s32[32]{0:T(128)}, u32[]{:S(2)}) copy-start(s32[32]{0:T(128)} %order_ref.1) | copy-start | bytes 388
  74.3 9.3 %collective-permute-start = (f32[416,128]{1,0:T(8,128)S(1)}, f32[416,128]{1,0:T(8,128)S(1)}, u32[]{:S(2)}, u32[]{:S(2)}) collective-permute-start(f32[416,128]{1,0:T(8,128)S(1)} %get-tuple-element.12), channel_id=1, source_target_pairs={{0,1},{1,2},{2,3},{3,4},{4,5},{5,6},{6,7},{7,8},{8,9},{9,10},{10,1... | collective-permute-start | bytes 638984 | tf_op jit(solution)/shard_map/ppermute | solution.py:338
  76.2 9.1 %collective-permute-start.1 = (f32[416,128]{1,0:T(8,128)S(1)}, f32[416,128]{1,0:T(8,128)S(1)}, u32[]{:S(2)}, u32[]{:S(2)}) collective-permute-start(f32[416,128]{1,0:T(8,128)S(1)} %get-tuple-element.13), channel_id=1, source_target_pairs={{0,15},{1,0},{2,1},{3,2},{4,3},{5,4},{6,5},{7,6},{8,7},{9,8},{10,9... | collective-permute-start | bytes 638984 | tf_op jit(solution)/shard_map/ppermute | solution.py:339

commit v2 on v1

--- a/solution.py
+++ b/solution.py
@@ -14,9 +14,12 @@
 ROWS = 24
 HALO = 6
 PAD = ROWS + 2 * HALO
-PERT_TILES = 9
-BASE_TILES = 14
-TILES = PERT_TILES + BASE_TILES
+PERT_PAIRS = 9
+PAIRS = 36
+QUADS = PAIRS // 4
+BASE_QUAD = PERT_PAIRS // 4
+TOP_CODE = 32000.0
+BASE_SCALE = 16384.0
 STEP_ROWS = tuple(HALO - section for section in range(6))
 BASE_HALO_ROWS = 6 * sum(STEP_ROWS)
 STATE_HALO_ROWS = 6 * HALO * 8
@@ -50,78 +53,125 @@
     return a, b, c, d
 
 
-def pack_kernel(pert_ref, traj_ref, out_ref):
+def join(first, second):
+    return (first & 0xFFFF) | (second << 16)
+
+
+def halves(value):
+    return (value << 16) >> 16, value >> 16
+
+
+def to_code(value):
+    return jnp.round(value).astype(jnp.int32)
+
+
+def spacing(level):
+    return jnp.exp2(level.astype(jnp.float32) * 0.125)
+
+
+def pack_kernel(pert_hbm, traj_hbm, out_ref, pert_ref, traj_ref, pair_ref, sems):
+    copies = [
+        pltpu.make_async_copy(pert_hbm, pert_ref, sems.at[0]),
+        pltpu.make_async_copy(traj_hbm, traj_ref, sems.at[1]),
+    ]
+    for copy in copies:
+        copy.start()
+    copies[0].wait()
+    largest = jnp.abs(pert_ref[0, 0:8])
+    for field in range(6):
+        for tile in range(3):
+            largest = jnp.maximum(largest, jnp.abs(pert_ref[field, 8 * tile : 8 * tile + 8]))
+    largest = jnp.maximum(jnp.max(largest, axis=(0, 1), keepdims=True), 1e-30)
+    level = jnp.ceil(8.0 * jnp.log2(largest)).astype(jnp.int32)
+    inverse = jnp.broadcast_to(1.0 / spacing(level), (8, 512))
+    level = jnp.broadcast_to(level, (8, 512))
+    lane = lax.broadcasted_iota(jnp.int32, (8, 512), 1)
+    line = lax.broadcasted_iota(jnp.int32, (8, 512), 0)
+
+    def code(value):
+        size = jnp.minimum(TOP_CODE * jnp.sqrt(jnp.abs(value) * inverse), 32767.0)
+        return to_code(jnp.where(value < 0, -size, size))
+
+    for pair in range(PERT_PAIRS):
+        field, tile = pair // 3, pair % 3
+        first = code(pert_ref[field, 8 * tile : 8 * tile + 8])
+        second = code(pert_ref[field + 3, 8 * tile : 8 * tile + 8])
+        pair_ref[8 * pair : 8 * pair + 8] = join(first, second)
+    copies[1].wait()
+    for section in range(3):
+        for field in range(3):
+            value = [
+                to_code(traj_ref[6 * section + i].astype(jnp.float32) * BASE_SCALE)
+                for i in (field, field + 3)
+            ]
+            both = join(*value)
+            for tile in range(3):
+                pair = PERT_PAIRS + 9 * tile + 3 * section + field
+                pair_ref[8 * pair : 8 * pair + 8] = both[8 * tile : 8 * tile + 8]
     group = lane_group((8, 128), 32)
     for parity in range(2):
         shift = 8 if parity == 0 else -8
-        units = []
-        for field in range(6):
-            value = roll_lanes(pert_ref[field], shift)
-            high = value.astype(jnp.bfloat16).astype(jnp.float32)
-            low = value - high
-            for tile in range(3):
-                rows = slice(8 * tile, 8 * tile + 8)
-                units += [high[rows], low[rows]]
-        base = []
-        for field in range(18):
-            base.append(roll_lanes(traj_ref[field].astype(jnp.float32), shift))
-        for tile in range(3):
-            for field in range(18):
-                units.append(base[field][8 * tile : 8 * tile + 8])
-        while len(units) < 4 * TILES:
-            units.append(jnp.zeros((8, 512), jnp.float32))
-        for part in range(4):
-            columns = slice(128 * part, 128 * part + 128)
-            blocks = [[], [], [], []]
-            for quad in range(TILES):
-                four = [units[4 * quad + i][:, columns] for i in range(4)]
-                for block, item in zip(blocks, quad_transpose(four, group)):
-                    block.append(item)
-            for position, block in enumerate(blocks):
-                target = 2 * (4 * part + position) + parity
-                out_ref[target] = jnp.concatenate(block, axis=0).astype(jnp.bfloat16)
-
-
-def unpack_kernel(order_ref, in_ref, state_ref, base_ref, up_ref, down_ref, held_ref):
-    rows = 8 * PERT_TILES
+        for quad in range(QUADS):
+            items = []
+            for i in range(4):
+                pair = 4 * quad + i
+                item = roll_lanes(pair_ref[8 * pair : 8 * pair + 8], shift)
+                if pair == 0:
+                    item = jnp.where((lane % 32 == 0) & (line == 0), level, item)
+                items.append(item)
+            for part in range(4):
+                columns = slice(128 * part, 128 * part + 128)
+                four = quad_transpose([item[:, columns] for item in items], group)
+                for position, item in enumerate(four):
+                    target = 2 * (4 * part + position) + parity
+                    out_ref[target, 8 * quad : 8 * quad + 8] = item
+
+
+def unpack_kernel(order_ref, in_ref, state_ref, base_ref, up_ref, down_ref):
     group = lane_group((8, 128), 32)
-    for vector in range(32):
-        value = in_ref[vector, 0:80].astype(jnp.float32)[:rows]
-        held_ref[rows * vector : rows * vector + rows] = value + roll_lanes(value, -32)
-    for quad in range(PERT_TILES):
+    column = lax.broadcasted_iota(jnp.int32, (8, 128), 1) % 32
+    scale = None
+    for quad in range(BASE_QUAD + 1):
         for row in range(8):
-            a, b, c, d = [
-                held_ref[pl.ds(8 * rows * i + 8 * quad + row, 8, stride=rows), :] for i in range(4)
+            items = [
+                in_ref[pl.ds(8 * QUADS * 8 * i + 8 * quad + row, 8, stride=8 * QUADS), :]
+                for i in range(4)
             ]
-            first = jnp.where(
-                group < 2,
-                jnp.where(group == 0, a, roll_lanes(b, 32)),
-                jnp.where(group == 2, roll_lanes(c, 64), roll_lanes(d, 96)),
-            )
-            second = jnp.where(
-                group < 2,
-                jnp.where(group == 0, roll_lanes(a, 64), roll_lanes(b, 96)),
-                jnp.where(group == 2, c, roll_lanes(d, 32)),
-            )
-            for unit, item in ((2 * quad, first), (2 * quad + 1, second)):
-                field, line = unit // 3, 8 * (unit % 3) + row
-                state_ref[field, line] = item
-                if line < HALO:
-                    up_ref[pl.ds(8 * (HALO * field + line), 8)] = item
-                if line >= ROWS - HALO:
-                    down_ref[pl.ds(8 * (HALO * field + line - ROWS + HALO), 8)] = item
+            for position, both in enumerate(quad_transpose(items, group)):
+                pair = 4 * quad + position
+                if pair >= PERT_PAIRS:
+                    continue
+                first, second = halves(both)
+                if scale is None:
+                    level = jnp.where(column == 0, first, 0)
+                    for shift in (1, 2, 4, 8, 16):
+                        level = level + roll_lanes(level, shift)
+                    scale = spacing(level) * (1.0 / (TOP_CODE * TOP_CODE))
+                for layer, item in enumerate((first, second)):
+                    item = item.astype(jnp.float32)
+                    item = item * jnp.abs(item) * scale
+                    field, line = pair // 3 + 3 * layer, 8 * (pair % 3) + row
+                    state_ref[field, line] = item
+                    if line < HALO:
+                        up_ref[pl.ds(8 * (HALO * field + line), 8)] = item
+                    if line >= ROWS - HALO:
+                        down_ref[pl.ds(8 * (HALO * field + line - ROWS + HALO), 8)] = item
     source = lax.broadcasted_iota(jnp.int32, (128, 512), 0)
     target = lax.broadcasted_iota(jnp.int32, (128, 512), 1)
     spread = ((source % 32 == target % 32) & (source // 32 == target // 128)).astype(jnp.float32)
     spread = spread.astype(jnp.bfloat16)
+    begin, end = 8 * BASE_QUAD, 8 * QUADS
+    for step in range(2):
+        block = in_ref[pl.ds(pl.multiple_of(order_ref[step] * end, 8) + begin, end - begin), :]
+        for layer, part in enumerate(halves(block)):
+            part = part.astype(jnp.float32).astype(jnp.bfloat16)
+            wide = jnp.dot(part, spread, preferred_element_type=jnp.float32) * (1.0 / BASE_SCALE)
+            for unit in range(27):
+                tile, field = unit // 9, 6 * (unit % 9 // 3) + unit % 3 + 3 * layer
+                at = PERT_PAIRS + unit - 4 * BASE_QUAD
+                item = wide[8 * (at // 4) : 8 * (at // 4) + 8, 128 * (at % 4) : 128 * (at % 4) + 128]
+                base_ref[18 * step + field, 8 * tile : 8 * tile + 8] = item
     place = STATE_HALO_ROWS
-    for step in range(2):
-        block = in_ref[order_ref[step]].astype(jnp.float32)[8 * PERT_TILES :]
-        wide = jnp.dot(block.astype(jnp.bfloat16), spread, preferred_element_type=jnp.float32)
-        for unit in range(54):
-            tile, field = unit // 18, unit % 18
-            item = wide[8 * (unit // 4) : 8 * (unit // 4) + 8, 128 * (unit % 4) : 128 * (unit % 4) + 128]
-            base_ref[18 * step + field, 8 * tile : 8 * tile + 8] = item
     for index in range(36):
         width = STEP_ROWS[index // 6]
         up_ref[place : place + width] = base_ref[index, 0:width]
@@ -306,13 +356,10 @@
             out_ref[field, 8 * tile : 8 * tile + 8, 128 * part : 128 * part + 128] = total
 
 
-def call(kernel, out_shape, name, scratch=(), smem=0):
+def call(kernel, out_shape, name, scratch=(), spaces=None):
     specs = {}
-    if smem:
-        specs = dict(
-            in_specs=[pl.BlockSpec(memory_space=pltpu.SMEM)] * smem
-            + [pl.BlockSpec(memory_space=pltpu.VMEM)]
-        )
+    if spaces:
+        specs = dict(in_specs=[pl.BlockSpec(memory_space=space) for space in spaces])
     return pl.pallas_call(
         kernel, out_shape=out_shape, scratch_shapes=list(scratch), compiler_params=LIMIT, name=name, **specs
     )
@@ -324,17 +371,25 @@
 
 def body(perturbation, trajectory, step_order):
     vectors, tiles = lax.axis_size("vec"), lax.axis_size("space")
-    sent = call(pack_kernel, jax.ShapeDtypeStruct((32, 8 * TILES, 128), jnp.bfloat16), "pack")(
-        perturbation[0], trajectory[0].reshape(18, ROWS, 512)
-    )
+    sent = call(
+        pack_kernel,
+        jax.ShapeDtypeStruct((32, 8 * QUADS, 128), jnp.int32),
+        "pack",
+        [
+            pltpu.VMEM((6, ROWS, 512), jnp.float32),
+            pltpu.VMEM((18, ROWS, 512), jnp.bfloat16),
+            pltpu.VMEM((8 * PAIRS, 512), jnp.int32),
+            pltpu.SemaphoreType.DMA((2,)),
+        ],
+        spaces=(pl.ANY, pl.ANY),
+    )(perturbation[0], trajectory[0].reshape(18, ROWS, 512))
     held = lax.all_to_all(sent, "vec", split_axis=0, concat_axis=0, tiled=True)
     state, base, up, down = call(
         unpack_kernel,
         (f32(6, ROWS, 8, 128), f32(36, ROWS, 128), f32(HALO_ROWS, 128), f32(HALO_ROWS, 128)),
         "unpack",
-        [pltpu.VMEM((32 * 8 * PERT_TILES, 128), jnp.float32)],
-        smem=1,
-    )(step_order, held)
+        spaces=(pltpu.SMEM, pltpu.VMEM),
+    )(step_order, held.reshape(32 * 8 * QUADS, 128))
     top = lax.ppermute(down, "space", [(i, (i + 1) % tiles) for i in range(tiles)])
     bottom = lax.ppermute(up, "space", [(i, (i - 1) % tiles) for i in range(tiles)])
     padded = pltpu.VMEM((6, PAD, 8, 128), jnp.float32)

time: 149 us -> 135 us (0.906)
  blocking collectives: 105 us -> 98.2 us
  Pallas kernels: 29.9 us -> 23.3 us
    pallas_call x1, Pallas kernels: 13 us -> 6.12 us  [body(): call(pack_kernel, jax.ShapeDtypeStruct((32, 8 * QUADS, 128), jnp.int32),...]
    all_to_all x1, blocking collectives: 57.3 us -> 50.5 us  [body(): held = lax.all_to_all(sent, 'vec', split_axis=0, concat_axis=0, tiled=True)]
where the time goes in v2:
time: 135 us
  blocking collectives  98.2 us (73%)
  Pallas kernels  23.3 us (17%)
  starting transfers between devices  7.67 us (6%)
  waiting for transfers between devices  3.34 us (2%)
  local copies, waits for them, and re-layouts  1.97 us (1%)
    all_to_all x1, blocking collectives, body(): held = lax.all_to_all(sent, 'vec', split_axis=0, concat_axis=0, tiled=True)  50.5 us
    all_to_all x1, blocking collectives, body(): lax.all_to_all(ortho, 'vec', split_axis=0, concat_axis=0, tiled=True)  18.5 us
    all_to_all x1, blocking collectives, body(): gram = lax.all_to_all(gram, 'vec', split_axis=0, concat_axis=0, tiled=True)  17.7 us
    all_to_all x1, blocking collectives, body(): lax.all_to_all(gram, 'space', split_axis=0, concat_axis=0, tiled=True)  11.4 us
    pallas_call x1, Pallas kernels, body(): call(step_kernel, (f32(32, 2304), f32(tiles, 8, 128)), 'steps', [padded,...  10.9 us
    pallas_call x1, Pallas kernels, body(): call(pack_kernel, jax.ShapeDtypeStruct((32, 8 * QUADS, 128), jnp.int32),...  6.12 us
    ppermute x1, starting transfers between devices, body(): lax.ppermute(up, 'space', [(i, (i - 1) % tiles) for i in range(tiles)])  5.75 us
    pallas_call x1, Pallas kernels, body(): call(lambda *refs: solve_kernel(entries, *refs), (f32(32, 1, 2304), f32(3...  3.31 us
  transfers between devices with their start and end apart: 2, of which 2 were waited for; matrix products, arithmetic and copies ran while one was open for 0% of the time, Pallas kernels for 0%

profile of v2, /device:TPU:8, one launch (start us, length us, event | category | flops | bytes accessed | tf_op | source)
XLA Modules:
  0.0 135.1 jit_solution(13281103564814598602)
XLA Ops:
  0.6 0.0 copy-start
  0.6 1.0 copy-done
  1.6 0.0 copy-start.1
  1.6 1.0 copy-done.1
  2.6 6.1 %pack.1 = s32[32,72,128]{2,1,0:T(8,128)S(1)} custom-call(f32[6,24,512]{2,1,0:T(8,128)S(1)} %bitcast.6, bf16[18,24,512]{2,1,0:T(8,128)(2,1)S(1)} %bitcast.5), custom_call_target="tpu_custom_call" | custom-call | tf_op jit(solution)/shard_map/pack/pallas_call | solution.py:374
  8.7 0.0 copy-start.2
  8.7 50.5 %all_to_all.20 = s32[32,72,128]{2,1,0:T(8,128)S(1)} all-to-all(s32[32,72,128]{2,1,0:T(8,128)S(1)} %pack.1), channel_id=1, replica_groups=mesh['vec'=32,'space'=16] {'vec'}, dimensions={0} | all-to-all | bytes 2359296 | tf_op jit(solution)/shard_map/all_to_all | solution.py:386
  59.3 0.0 copy-done.2
  59.3 1.6 %unpack.1 = (f32[6,24,8,128]{3,2,1,0:T(8,128)S(1)}, f32[36,24,128]{2,1,0:T(8,128)S(1)}, f32[416,128]{1,0:T(8,128)S(1)}, f32[416,128]{1,0:T(8,128)S(1)}) custom-call(s32[32]{0:T(128)S(1)} %copy-done.2, s32[2304,128]{1,0:T(8,128)S(1)} %bitcast.4), custom_call_target="tpu_custom_call" | custom-call | tf_op jit(solution)/shard_map/unpack/pallas_call | solution.py:387
  60.9 1.9 %collective-permute-start = (f32[416,128]{1,0:T(8,128)S(1)}, f32[416,128]{1,0:T(8,128)S(1)}, u32[]{:S(2)}, u32[]{:S(2)}) collective-permute-start(f32[416,128]{1,0:T(8,128)S(1)} %get-tuple-element.12), channel_id=1, source_target_pairs={{0,1},{1,2},{2,3},{3,4},{4,5},{5,6},{6,7},{7,8},{8,9},{9,10},{10,1... | collective-permute-start | bytes 638984 | tf_op jit(solution)/shard_map/ppermute | solution.py:393
  62.8 5.8 %collective-permute-start.1 = (f32[416,128]{1,0:T(8,128)S(1)}, f32[416,128]{1,0:T(8,128)S(1)}, u32[]{:S(2)}, u32[]{:S(2)}) collective-permute-start(f32[416,128]{1,0:T(8,128)S(1)} %get-tuple-element.13), channel_id=1, source_target_pairs={{0,15},{1,0},{2,1},{3,2},{4,3},{5,4},{6,5},{7,6},{8,7},{9,8},{10,9... | collective-permute-start | bytes 638984 | tf_op jit(solution)/shard_map/ppermute | solution.py:394
  68.6 1.6 %collective-permute-done.top_ref = f32[416,128]{1,0:T(8,128)S(1)} collective-permute-done((f32[416,128]{1,0:T(8,128)S(1)}, f32[416,128]{1,0:T(8,128)S(1)}, u32[]{:S(2)}, u32[]{:S(2)}) %collective-permute-start) | collective-permute-done | bytes 213024 | tf_op jit(solution)/shard_map/ppermute | solution.py:393
  70.2 1.8 %collective-permute-done.1.bottom_ref = f32[416,128]{1,0:T(8,128)S(1)} collective-permute-done((f32[416,128]{1,0:T(8,128)S(1)}, f32[416,128]{1,0:T(8,128)S(1)}, u32[]{:S(2)}, u32[]{:S(2)}) %collective-permute-start.1) | collective-permute-done | bytes 213024 | tf_op jit(solution)/shard_map/ppermute | solution.py:394
  71.9 10.9 %steps.1 = (f32[32,2304]{1,0:T(8,128)S(1)}, f32[16,8,128]{2,1,0:T(8,128)S(1)}) custom-call(f32[6,24,8,128]{3,2,1,0:T(8,128)S(1)} %get-tuple-element.10.state_ref, f32[36,24,128]{2,1,0:T(8,128)S(1)} %get-tuple-element.11.base_ref, f32[416,128]{1,0:T(8,128)S(1)} %collective-permute-done.top_ref, f32[416,128]{1,0:T(8,128)S(1)} %collective-permute-done.1.bottom_ref), custom_call_target="tpu_custom_call" | custom-call | tf_op jit(solution)/shard_map/steps/pallas_call | solution.py:396
  82.8 11.4 %all_to_all.21.in_ref = f32[16,8,128]{2,1,0:T(8,128)S(1)} all-to-all(f32[16,8,128]{2,1,0:T(8,128)S(1)} %get-tuple-element.14), channel_id=1, replica_groups=mesh['vec'=32,'space'=16] {'space'}, dimensions={0} | all-to-all | bytes 131072 | tf_op jit(solution)/shard_map/all_to_all | solution.py:402
  94.2 17.7 %all_to_all.22.refs_0_ = f32[32,8,128]{2,1,0:T(8,128)S(1)} all-to-all(f32[32,8,128]{2,1,0:T(8,128)S(1)} %sums.1), channel_id=1, replica_groups=mesh['vec'=32,'space'=16] {'vec'}, dimensions={0} | all-to-all | bytes 262144 | tf_op jit(solution)/shard_map/all_to_all | solution.py:404
  111.9 3.3 %solve.1 = (f32[32,1,2304]{2,1,0:T(1,128)S(1)}, f32[32,32]{1,0:T(8,128)}) custom-call(f32[32,8,128]{2,1,0:T(8,128)S(1)} %all_to_all.22.refs_0_, f32[32,2304]{1,0:T(8,128)S(1)} %get-tuple-element.15.refs_1_), custom_call_target="tpu_custom_call" | custom-call | tf_op jit(solution)/shard_map/solve/pallas_call | solution.py:406
  115.2 18.5 %all_to_all.23.in_ref = f32[32,1,2304]{2,1,0:T(1,128)S(1)} all-to-all(f32[32,1,2304]{2,1,0:T(1,128)S(1)} %get-tuple-element.16), channel_id=1, replica_groups=mesh['vec'=32,'space'=16] {'vec'}, dimensions={0} | all-to-all | bytes 589824 | tf_op jit(solution)/shard_map/all_to_all | solution.py:409
  133.8 1.3 place.1
  (1 shorter events, 0.0 us)
Async XLA Ops:
  0.6 1.0 copy-start
  1.6 1.0 copy-start.1
  8.7 50.5 %copy-start.2 = (s32[32]{0:T(128)S(1)}, s32[32]{0:T(128)}, u32[]{:S(2)}) copy-start(s32[32]{0:T(128)} %order_ref.1) | copy-start | bytes 388
  60.9 9.3 %collective-permute-start = (f32[416,128]{1,0:T(8,128)S(1)}, f32[416,128]{1,0:T(8,128)S(1)}, u32[]{:S(2)}, u32[]{:S(2)}) collective-permute-start(f32[416,128]{1,0:T(8,128)S(1)} %get-tuple-element.12), channel_id=1, source_target_pairs={{0,1},{1,2},{2,3},{3,4},{4,5},{5,6},{6,7},{7,8},{8,9},{9,10},{10,1... | collective-permute-start | bytes 638984 | tf_op jit(solution)/shard_map/ppermute | solution.py:393
  62.8 9.1 %collective-permute-start.1 = (f32[416,128]{1,0:T(8,128)S(1)}, f32[416,128]{1,0:T(8,128)S(1)}, u32[]{:S(2)}, u32[]{:S(2)}) collective-permute-start(f32[416,128]{1,0:T(8,128)S(1)} %get-tuple-element.13), channel_id=1, source_target_pairs={{0,15},{1,0},{2,1},{3,2},{4,3},{5,4},{6,5},{7,6},{8,7},{9,8},{10,9... | collective-permute-start | bytes 638984 | tf_op jit(solution)/shard_map/ppermute | solution.py:394

commit v3 on v2

v3 whole, which is shorter than its diff:
```python
import jax
import jax.numpy as jnp
from jax import lax
from jax.experimental import pallas as pl
from jax.experimental.pallas import tpu as pltpu
from jax.sharding import PartitionSpec as P

GRAVITY_TOP = 1.0
GRAVITY_LOW = 0.5
DEPTH = 1.0
CORIOLIS = 0.3
TIME_STEP = 0.25

ROWS = 24
HALO = 6
PAD = ROWS + 2 * HALO
PERT_PAIRS = 9
PAIRS = 36
QUADS = PAIRS // 4
BASE_QUAD = PERT_PAIRS // 4
TOP_CODE = 32000.0
BASE_SCALE = 16384.0
STEP_ROWS = tuple(HALO - section for section in range(6))
BASE_HALO_ROWS = 6 * sum(STEP_ROWS)
STATE_HALO_ROWS = 6 * HALO * 8
HALO_ROWS = STATE_HALO_ROWS + BASE_HALO_ROWS + 2
COEF = 14


def roll_lanes(value, shift):
    shift %= value.shape[-1]
    return pltpu.roll(value, shift, 1) if shift else value


def roll_rows(value, shift):
    shift %= value.shape[0]
    return pltpu.roll(value, shift, 0) if shift else value


def lane_group(shape, size):
    return lax.broadcasted_iota(jnp.int32, shape, 1) // size


def quad_transposes(quads):
    group = lane_group((8, 128), 32)
    odd, upper = (group % 2) == 1, group >= 2
    moved = [(roll_lanes(b, 32), roll_lanes(a, -32), roll_lanes(d, 32), roll_lanes(c, -32)) for a, b, c, d in quads]
    quads = [
        (jnp.where(odd, p, a), jnp.where(odd, b, q), jnp.where(odd, r, c), jnp.where(odd, d, t))
        for (a, b, c, d), (p, q, r, t) in zip(quads, moved)
    ]
    moved = [tuple(roll_lanes(item, 64) for item in quad) for quad in quads]
    return [
        (jnp.where(upper, r, a), jnp.where(upper, t, b), jnp.where(upper, c, p), jnp.where(upper, d, q))
        for (a, b, c, d), (p, q, r, t) in zip(quads, moved)
    ]


def join(first, second):
    return (first & 0xFFFF) | (second << 16)


def halves(value):
    return (value << 16) >> 16, value >> 16


def to_code(value):
    return jnp.round(value).astype(jnp.int32)


def level_of(largest):
    return jnp.ceil(8.0 * jnp.log2(jnp.maximum(largest, 1e-30))).astype(jnp.int32)


def spacing(level):
    return jnp.exp2(level.astype(jnp.float32) * 0.125)


def root_code(value, inverse):
    size = jnp.minimum(TOP_CODE * jnp.sqrt(jnp.abs(value) * inverse), 32767.0)
    return to_code(jnp.where(value < 0, -size, size))


def from_root_code(code, scale):
    code = code.astype(jnp.float32)
    return code * jnp.abs(code) * scale


def code_scale(level):
    return spacing(level) * (1.0 / (TOP_CODE * TOP_CODE))


def pack_kernel(pert_hbm, traj_hbm, out_ref, pert_ref, traj_ref, pair_ref, sems):
    copies = [
        pltpu.make_async_copy(pert_hbm, pert_ref, sems.at[0]),
        pltpu.make_async_copy(traj_hbm, traj_ref, sems.at[1]),
    ]
    for copy in copies:
        copy.start()
    copies[0].wait()
    largest = jnp.abs(pert_ref[0, 0:8])
    for field in range(6):
        for tile in range(3):
            largest = jnp.maximum(largest, jnp.abs(pert_ref[field, 8 * tile : 8 * tile + 8]))
    level = level_of(jnp.max(largest, axis=(0, 1), keepdims=True))
    inverse = jnp.broadcast_to(1.0 / spacing(level), (8, 512))
    level = jnp.broadcast_to(level, (8, 512))
    lane = lax.broadcasted_iota(jnp.int32, (8, 512), 1)
    line = lax.broadcasted_iota(jnp.int32, (8, 512), 0)

    for pair in range(PERT_PAIRS):
        field, tile = pair // 3, pair % 3
        first = root_code(pert_ref[field, 8 * tile : 8 * tile + 8], inverse)
        second = root_code(pert_ref[field + 3, 8 * tile : 8 * tile + 8], inverse)
        pair_ref[8 * pair : 8 * pair + 8] = join(first, second)
    copies[1].wait()
    for section in range(3):
        for field in range(3):
            value = [
                to_code(traj_ref[6 * section + i].astype(jnp.float32) * BASE_SCALE)
                for i in (field, field + 3)
            ]
            both = join(*value)
            for tile in range(3):
                pair = PERT_PAIRS + 9 * tile + 3 * section + field
                pair_ref[8 * pair : 8 * pair + 8] = both[8 * tile : 8 * tile + 8]
    for begin in range(0, QUADS, 3):
        places, quads = [], []
        for quad in range(begin, begin + 3):
            raw = [pair_ref[8 * pair : 8 * pair + 8] for pair in range(4 * quad, 4 * quad + 4)]
            for parity in range(2):
                items = [roll_lanes(item, 8 if parity == 0 else -8) for item in raw]
                if quad == 0:
                    items[0] = jnp.where((lane % 32 == 0) & (line == 0), level, items[0])
                for part in range(4):
                    columns = slice(128 * part, 128 * part + 128)
                    places.append((8 * part + parity, 8 * quad))
                    quads.append([item[:, columns] for item in items])
        for (target, at), four in zip(places, quad_transposes(quads)):
            for position, item in enumerate(four):
                out_ref[target + 2 * position, at : at + 8] = item


def unpack_kernel(order_ref, in_ref, state_ref, base_ref, up_ref, down_ref):
    column = lax.broadcasted_iota(jnp.int32, (8, 128), 1) % 32
    scale = None
    for quad in range(BASE_QUAD + 1):
        rows = [
            [
                in_ref[pl.ds(8 * QUADS * 8 * i + 8 * quad + row, 8, stride=8 * QUADS), :]
                for i in range(4)
            ]
            for row in range(8)
        ]
        for row, four in enumerate(quad_transposes(rows)):
            for pair, both in enumerate(four, 4 * quad):
                if pair >= PERT_PAIRS:
                    continue
                first, second = halves(both)
                if scale is None:
                    level = jnp.where(column == 0, first, 0)
                    for shift in (1, 2, 4, 8, 16):
                        level = level + roll_lanes(level, shift)
                    scale = code_scale(level)
                for layer, item in enumerate((first, second)):
                    item = from_root_code(item, scale)
                    field, line = pair // 3 + 3 * layer, 8 * (pair % 3) + row
                    state_ref[field, line] = item
                    if line < HALO:
                        up_ref[pl.ds(8 * (HALO * field + line), 8)] = item
                    if line >= ROWS - HALO:
                        down_ref[pl.ds(8 * (HALO * field + line - ROWS + HALO), 8)] = item
    source = lax.broadcasted_iota(jnp.int32, (128, 512), 0)
    target = lax.broadcasted_iota(jnp.int32, (128, 512), 1)
    spread = ((source % 32 == target % 32) & (source // 32 == target // 128)).astype(jnp.float32)
    spread = spread.astype(jnp.bfloat16)
    begin, end = 8 * BASE_QUAD, 8 * QUADS
    for step in range(2):
        block = in_ref[pl.ds(pl.multiple_of(order_ref[step] * end, 8) + begin, end - begin), :]
        for layer, part in enumerate(halves(block)):
            part = part.astype(jnp.float32).astype(jnp.bfloat16)
            wide = jnp.dot(part, spread, preferred_element_type=jnp.float32) * (1.0 / BASE_SCALE)
            for unit in range(27):
                tile, field = unit // 9, 6 * (unit % 9 // 3) + unit % 3 + 3 * layer
                at = PERT_PAIRS + unit - 4 * BASE_QUAD
                item = wide[8 * (at // 4) : 8 * (at // 4) + 8, 128 * (at % 4) : 128 * (at % 4) + 128]
                base_ref[18 * step + field, 8 * tile : 8 * tile + 8] = item
    place = STATE_HALO_ROWS
    for index in range(36):
        width = STEP_ROWS[index // 6]
        up_ref[place : place + width] = base_ref[index, 0:width]
        down_ref[place : place + width] = base_ref[index, ROWS - width : ROWS]
        place += width
    up_ref[place : place + 2] = jnp.zeros((2, 128), jnp.float32)
    down_ref[place : place + 2] = jnp.zeros((2, 128), jnp.float32)


def coefficients(fields, scale):
    results = []
    dx = lambda f: roll_rows(f, -1) - roll_rows(f, 1)
    dy = lambda f: roll_lanes(f, -1) - roll_lanes(f, 1)
    for layer in range(2):
        depth, xvel, yvel = fields[3 * layer : 3 * layer + 3]
        results += [
            scale * (depth + DEPTH),
            scale * xvel,
            scale * yvel,
            scale * dx(xvel),
            scale * dy(xvel) - TIME_STEP * CORIOLIS,
            scale * dx(yvel) + TIME_STEP * CORIOLIS,
            scale * dy(yvel),
        ]
    return results


def section_rows(cur_ref, anchor_ref, new_ref, coef, section):
    scale = 0.5 * TIME_STEP
    kind = section % 3

    def dy(value):
        return roll_lanes(value, -1) - roll_lanes(value, 1)

    def block(row, count):
        span = range(-1, count + 1)
        h = [[cur_ref[3 * layer, row + i] for i in span] for layer in range(2)]
        top = [(scale * GRAVITY_TOP) * (h[0][i] + h[1][i]) for i in range(count + 2)]
        low = [top[i] + (scale * GRAVITY_LOW) * h[1][i] for i in range(count + 2)]
        for layer, pressure in enumerate((top, low)):
            at = COEF // 2 * layer
            u = [cur_ref[3 * layer + 1, row + i] for i in span]
            v = [cur_ref[3 * layer + 2, row + i] for i in span]
            depth = [coef(at, row + i) for i in span]
            xvel = [coef(at + 1, row + i) for i in span]
            flux = [depth[i] * u[i] + h[layer][i] * xvel[i] for i in range(count + 2)]
            for i in range(1, count + 1):
                line = row + i - 1
                h_i, u_i, v_i = h[layer][i], u[i], v[i]
                yvel, xvel_dx, xvel_dy, yvel_dx, yvel_dy = [coef(at + k, line) for k in range(2, 7)]
                h_new = h_i - (flux[i + 1] - flux[i - 1]) - dy(depth[i] * v_i + h_i * yvel)
                u_new = u_i - (
                    xvel[i] * (u[i + 1] - u[i - 1])
                    + u_i * xvel_dx
                    + yvel * dy(u_i)
                    + v_i * xvel_dy
                    + (pressure[i + 1] - pressure[i - 1])
                )
                v_new = v_i - (
                    xvel[i] * (v[i + 1] - v[i - 1])
                    + u_i * yvel_dx
                    + yvel * dy(v_i)
                    + v_i * yvel_dy
                    + dy(pressure[i])
                )
                for field, value in enumerate((h_new, u_new, v_new)):
                    field += 3 * layer
                    if kind == 1:
                        value = 0.75 * anchor_ref[field, line] + 0.25 * value
                    if kind == 2:
                        value = (1.0 / 3.0) * anchor_ref[field, line] + (2.0 / 3.0) * value
                    new_ref[field, line] = value

    block(section + 1, PAD - 2 - 2 * section)


def step_kernel(
    state_ref, base_ref, top_ref, bottom_ref, cells_ref, gram_ref, start_ref, one_ref, two_ref, coef_ref
):
    for field in range(6):
        start_ref[field, HALO : HALO + ROWS] = state_ref[field]
        for line in range(HALO):
            at = 8 * (HALO * field + line)
            start_ref[field, line] = top_ref[at : at + 8]
            start_ref[field, HALO + ROWS + line] = bottom_ref[at : at + 8]
    place = STATE_HALO_ROWS
    buffers = (start_ref, one_ref, two_ref, start_ref)
    for section in range(6):
        width = STEP_ROWS[section]
        fields = []
        for field in range(6):
            pieces = [
                top_ref[place : place + width],
                base_ref[6 * section + field],
                bottom_ref[place : place + width],
            ]
            if width < 8:
                pieces.append(jnp.zeros((16 - 2 * width, 128), jnp.float32))
            fields.append(jnp.concatenate(pieces, axis=0))
            place += width
        for index, value in enumerate(coefficients(fields, 0.5 * TIME_STEP)):
            coef_ref[index] = value

        def coef(index, row):
            return coef_ref[index, pl.ds(row - HALO + width, 8, stride=0), :]

        kind = section % 3
        section_rows(buffers[kind], start_ref, buffers[kind + 1], coef, section)
    block = lane_group((8, 128), 16)
    for unit in range(18):
        field, tile = unit // 3, unit % 3
        lines = [start_ref[field, HALO + 8 * tile + row] for row in range(8)]
        for quarter in range(4):
            total = None
            for row in range(8):
                moved = roll_lanes(lines[row], 16 * row - 32 * quarter - 8)
                total = moved if total is None else jnp.where(block == row, moved, total)
            cells_ref[8 * quarter : 8 * quarter + 8, 128 * unit : 128 * unit + 128] = total
    cells = cells_ref[...]
    gram = lax.dot_general(
        cells,
        cells,
        (((1,), (1,)), ((), ())),
        precision=lax.Precision.HIGHEST,
        preferred_element_type=jnp.float32,
    )
    compact = jnp.concatenate([gram[8 * i : 8 * i + 8] for i in range(4)], axis=1)
    for peer in range(gram_ref.shape[0]):
        gram_ref[peer] = compact


def sum_kernel(in_ref, out_ref):
    total = in_ref[0]
    for peer in range(1, in_ref.shape[0]):
        total = total + in_ref[peer]
    for peer in range(out_ref.shape[0]):
        out_ref[peer] = total


def solve_kernel(entries, parts_ref, cells_ref, ortho_ref, upper_ref):
    total = parts_ref[0]
    for peer in range(1, parts_ref.shape[0]):
        total = total + parts_ref[peer]
    total = total / entries
    lane = lax.broadcasted_iota(jnp.int32, (32, 128), 1)
    line = lax.broadcasted_iota(jnp.int32, (32, 128), 0)
    wide = jnp.concatenate([roll_lanes(total, -32 * i) for i in range(4)], axis=0)
    work = jnp.where(lane < 32, wide, jnp.where(lane == line + 32, 1.0, 0.0))
    roots = jnp.zeros((32, 128), jnp.float32)
    for k in range(32):
        row = work[k : k + 1]
        pivot = row[:, k : k + 1]
        factor = jnp.where(line[:, :1] > k, work[:, k : k + 1] / pivot, 0.0)
        roots = jnp.where(line == k, jnp.broadcast_to(pivot, (32, 128)), roots)
        work = work - factor * row
    work = work / jnp.sqrt(roots)
    upper_ref[...] = jnp.where(lane >= line, work, 0.0)[:, :32]
    inverse = roll_lanes(work, -32)[:, :32]
    ortho = jnp.dot(
        inverse, cells_ref[...], precision=lax.Precision.HIGHEST, preferred_element_type=jnp.float32
    )
    level = level_of(jnp.max(jnp.abs(ortho), axis=1, keepdims=True))
    code = root_code(ortho, 1.0 / spacing(level))
    half = ortho.shape[1] // 2
    both = join(code[:, :half], code[:, half:])
    ortho_ref[:, 0, :half] = both
    ortho_ref[:, 0, half:] = jnp.broadcast_to(level, (32, 128))


def place_kernel(in_ref, out_ref):
    block = lane_group((8, 128), 16)
    line = lax.broadcasted_iota(jnp.int32, (8, 128), 0)
    distance = (block - line) % 8
    for part in range(4):
        sources = slice(8 * part, 8 * part + 8)
        scale = code_scale(in_ref[sources, 0, 1152:1280])
        for pair in range(9):
            both = in_ref[sources, 0, 128 * pair : 128 * pair + 128]
            for unit, code in zip((pair, pair + 9), halves(both)):
                field, tile = unit // 3, unit % 3
                value = from_root_code(code, scale)
                total = value
                for k in range(1, 8):
                    moved = roll_rows(roll_lanes(value, 16 * k), -k)
                    total = jnp.where(distance == k, moved, total)
                out_ref[field, 8 * tile : 8 * tile + 8, 128 * part : 128 * part + 128] = total


def call(kernel, out_shape, name, scratch=(), spaces=None, vmem=40):
    specs = {}
    if spaces:
        specs = dict(in_specs=[pl.BlockSpec(memory_space=space) for space in spaces])
    return pl.pallas_call(
        kernel,
        out_shape=out_shape,
        scratch_shapes=list(scratch),
        compiler_params=pltpu.CompilerParams(vmem_limit_bytes=vmem * 1024 * 1024),
        name=name,
        **specs,
    )


def f32(*shape):
    return jax.ShapeDtypeStruct(shape, jnp.float32)


VEC = ("z_hi", "y")
SPACE = ("x", "z_lo", "core")
LINE = ("z_hi", "z_lo", "core")
PLANE = ("x", "y")


def body(perturbation, trajectory, step_order):
    tiles = lax.axis_size(SPACE)
    first, second = lax.axis_size(LINE), lax.axis_size(PLANE)
    sent = call(
        pack_kernel,
        jax.ShapeDtypeStruct((32, 8 * QUADS, 128), jnp.int32),
        "pack",
        [
            pltpu.VMEM((6, ROWS, 512), jnp.float32),
            pltpu.VMEM((18, ROWS, 512), jnp.bfloat16),
            pltpu.VMEM((8 * PAIRS, 512), jnp.int32),
            pltpu.SemaphoreType.DMA((2,)),
        ],
        spaces=(pltpu.HBM, pltpu.HBM),
        vmem=60,
    )(perturbation[0], trajectory[0].reshape(18, ROWS, 512))
    held = lax.all_to_all(sent, VEC, split_axis=0, concat_axis=0, tiled=True)
    state, base, up, down = call(
        unpack_kernel,
        (f32(6, ROWS, 8, 128), f32(36, ROWS, 128), f32(HALO_ROWS, 128), f32(HALO_ROWS, 128)),
        "unpack",
        spaces=(pltpu.SMEM, pltpu.VMEM),
    )(step_order, held.reshape(32 * 8 * QUADS, 128))
    top = lax.ppermute(down, SPACE, [(i, (i + 1) % tiles) for i in range(tiles)])
    bottom = lax.ppermute(up, SPACE, [(i, (i - 1) % tiles) for i in range(tiles)])
    padded = pltpu.VMEM((6, PAD, 8, 128), jnp.float32)
    cells, gram = call(
        step_kernel,
        (f32(32, 2304), f32(first, 8, 128)),
        "steps",
        [padded, padded, padded, pltpu.VMEM((COEF, ROWS + 16, 128), jnp.float32)],
    )(state, base, top, bottom)
    gram = lax.all_to_all(gram, LINE, split_axis=0, concat_axis=0, tiled=True)
    gram = call(sum_kernel, f32(second, 8, 128), "sums")(gram)
    gram = lax.all_to_all(gram, PLANE, split_axis=0, concat_axis=0, tiled=True)
    entries = float(6 * ROWS * 512 * tiles)
    ortho, upper = call(
        lambda *refs: solve_kernel(entries, *refs), (jax.ShapeDtypeStruct((32, 1, 1280), jnp.int32), f32(32, 32)), "solve"
    )(gram, cells)
    ortho = lax.all_to_all(ortho, VEC, split_axis=0, concat_axis=0, tiled=True)
    placed = call(place_kernel, f32(6, ROWS, 512), "place")(ortho)
    return placed[None], upper


def solution(mesh):
    fine = jax.sharding.Mesh(mesh.devices.reshape(4, 8, 4, 2, 2), VEC + SPACE)
    in_specs = (P(VEC, None, SPACE, None), P(VEC, None, None, SPACE, None), P())
    out_specs = (P(VEC, None, SPACE, None), P())
    return jax.shard_map(body, mesh=fine, in_specs=in_specs, out_specs=out_specs, check_vma=False)
```

time: 135 us -> 120 us (0.89)
  Pallas kernels: 23.3 us -> 13.6 us
  blocking collectives: 98.2 us -> 94.7 us
  local copies, waits for them, and re-layouts: 1.97 us -> 0.01 us
    pallas_call x3, Pallas kernels: 14.2 us -> 7.65 us  [the longest x1 4.2 us: body(): call(step_kernel, (f32(32, 2304), f32(first, 8, 128)), 'steps', [padded,...]
    all_to_all x4, blocking collectives: 98.2 us -> 94.7 us  [the longest x1 50.7 us: body(): held = lax.all_to_all(sent, VEC, split_axis=0, concat_axis=0, tiled=True)]
    pallas_call x1, Pallas kernels: 6.12 us -> 3.28 us  [body(): call(pack_kernel, jax.ShapeDtypeStruct((32, 8 * QUADS, 128), jnp.int32),...]
    unnamed x6 -> x2, local copies, waits for them, and re-layouts: 1.97 us -> 0.01 us
where the time goes in v3:
time: 120 us
  blocking collectives  94.7 us (79%)
  Pallas kernels  13.6 us (11%)
  starting transfers between devices  7.67 us (6%)
  waiting for transfers between devices  3.34 us (3%)
    all_to_all x1, blocking collectives, body(): held = lax.all_to_all(sent, VEC, split_axis=0, concat_axis=0, tiled=True)  50.7 us
    all_to_all x1, blocking collectives, body(): gram = lax.all_to_all(gram, PLANE, split_axis=0, concat_axis=0, tiled=True)  17.1 us
    all_to_all x1, blocking collectives, body(): ortho = lax.all_to_all(ortho, VEC, split_axis=0, concat_axis=0, tiled=True)  16.1 us
    all_to_all x1, blocking collectives, body(): gram = lax.all_to_all(gram, LINE, split_axis=0, concat_axis=0, tiled=True)  10.7 us
    ppermute x1, starting transfers between devices, body(): lax.ppermute(up, SPACE, [(i, (i - 1) % tiles) for i in range(tiles)])  5.75 us
    pallas_call x1, Pallas kernels, body(): call(step_kernel, (f32(32, 2304), f32(first, 8, 128)), 'steps', [padded,...  4.2 us
    pallas_call x1, Pallas kernels, body(): call(lambda *refs: solve_kernel(entries, *refs), (jax.ShapeDtypeStruct((3...  3.43 us
    pallas_call x1, Pallas kernels, body(): call(pack_kernel, jax.ShapeDtypeStruct((32, 8 * QUADS, 128), jnp.int32),...  3.28 us
  transfers between devices with their start and end apart: 2, of which 2 were waited for; matrix products, arithmetic and copies ran while one was open for 0% of the time, Pallas kernels for 0%

profile of v3, /device:TPU:8, one launch (start us, length us, event | category | flops | bytes accessed | tf_op | source)
XLA Modules:
  0.0 120.0 jit_solution(5597348876963804268)
XLA Ops:
  0.6 3.3 %pack.1 = s32[32,72,128]{2,1,0:T(8,128)} custom-call(f32[6,24,512]{2,1,0:T(8,128)} %bitcast.7, bf16[18,24,512]{2,1,0:T(8,128)(2,1)} %bitcast.5), custom_call_target="tpu_custom_call" | custom-call | tf_op jit(solution)/shard_map/pack/pallas_call | solution.py:404
  3.9 0.0 copy-start
  3.9 50.7 %all_to_all.20 = s32[32,72,128]{2,1,0:T(8,128)S(1)} all-to-all(s32[32,72,128]{2,1,0:T(8,128)} %pack.1), channel_id=1, replica_groups=mesh['z_hi'=4,'y'=8,'x'=4,'z_lo'=2,'core'=2] {'z_hi','y'}, dimensions={0} | all-to-all | bytes 2359296 | tf_op jit(solution)/shard_map/all_to_all | solution.py:417
  54.7 0.0 copy-done
  54.7 1.2 unpack.1
  55.8 1.9 %collective-permute-start = (f32[416,128]{1,0:T(8,128)S(1)}, f32[416,128]{1,0:T(8,128)S(1)}, u32[]{:S(2)}, u32[]{:S(2)}) collective-permute-start(f32[416,128]{1,0:T(8,128)S(1)} %get-tuple-element.12), channel_id=1, source_target_pairs={{0,1},{1,2},{2,3},{3,4},{4,5},{5,6},{6,7},{7,8},{8,9},{9,10},{10,1... | collective-permute-start | bytes 638984 | tf_op jit(solution)/shard_map/ppermute | solution.py:424
  57.8 5.8 %collective-permute-start.1 = (f32[416,128]{1,0:T(8,128)S(1)}, f32[416,128]{1,0:T(8,128)S(1)}, u32[]{:S(2)}, u32[]{:S(2)}) collective-permute-start(f32[416,128]{1,0:T(8,128)S(1)} %get-tuple-element.13), channel_id=1, source_target_pairs={{0,15},{1,0},{2,1},{3,2},{4,3},{5,4},{6,5},{7,6},{8,7},{9,8},{10,9... | collective-permute-start | bytes 638984 | tf_op jit(solution)/shard_map/ppermute | solution.py:425
  63.5 1.6 %collective-permute-done.top_ref = f32[416,128]{1,0:T(8,128)S(1)} collective-permute-done((f32[416,128]{1,0:T(8,128)S(1)}, f32[416,128]{1,0:T(8,128)S(1)}, u32[]{:S(2)}, u32[]{:S(2)}) %collective-permute-start) | collective-permute-done | bytes 213024 | tf_op jit(solution)/shard_map/ppermute | solution.py:424
  65.1 1.8 %collective-permute-done.1.bottom_ref = f32[416,128]{1,0:T(8,128)S(1)} collective-permute-done((f32[416,128]{1,0:T(8,128)S(1)}, f32[416,128]{1,0:T(8,128)S(1)}, u32[]{:S(2)}, u32[]{:S(2)}) %collective-permute-start.1) | collective-permute-done | bytes 213024 | tf_op jit(solution)/shard_map/ppermute | solution.py:425
  66.9 4.2 %steps.1 = (f32[32,2304]{1,0:T(8,128)S(1)}, f32[16,8,128]{2,1,0:T(8,128)S(1)}) custom-call(f32[6,24,8,128]{3,2,1,0:T(8,128)S(1)} %get-tuple-element.10.state_ref, f32[36,24,128]{2,1,0:T(8,128)S(1)} %get-tuple-element.11.base_ref, f32[416,128]{1,0:T(8,128)S(1)} %collective-permute-done.top_ref, f32[416,128]{1,0:T(8,128)S(1)} %collective-permute-done.1.bottom_ref), custom_call_target="tpu_custom_call" | custom-call | tf_op jit(solution)/shard_map/steps/pallas_call | solution.py:427
  71.1 10.7 %all_to_all.21.in_ref = f32[16,8,128]{2,1,0:T(8,128)S(1)} all-to-all(f32[16,8,128]{2,1,0:T(8,128)S(1)} %get-tuple-element.14), channel_id=1, replica_groups=mesh['z_hi'=4,'y'=8,'x'=4,'z_lo'=2,'core'=2] {'z_hi','z_lo','core'}, dimensions={0} | all-to-all | bytes 131072 | tf_op jit(solution)/shard_map/all_to_all | solution.py:433
  81.8 17.1 %all_to_all.22.refs_0_ = f32[32,8,128]{2,1,0:T(8,128)S(1)} all-to-all(f32[32,8,128]{2,1,0:T(8,128)S(1)} %sums.1), channel_id=1, replica_groups=mesh['z_hi'=4,'y'=8,'x'=4,'z_lo'=2,'core'=2] {'x','y'}, dimensions={0} | all-to-all | bytes 262144 | tf_op jit(solution)/shard_map/all_to_all | solution.py:435
  98.9 3.4 %solve.1 = (s32[32,1,1280]{2,1,0:T(1,128)S(1)}, f32[32,32]{1,0:T(8,128)}) custom-call(f32[32,8,128]{2,1,0:T(8,128)S(1)} %all_to_all.22.refs_0_, f32[32,2304]{1,0:T(8,128)S(1)} %get-tuple-element.15.refs_1_), custom_call_target="tpu_custom_call" | custom-call | tf_op jit(solution)/shard_map/solve/pallas_call | solution.py:437
  102.4 16.1 %all_to_all.23.in_ref = s32[32,1,1280]{2,1,0:T(1,128)S(1)} all-to-all(s32[32,1,1280]{2,1,0:T(1,128)S(1)} %get-tuple-element.16), channel_id=1, replica_groups=mesh['z_hi'=4,'y'=8,'x'=4,'z_lo'=2,'core'=2] {'z_hi','y'}, dimensions={0} | all-to-all | bytes 327680 | tf_op jit(solution)/shard_map/all_to_all | solution.py:440
  118.5 1.5 %place.1 = f32[6,24,512]{2,1,0:T(8,128)} custom-call(s32[32,1,1280]{2,1,0:T(1,128)S(1)} %all_to_all.23.in_ref), custom_call_target="tpu_custom_call" | custom-call | tf_op jit(solution)/shard_map/place/pallas_call | solution.py:441
  (1 shorter events, 0.0 us)
Async XLA Ops:
  3.9 50.8 %copy-start = (s32[32]{0:T(128)S(1)}, s32[32]{0:T(128)}, u32[]{:S(2)}) copy-start(s32[32]{0:T(128)} %order_ref.1) | copy-start | bytes 388
  55.8 9.3 %collective-permute-start = (f32[416,128]{1,0:T(8,128)S(1)}, f32[416,128]{1,0:T(8,128)S(1)}, u32[]{:S(2)}, u32[]{:S(2)}) collective-permute-start(f32[416,128]{1,0:T(8,128)S(1)} %get-tuple-element.12), channel_id=1, source_target_pairs={{0,1},{1,2},{2,3},{3,4},{4,5},{5,6},{6,7},{7,8},{8,9},{9,10},{10,1... | collective-permute-start | bytes 638984 | tf_op jit(solution)/shard_map/ppermute | solution.py:424
  57.8 9.1 %collective-permute-start.1 = (f32[416,128]{1,0:T(8,128)S(1)}, f32[416,128]{1,0:T(8,128)S(1)}, u32[]{:S(2)}, u32[]{:S(2)}) collective-permute-start(f32[416,128]{1,0:T(8,128)S(1)} %get-tuple-element.13), channel_id=1, source_target_pairs={{0,15},{1,0},{2,1},{3,2},{4,3},{5,4},{6,5},{7,6},{8,7},{9,8},{10,9... | collective-permute-start | bytes 638984 | tf_op jit(solution)/shard_map/ppermute | solution.py:425

commit v4 on v3

--- a/solution.py
+++ b/solution.py
@@ -13,10 +13,13 @@
 
 ROWS = 24
 HALO = 6
+WINDOW = 28
 PAD = ROWS + 2 * HALO
 PERT_PAIRS = 9
 PAIRS = 36
-QUADS = PAIRS // 4
+WHOLE = 32
+SPLIT_FROM = 4
+QUADS = WHOLE // 4
 BASE_QUAD = PERT_PAIRS // 4
 TOP_CODE = 32000.0
 BASE_SCALE = 16384.0
@@ -90,7 +93,7 @@
     return spacing(level) * (1.0 / (TOP_CODE * TOP_CODE))
 
 
-def pack_kernel(pert_hbm, traj_hbm, out_ref, pert_ref, traj_ref, pair_ref, sems):
+def pack_kernel(pert_hbm, traj_hbm, out_ref, pert_ref, traj_ref, pair_ref, split_ref, sems):
     copies = [
         pltpu.make_async_copy(pert_hbm, pert_ref, sems.at[0]),
         pltpu.make_async_copy(traj_hbm, traj_ref, sems.at[1]),
@@ -104,9 +107,7 @@
             largest = jnp.maximum(largest, jnp.abs(pert_ref[field, 8 * tile : 8 * tile + 8]))
     level = level_of(jnp.max(largest, axis=(0, 1), keepdims=True))
     inverse = jnp.broadcast_to(1.0 / spacing(level), (8, 512))
-    level = jnp.broadcast_to(level, (8, 512))
-    lane = lax.broadcasted_iota(jnp.int32, (8, 512), 1)
-    line = lax.broadcasted_iota(jnp.int32, (8, 512), 0)
+    level = jnp.broadcast_to(level, (8, 128))
 
     for pair in range(PERT_PAIRS):
         field, tile = pair // 3, pair % 3
@@ -124,24 +125,38 @@
             for tile in range(3):
                 pair = PERT_PAIRS + 9 * tile + 3 * section + field
                 pair_ref[8 * pair : 8 * pair + 8] = both[8 * tile : 8 * tile + 8]
-    for begin in range(0, QUADS, 3):
+    spare = lax.broadcasted_iota(jnp.int32, (8, 128), 1) % 32 >= WINDOW
+    for parity in range(2):
+        split_ref[parity] = roll_lanes(pair_ref[8 * WHOLE :], 6 - 16 * parity)
+    for begin in range(0, QUADS, 2):
         places, quads = [], []
-        for quad in range(begin, begin + 3):
+        for quad in range(begin, begin + 2):
             raw = [pair_ref[8 * pair : 8 * pair + 8] for pair in range(4 * quad, 4 * quad + 4)]
             for parity in range(2):
-                items = [roll_lanes(item, 8 if parity == 0 else -8) for item in raw]
-                if quad == 0:
-                    items[0] = jnp.where((lane % 32 == 0) & (line == 0), level, items[0])
+                items = [roll_lanes(item, 6 - 16 * parity) for item in raw]
                 for part in range(4):
                     columns = slice(128 * part, 128 * part + 128)
+                    four = [item[:, columns] for item in items]
+                    for i in range(4):
+                        piece = 4 * quad + i - SPLIT_FROM
+                        if piece >= 0:
+                            moved = split_ref[parity, 8 * (piece // 7) : 8 * (piece // 7) + 8, columns]
+                            moved = roll_lanes(moved, WINDOW - 4 * (piece % 7))
+                            four[i] = jnp.where(spare, moved, four[i])
+                        elif piece == -SPLIT_FROM:
+                            four[i] = jnp.where(spare, level, four[i])
                     places.append((8 * part + parity, 8 * quad))
-                    quads.append([item[:, columns] for item in items])
+                    quads.append(four)
         for (target, at), four in zip(places, quad_transposes(quads)):
             for position, item in enumerate(four):
                 out_ref[target + 2 * position, at : at + 8] = item
 
 
-def unpack_kernel(order_ref, in_ref, state_ref, base_ref, up_ref, down_ref):
+def odd_tile():
+    return lax.axis_index("core") == 1
+
+
+def unpack_kernel(order_ref, in_ref, state_ref, base_ref, far_ref, near_ref, up_ref, down_ref):
     column = lax.broadcasted_iota(jnp.int32, (8, 128), 1) % 32
     scale = None
     for quad in range(BASE_QUAD + 1):
@@ -158,7 +173,7 @@
                     continue
                 first, second = halves(both)
                 if scale is None:
-                    level = jnp.where(column == 0, first, 0)
+                    level = roll_lanes(jnp.where(column == WINDOW, first, 0), -WINDOW)
                     for shift in (1, 2, 4, 8, 16):
                         level = level + roll_lanes(level, shift)
                     scale = code_scale(level)
@@ -174,9 +189,17 @@
     target = lax.broadcasted_iota(jnp.int32, (128, 512), 1)
     spread = ((source % 32 == target % 32) & (source // 32 == target // 128)).astype(jnp.float32)
     spread = spread.astype(jnp.bfloat16)
-    begin, end = 8 * BASE_QUAD, 8 * QUADS
+    lane = lax.broadcasted_iota(jnp.int32, (8, 128), 1)
     for step in range(2):
-        block = in_ref[pl.ds(pl.multiple_of(order_ref[step] * end, 8) + begin, end - begin), :]
+        block = in_ref[pl.ds(pl.multiple_of(order_ref[step] * (8 * QUADS), 8), 8 * QUADS), :]
+        pieces = jnp.zeros((8, 128), jnp.int32)
+        for piece in range(WHOLE - SPLIT_FROM):
+            source = piece + SPLIT_FROM
+            to = 32 * (piece // 7) + 4 * (piece % 7)
+            moved = block[8 * (source // 4) : 8 * (source // 4) + 8]
+            moved = roll_lanes(moved, to - 32 * (source % 4) - WINDOW)
+            pieces = jnp.where((lane >= to) & (lane < to + 4), moved, pieces)
+        block = jnp.concatenate([block[8 * BASE_QUAD :], pieces], axis=0)
         for layer, part in enumerate(halves(block)):
             part = part.astype(jnp.float32).astype(jnp.bfloat16)
             wide = jnp.dot(part, spread, preferred_element_type=jnp.float32) * (1.0 / BASE_SCALE)
@@ -193,6 +216,17 @@
         place += width
     up_ref[place : place + 2] = jnp.zeros((2, 128), jnp.float32)
     down_ref[place : place + 2] = jnp.zeros((2, 128), jnp.float32)
+    odd = odd_tile()
+
+    @pl.when(odd)
+    def _():
+        far_ref[...] = down_ref[...]
+        near_ref[...] = up_ref[...]
+
+    @pl.when(jnp.logical_not(odd))
+    def _():
+        far_ref[...] = up_ref[...]
+        near_ref[...] = down_ref[...]
 
 
 def coefficients(fields, scale):
@@ -263,8 +297,21 @@
 
 
 def step_kernel(
-    state_ref, base_ref, top_ref, bottom_ref, cells_ref, gram_ref, start_ref, one_ref, two_ref, coef_ref
+    state_ref, base_ref, far_ref, near_ref, cells_ref, gram_ref, start_ref, one_ref, two_ref, coef_ref, sides_ref
 ):
+    odd = odd_tile()
+    top_ref, bottom_ref = sides_ref.at[0], sides_ref.at[1]
+
+    @pl.when(odd)
+    def _():
+        top_ref[...] = near_ref[...]
+        bottom_ref[...] = far_ref[...]
+
+    @pl.when(jnp.logical_not(odd))
+    def _():
+        top_ref[...] = far_ref[...]
+        bottom_ref[...] = near_ref[...]
+
     for field in range(6):
         start_ref[field, HALO : HALO + ROWS] = state_ref[field]
         for line in range(HALO):
@@ -301,7 +348,7 @@
         for quarter in range(4):
             total = None
             for row in range(8):
-                moved = roll_lanes(lines[row], 16 * row - 32 * quarter - 8)
+                moved = roll_lanes(lines[row], 16 * row - 32 * quarter - HALO)
                 total = moved if total is None else jnp.where(block == row, moved, total)
             cells_ref[8 * quarter : 8 * quarter + 8, 128 * unit : 128 * unit + 128] = total
     cells = cells_ref[...]
@@ -335,12 +382,21 @@
     wide = jnp.concatenate([roll_lanes(total, -32 * i) for i in range(4)], axis=0)
     work = jnp.where(lane < 32, wide, jnp.where(lane == line + 32, 1.0, 0.0))
     roots = jnp.zeros((32, 128), jnp.float32)
-    for k in range(32):
-        row = work[k : k + 1]
-        pivot = row[:, k : k + 1]
-        factor = jnp.where(line[:, :1] > k, work[:, k : k + 1] / pivot, 0.0)
-        roots = jnp.where(line == k, jnp.broadcast_to(pivot, (32, 128)), roots)
-        work = work - factor * row
+    for begin in range(0, 32, 8):
+        columns = [jnp.broadcast_to(work[:, k : k + 1], (32, 128)) for k in range(begin, begin + 8)]
+        rows = [work[k : k + 1] for k in range(begin, begin + 8)]
+        factors = []
+        for j in range(8):
+            k = begin + j
+            pivot = columns[j][k : k + 1]
+            roots = jnp.where(line == k, pivot, roots)
+            factor = jnp.where(line > k, columns[j] * (1.0 / pivot), 0.0)
+            factors.append(factor)
+            for i in range(j + 1, 8):
+                columns[i] = columns[i] - factor * columns[i][k : k + 1]
+                rows[i] = rows[i] - factor[begin + i : begin + i + 1] * rows[j]
+        for factor, row in zip(factors, rows):
+            work = work - factor * row
     work = work / jnp.sqrt(roots)
     upper_ref[...] = jnp.where(lane >= line, work, 0.0)[:, :32]
     inverse = roll_lanes(work, -32)[:, :32]
@@ -409,27 +465,35 @@
             pltpu.VMEM((6, ROWS, 512), jnp.float32),
             pltpu.VMEM((18, ROWS, 512), jnp.bfloat16),
             pltpu.VMEM((8 * PAIRS, 512), jnp.int32),
+            pltpu.VMEM((2, 8 * (PAIRS - WHOLE), 512), jnp.int32),
             pltpu.SemaphoreType.DMA((2,)),
         ],
         spaces=(pltpu.HBM, pltpu.HBM),
         vmem=60,
     )(perturbation[0], trajectory[0].reshape(18, ROWS, 512))
     held = lax.all_to_all(sent, VEC, split_axis=0, concat_axis=0, tiled=True)
-    state, base, up, down = call(
+    state, base, far, near = call(
         unpack_kernel,
         (f32(6, ROWS, 8, 128), f32(36, ROWS, 128), f32(HALO_ROWS, 128), f32(HALO_ROWS, 128)),
         "unpack",
+        [pltpu.VMEM((HALO_ROWS, 128), jnp.float32)] * 2,
         spaces=(pltpu.SMEM, pltpu.VMEM),
     )(step_order, held.reshape(32 * 8 * QUADS, 128))
-    top = lax.ppermute(down, SPACE, [(i, (i + 1) % tiles) for i in range(tiles)])
-    bottom = lax.ppermute(up, SPACE, [(i, (i - 1) % tiles) for i in range(tiles)])
+    far = lax.ppermute(far, SPACE, [(i, (i + 1 if i % 2 else i - 1) % tiles) for i in range(tiles)])
+    near = lax.ppermute(near, SPACE, [(i, i ^ 1) for i in range(tiles)])
     padded = pltpu.VMEM((6, PAD, 8, 128), jnp.float32)
     cells, gram = call(
         step_kernel,
         (f32(32, 2304), f32(first, 8, 128)),
         "steps",
-        [padded, padded, padded, pltpu.VMEM((COEF, ROWS + 16, 128), jnp.float32)],
-    )(state, base, top, bottom)
+        [
+            padded,
+            padded,
+            padded,
+            pltpu.VMEM((COEF, ROWS + 16, 128), jnp.float32),
+            pltpu.VMEM((2, HALO_ROWS, 128), jnp.float32),
+        ],
+    )(state, base, far, near)
     gram = lax.all_to_all(gram, LINE, split_axis=0, concat_axis=0, tiled=True)
     gram = call(sum_kernel, f32(second, 8, 128), "sums")(gram)
     gram = lax.all_to_all(gram, PLANE, split_axis=0, concat_axis=0, tiled=True)

time: 120 us -> 116 us (0.967)
  blocking collectives: 94.7 us -> 90.3 us
  waiting for transfers between devices: 3.34 us -> 6.15 us
  starting transfers between devices: 7.67 us -> 5.34 us
  Pallas kernels: 13.6 us -> 12 us
    all_to_all x1, blocking collectives: 50.7 us -> 47.4 us  [body(): held = lax.all_to_all(sent, VEC, split_axis=0, concat_axis=0, tiled=True)]
    ppermute x2, waiting for transfers between devices: 3.34 us -> 6.15 us  [the longest x1 6.15 us: body(): lax.ppermute(far, SPACE, [(i, (i + 1 if i % 2 else i - 1) % tiles) for i...]
    ppermute x2, starting transfers between devices: 7.67 us -> 5.34 us  [the longest x1 3.04 us: body(): near = lax.ppermute(near, SPACE, [(i, i ^ 1) for i in range(tiles)])]
    pallas_call x1, Pallas kernels: 3.43 us -> 1.53 us  [body(): call(lambda *refs: solve_kernel(entries, *refs), (jax.ShapeDtypeStruct((3...]
  transfers between devices with their start and end apart: 2 -> 2, of which waited for: 2 -> 1; matrix products, arithmetic and copies ran while one was open for 0% -> 0% of each run, Pallas kernels for 0% -> 0%
where the time goes in v4:
time: 116 us; the launch traced here: 115 us
  blocking collectives  90.3 us (78%)
  Pallas kernels  12 us (10%)
  waiting for transfers between devices  6.15 us (5%)
  starting transfers between devices  5.34 us (5%)
    all_to_all x1, blocking collectives, body(): held = lax.all_to_all(sent, VEC, split_axis=0, concat_axis=0, tiled=True)  47.4 us
    all_to_all x1, blocking collectives, body(): gram = lax.all_to_all(gram, PLANE, split_axis=0, concat_axis=0, tiled=True)  16.4 us
    all_to_all x1, blocking collectives, body(): ortho = lax.all_to_all(ortho, VEC, split_axis=0, concat_axis=0, tiled=True)  16.1 us
    all_to_all x1, blocking collectives, body(): gram = lax.all_to_all(gram, LINE, split_axis=0, concat_axis=0, tiled=True)  10.4 us
    ppermute x1, waiting for transfers between devices, body(): lax.ppermute(far, SPACE, [(i, (i + 1 if i % 2 else i - 1) % tiles) for i...  6.15 us
    pallas_call x1, Pallas kernels, body(): call(step_kernel, (f32(32, 2304), f32(first, 8, 128)), 'steps', [padded,...  4.23 us
    pallas_call x1, Pallas kernels, body(): call(pack_kernel, jax.ShapeDtypeStruct((32, 8 * QUADS, 128), jnp.int32),...  3.42 us
    ppermute x1, starting transfers between devices, body(): near = lax.ppermute(near, SPACE, [(i, i ^ 1) for i in range(tiles)])  3.04 us
  transfers between devices with their start and end apart: 2, of which 1 were waited for; matrix products, arithmetic and copies ran while one was open for 0% of the time, Pallas kernels for 0%

profile of v4, /device:TPU:8, one launch (start us, length us, event | category | flops | bytes accessed | tf_op | source)
XLA Modules:
  0.0 115.1 jit_solution(4740778177340083340)
XLA Ops:
  0.6 3.4 %pack.1 = s32[32,64,128]{2,1,0:T(8,128)} custom-call(f32[6,24,512]{2,1,0:T(8,128)} %bitcast.6, bf16[18,24,512]{2,1,0:T(8,128)(2,1)} %bitcast.5), custom_call_target="tpu_custom_call" | custom-call | tf_op jit(solution)/shard_map/pack/pallas_call | solution.py:460
  4.1 47.4 %all_to_all.20 = s32[32,64,128]{2,1,0:T(8,128)S(1)} all-to-all(s32[32,64,128]{2,1,0:T(8,128)} %pack.1), channel_id=1, replica_groups=mesh['z_hi'=4,'y'=8,'x'=4,'z_lo'=2,'core'=2] {'z_hi','y'}, dimensions={0} | all-to-all | bytes 2097152 | tf_op jit(solution)/shard_map/all_to_all | solution.py:474
  51.4 0.0 copy-start
  51.4 0.7 copy-done
  52.1 1.3 %unpack.1 = (f32[6,24,8,128]{3,2,1,0:T(8,128)S(1)}, f32[36,24,128]{2,1,0:T(8,128)S(1)}, f32[416,128]{1,0:T(8,128)S(1)}, f32[416,128]{1,0:T(8,128)S(1)}) custom-call(s32[32]{0:T(128)S(1)} %copy-done, s32[2048,128]{1,0:T(8,128)S(1)} %bitcast.4), custom_call_target="tpu_custom_call" | custom-call | tf_op jit(solution)/shard_map/unpack/pallas_call | solution.py:475
  53.4 2.3 %collective-permute-start = (f32[416,128]{1,0:T(8,128)S(1)}, f32[416,128]{1,0:T(8,128)S(1)}, u32[]{:S(2)}, u32[]{:S(2)}) collective-permute-start(f32[416,128]{1,0:T(8,128)S(1)} %get-tuple-element.12), channel_id=1, source_target_pairs={{0,15},{1,2},{2,1},{3,4},{4,3},{5,6},{6,5},{7,8},{8,7},{9,10},{10,... | collective-permute-start | bytes 638984 | tf_op jit(solution)/shard_map/ppermute | solution.py:482
  55.7 3.0 %collective-permute-start.1 = (f32[416,128]{1,0:T(8,128)S(1)}, f32[416,128]{1,0:T(8,128)S(1)}, u32[]{:S(2)}, u32[]{:S(2)}) collective-permute-start(f32[416,128]{1,0:T(8,128)S(1)} %get-tuple-element.13), channel_id=1, source_target_pairs={{0,1},{1,0},{2,3},{3,2},{4,5},{5,4},{6,7},{7,6},{8,9},{9,8},{10,11... | collective-permute-start | bytes 638984 | tf_op jit(solution)/shard_map/ppermute | solution.py:483
  58.7 6.1 %collective-permute-done.far_ref = f32[416,128]{1,0:T(8,128)S(1)} collective-permute-done((f32[416,128]{1,0:T(8,128)S(1)}, f32[416,128]{1,0:T(8,128)S(1)}, u32[]{:S(2)}, u32[]{:S(2)}) %collective-permute-start) | collective-permute-done | bytes 213024 | tf_op jit(solution)/shard_map/ppermute | solution.py:482
  64.9 0.0 collective-permute-done.1.near_ref
  64.9 4.2 %steps.1 = (f32[32,2304]{1,0:T(8,128)S(1)}, f32[16,8,128]{2,1,0:T(8,128)S(1)}) custom-call(f32[6,24,8,128]{3,2,1,0:T(8,128)S(1)} %get-tuple-element.10.state_ref, f32[36,24,128]{2,1,0:T(8,128)S(1)} %get-tuple-element.11.base_ref, f32[416,128]{1,0:T(8,128)S(1)} %collective-permute-done.far_ref, f32[416,128]{1,0:T(8,128)S(1)} %collective-permute-done.1.near_ref), custom_call_target="tpu_custom_call" | custom-call | tf_op jit(solution)/shard_map/steps/pallas_call | solution.py:485
  69.1 10.4 %all_to_all.21.in_ref = f32[16,8,128]{2,1,0:T(8,128)S(1)} all-to-all(f32[16,8,128]{2,1,0:T(8,128)S(1)} %get-tuple-element.14), channel_id=1, replica_groups=mesh['z_hi'=4,'y'=8,'x'=4,'z_lo'=2,'core'=2] {'z_hi','z_lo','core'}, dimensions={0} | all-to-all | bytes 131072 | tf_op jit(solution)/shard_map/all_to_all | solution.py:497
  79.5 16.4 %all_to_all.22.refs_0_ = f32[32,8,128]{2,1,0:T(8,128)S(1)} all-to-all(f32[32,8,128]{2,1,0:T(8,128)S(1)} %sums.1), channel_id=1, replica_groups=mesh['z_hi'=4,'y'=8,'x'=4,'z_lo'=2,'core'=2] {'x','y'}, dimensions={0} | all-to-all | bytes 262144 | tf_op jit(solution)/shard_map/all_to_all | solution.py:499
  96.0 1.5 %solve.1 = (s32[32,1,1280]{2,1,0:T(1,128)S(1)}, f32[32,32]{1,0:T(8,128)}) custom-call(f32[32,8,128]{2,1,0:T(8,128)S(1)} %all_to_all.22.refs_0_, f32[32,2304]{1,0:T(8,128)S(1)} %get-tuple-element.15.refs_1_), custom_call_target="tpu_custom_call" | custom-call | tf_op jit(solution)/shard_map/solve/pallas_call | solution.py:501
  97.5 16.1 %all_to_all.23.in_ref = s32[32,1,1280]{2,1,0:T(1,128)S(1)} all-to-all(s32[32,1,1280]{2,1,0:T(1,128)S(1)} %get-tuple-element.16), channel_id=1, replica_groups=mesh['z_hi'=4,'y'=8,'x'=4,'z_lo'=2,'core'=2] {'z_hi','y'}, dimensions={0} | all-to-all | bytes 327680 | tf_op jit(solution)/shard_map/all_to_all | solution.py:504
  113.6 1.5 %place.1 = f32[6,24,512]{2,1,0:T(8,128)} custom-call(s32[32,1,1280]{2,1,0:T(1,128)S(1)} %all_to_all.23.in_ref), custom_call_target="tpu_custom_call" | custom-call | tf_op jit(solution)/shard_map/place/pallas_call | solution.py:505
  (1 shorter events, 0.0 us)
Async XLA Ops:
  51.4 0.7 copy-start
  53.4 11.5 %collective-permute-start = (f32[416,128]{1,0:T(8,128)S(1)}, f32[416,128]{1,0:T(8,128)S(1)}, u32[]{:S(2)}, u32[]{:S(2)}) collective-permute-start(f32[416,128]{1,0:T(8,128)S(1)} %get-tuple-element.12), channel_id=1, source_target_pairs={{0,15},{1,2},{2,1},{3,4},{4,3},{5,6},{6,5},{7,8},{8,7},{9,10},{10,... | collective-permute-start | bytes 638984 | tf_op jit(solution)/shard_map/ppermute | solution.py:482
  55.7 9.2 %collective-permute-start.1 = (f32[416,128]{1,0:T(8,128)S(1)}, f32[416,128]{1,0:T(8,128)S(1)}, u32[]{:S(2)}, u32[]{:S(2)}) collective-permute-start(f32[416,128]{1,0:T(8,128)S(1)} %get-tuple-element.13), channel_id=1, source_target_pairs={{0,1},{1,0},{2,3},{3,2},{4,5},{5,4},{6,7},{7,6},{8,9},{9,8},{10,11... | collective-permute-start | bytes 638984 | tf_op jit(solution)/shard_map/ppermute | solution.py:483

commit v5 on v4

--- a/solution.py
+++ b/solution.py
@@ -247,57 +247,95 @@
     return results
 
 
-def section_rows(cur_ref, anchor_ref, new_ref, coef, section):
+def section_rows(cur, anchor, put, coef, kind, row, count):
     scale = 0.5 * TIME_STEP
-    kind = section % 3
 
     def dy(value):
         return roll_lanes(value, -1) - roll_lanes(value, 1)
 
-    def block(row, count):
-        span = range(-1, count + 1)
-        h = [[cur_ref[3 * layer, row + i] for i in span] for layer in range(2)]
-        top = [(scale * GRAVITY_TOP) * (h[0][i] + h[1][i]) for i in range(count + 2)]
-        low = [top[i] + (scale * GRAVITY_LOW) * h[1][i] for i in range(count + 2)]
-        for layer, pressure in enumerate((top, low)):
-            at = COEF // 2 * layer
-            u = [cur_ref[3 * layer + 1, row + i] for i in span]
-            v = [cur_ref[3 * layer + 2, row + i] for i in span]
-            depth = [coef(at, row + i) for i in span]
-            xvel = [coef(at + 1, row + i) for i in span]
-            flux = [depth[i] * u[i] + h[layer][i] * xvel[i] for i in range(count + 2)]
-            for i in range(1, count + 1):
-                line = row + i - 1
-                h_i, u_i, v_i = h[layer][i], u[i], v[i]
-                yvel, xvel_dx, xvel_dy, yvel_dx, yvel_dy = [coef(at + k, line) for k in range(2, 7)]
-                h_new = h_i - (flux[i + 1] - flux[i - 1]) - dy(depth[i] * v_i + h_i * yvel)
-                u_new = u_i - (
-                    xvel[i] * (u[i + 1] - u[i - 1])
-                    + u_i * xvel_dx
-                    + yvel * dy(u_i)
-                    + v_i * xvel_dy
-                    + (pressure[i + 1] - pressure[i - 1])
-                )
-                v_new = v_i - (
-                    xvel[i] * (v[i + 1] - v[i - 1])
-                    + u_i * yvel_dx
-                    + yvel * dy(v_i)
-                    + v_i * yvel_dy
-                    + dy(pressure[i])
-                )
-                for field, value in enumerate((h_new, u_new, v_new)):
-                    field += 3 * layer
-                    if kind == 1:
-                        value = 0.75 * anchor_ref[field, line] + 0.25 * value
-                    if kind == 2:
-                        value = (1.0 / 3.0) * anchor_ref[field, line] + (2.0 / 3.0) * value
-                    new_ref[field, line] = value
-
-    block(section + 1, PAD - 2 - 2 * section)
-
-
-def step_kernel(
-    state_ref, base_ref, far_ref, near_ref, cells_ref, gram_ref, start_ref, one_ref, two_ref, coef_ref, sides_ref
+    span = range(row - 1, row + count + 1)
+    h = [[cur(3 * layer, i) for i in span] for layer in range(2)]
+    top = [(scale * GRAVITY_TOP) * (h[0][i] + h[1][i]) for i in range(count + 2)]
+    low = [top[i] + (scale * GRAVITY_LOW) * h[1][i] for i in range(count + 2)]
+    for layer, pressure in enumerate((top, low)):
+        at = COEF // 2 * layer
+        u = [cur(3 * layer + 1, i) for i in span]
+        v = [cur(3 * layer + 2, i) for i in span]
+        depth = [coef(at, i) for i in span]
+        xvel = [coef(at + 1, i) for i in span]
+        flux = [depth[i] * u[i] + h[layer][i] * xvel[i] for i in range(count + 2)]
+        for i in range(1, count + 1):
+            line = row + i - 1
+            h_i, u_i, v_i = h[layer][i], u[i], v[i]
+            yvel, xvel_dx, xvel_dy, yvel_dx, yvel_dy = [coef(at + k, line) for k in range(2, 7)]
+            h_new = h_i - (flux[i + 1] - flux[i - 1]) - dy(depth[i] * v_i + h_i * yvel)
+            u_new = u_i - (
+                xvel[i] * (u[i + 1] - u[i - 1])
+                + u_i * xvel_dx
+                + yvel * dy(u_i)
+                + v_i * xvel_dy
+                + (pressure[i + 1] - pressure[i - 1])
+            )
+            v_new = v_i - (
+                xvel[i] * (v[i + 1] - v[i - 1])
+                + u_i * yvel_dx
+                + yvel * dy(v_i)
+                + v_i * yvel_dy
+                + dy(pressure[i])
+            )
+            for field, value in enumerate((h_new, u_new, v_new)):
+                field += 3 * layer
+                if kind == 1:
+                    value = 0.75 * anchor(field, line) + 0.25 * value
+                if kind == 2:
+                    value = (1.0 / 3.0) * anchor(field, line) + (2.0 / 3.0) * value
+                put(field, line, value)
+
+
+def own_cells(lines):
+    block = lane_group((8, 128), 16)
+    results = []
+    for quarter in range(4):
+        total = None
+        for row in range(8):
+            moved = roll_lanes(lines[row], 16 * row - 32 * quarter - HALO)
+            total = moved if total is None else jnp.where(block == row, moved, total)
+        results.append(total)
+    return results
+
+
+def inside(section, row):
+    return section < row < ROWS - 1 - section
+
+
+def inner_kernel(state_ref, base_ref, kept_ref, middle_ref, coef_ref):
+    for section in range(6):
+        fields = [base_ref[6 * section + field] for field in range(6)]
+        for index, value in enumerate(coefficients(fields, 0.5 * TIME_STEP)):
+            coef_ref[section % 2, index] = value
+        source = state_ref if section == 0 else kept_ref.at[section - 1]
+        anchor = state_ref if section < 3 else kept_ref.at[2]
+
+        def put(field, row, value):
+            kept_ref[section, field, row] = value
+
+        section_rows(
+            lambda field, row: source[field, row],
+            lambda field, row: anchor[field, row],
+            put,
+            lambda index, row: coef_ref[section % 2, index, pl.ds(row, 8, stride=0), :],
+            section % 3,
+            section + 1,
+            ROWS - 2 - 2 * section,
+        )
+    for field in range(6):
+        cells = own_cells([kept_ref[5, field, 8 + row] for row in range(8)])
+        for quarter, item in enumerate(cells):
+            middle_ref[8 * quarter : 8 * quarter + 8, 128 * field : 128 * field + 128] = item
+
+
+def outer_kernel(
+    state_ref, base_ref, far_ref, near_ref, kept_ref, middle_ref, cells_ref, gram_ref, edge_ref, coef_ref, sides_ref
 ):
     odd = odd_tile()
     top_ref, bottom_ref = sides_ref.at[0], sides_ref.at[1]
@@ -312,14 +350,24 @@
         top_ref[...] = far_ref[...]
         bottom_ref[...] = near_ref[...]
 
-    for field in range(6):
-        start_ref[field, HALO : HALO + ROWS] = state_ref[field]
-        for line in range(HALO):
-            at = 8 * (HALO * field + line)
-            start_ref[field, line] = top_ref[at : at + 8]
-            start_ref[field, HALO + ROWS + line] = bottom_ref[at : at + 8]
+    def slot(row):
+        return row + HALO if row < ROWS // 2 else row - HALO
+
+    def after(section):
+        def read(field, row):
+            if section < 0:
+                if row < 0:
+                    return top_ref[pl.ds(8 * (HALO * field + row + HALO), 8)]
+                if row >= ROWS:
+                    return bottom_ref[pl.ds(8 * (HALO * field + row - ROWS), 8)]
+                return state_ref[field, row]
+            if inside(section, row):
+                return kept_ref[section, field, row]
+            return edge_ref[section, field, slot(row)]
+
+        return read
+
     place = STATE_HALO_ROWS
-    buffers = (start_ref, one_ref, two_ref, start_ref)
     for section in range(6):
         width = STEP_ROWS[section]
         fields = []
@@ -328,29 +376,36 @@
                 top_ref[place : place + width],
                 base_ref[6 * section + field],
                 bottom_ref[place : place + width],
+                jnp.zeros((16 - 2 * width, 128), jnp.float32),
             ]
-            if width < 8:
-                pieces.append(jnp.zeros((16 - 2 * width, 128), jnp.float32))
             fields.append(jnp.concatenate(pieces, axis=0))
             place += width
         for index, value in enumerate(coefficients(fields, 0.5 * TIME_STEP)):
-            coef_ref[index] = value
-
-        def coef(index, row):
-            return coef_ref[index, pl.ds(row - HALO + width, 8, stride=0), :]
-
-        kind = section % 3
-        section_rows(buffers[kind], start_ref, buffers[kind + 1], coef, section)
-    block = lane_group((8, 128), 16)
+            coef_ref[section % 2, index] = value
+
+        def put(field, row, value):
+            edge_ref[section, field, slot(row)] = value
+
+        for begin in (section + 1 - HALO, ROWS - 1 - section):
+            section_rows(
+                after(section - 1),
+                after(-1 if section < 3 else 2),
+                put,
+                lambda index, row: coef_ref[section % 2, index, pl.ds(row + width, 8, stride=0), :],
+                section % 3,
+                begin,
+                HALO,
+            )
+    last = after(5)
     for unit in range(18):
         field, tile = unit // 3, unit % 3
-        lines = [start_ref[field, HALO + 8 * tile + row] for row in range(8)]
-        for quarter in range(4):
-            total = None
-            for row in range(8):
-                moved = roll_lanes(lines[row], 16 * row - 32 * quarter - HALO)
-                total = moved if total is None else jnp.where(block == row, moved, total)
-            cells_ref[8 * quarter : 8 * quarter + 8, 128 * unit : 128 * unit + 128] = total
+        columns = slice(128 * unit, 128 * unit + 128)
+        if tile == 1:
+            cells_ref[:, columns] = middle_ref[:, 128 * field : 128 * field + 128]
+            continue
+        cells = own_cells([last(field, 8 * tile + row) for row in range(8)])
+        for quarter, item in enumerate(cells):
+            cells_ref[8 * quarter : 8 * quarter + 8, columns] = item
     cells = cells_ref[...]
     gram = lax.dot_general(
         cells,
@@ -430,7 +485,7 @@
                 out_ref[field, 8 * tile : 8 * tile + 8, 128 * part : 128 * part + 128] = total
 
 
-def call(kernel, out_shape, name, scratch=(), spaces=None, vmem=40):
+def call(kernel, out_shape, name, scratch=(), spaces=None, vmem=40, cost=None):
     specs = {}
     if spaces:
         specs = dict(in_specs=[pl.BlockSpec(memory_space=space) for space in spaces])
@@ -440,6 +495,7 @@
         scratch_shapes=list(scratch),
         compiler_params=pltpu.CompilerParams(vmem_limit_bytes=vmem * 1024 * 1024),
         name=name,
+        cost_estimate=cost,
         **specs,
     )
 
@@ -481,19 +537,24 @@
     )(step_order, held.reshape(32 * 8 * QUADS, 128))
     far = lax.ppermute(far, SPACE, [(i, (i + 1 if i % 2 else i - 1) % tiles) for i in range(tiles)])
     near = lax.ppermute(near, SPACE, [(i, i ^ 1) for i in range(tiles)])
-    padded = pltpu.VMEM((6, PAD, 8, 128), jnp.float32)
+    coefs = pltpu.VMEM((2, COEF, ROWS + 16, 128), jnp.float32)
+    kept, middle = call(
+        inner_kernel,
+        (f32(6, 6, ROWS, 8, 128), f32(32, 768)),
+        "inner",
+        [pltpu.VMEM((2, COEF, ROWS, 128), jnp.float32)],
+        cost=pl.CostEstimate(flops=20_000_000, bytes_accessed=8_000_000, transcendentals=0),
+    )(state, base)
     cells, gram = call(
-        step_kernel,
+        outer_kernel,
         (f32(32, 2304), f32(first, 8, 128)),
-        "steps",
+        "outer",
         [
-            padded,
-            padded,
-            padded,
-            pltpu.VMEM((COEF, ROWS + 16, 128), jnp.float32),
+            pltpu.VMEM((6, 6, ROWS, 8, 128), jnp.float32),
+            coefs,
             pltpu.VMEM((2, HALO_ROWS, 128), jnp.float32),
         ],
-    )(state, base, far, near)
+    )(state, base, far, near, kept, middle)
     gram = lax.all_to_all(gram, LINE, split_axis=0, concat_axis=0, tiled=True)
     gram = call(sum_kernel, f32(second, 8, 128), "sums")(gram)
     gram = lax.all_to_all(gram, PLANE, split_axis=0, concat_axis=0, tiled=True)

time: 116 us -> 113 us (0.974)
  waiting for transfers between devices: 6.15 us -> 3.82 us
    ppermute x1, waiting for transfers between devices: 6.15 us -> 3.82 us  [body(): lax.ppermute(far, SPACE, [(i, (i + 1 if i % 2 else i - 1) % tiles) for i...]
    pallas_call x1 -> x2, Pallas kernels: 4.23 us -> 4.54 us  [the longest x1 2.33 us: body(): call(inner_kernel, (f32(6, 6, ROWS, 8, 128), f32(32, 768)), 'inner', [plt...]
  transfers between devices with their start and end apart: 2 -> 2, of which waited for: 1 -> 1; matrix products, arithmetic and copies ran while one was open for 0% -> 0% of each run, Pallas kernels for 0% -> 2%
where the time goes in v5:
time: 113 us; the launch traced here: 112 us
  blocking collectives  90.3 us (80%)
  Pallas kernels  12.3 us (11%)
  starting transfers between devices  5.34 us (5%)
  waiting for transfers between devices  3.82 us (3%)
    all_to_all x1, blocking collectives, body(): held = lax.all_to_all(sent, VEC, split_axis=0, concat_axis=0, tiled=True)  47.4 us
    all_to_all x1, blocking collectives, body(): gram = lax.all_to_all(gram, PLANE, split_axis=0, concat_axis=0, tiled=True)  16.4 us
    all_to_all x1, blocking collectives, body(): ortho = lax.all_to_all(ortho, VEC, split_axis=0, concat_axis=0, tiled=True)  16.1 us
    all_to_all x1, blocking collectives, body(): gram = lax.all_to_all(gram, LINE, split_axis=0, concat_axis=0, tiled=True)  10.4 us
    ppermute x1, waiting for transfers between devices, body(): lax.ppermute(far, SPACE, [(i, (i + 1 if i % 2 else i - 1) % tiles) for i...  3.82 us
    pallas_call x1, Pallas kernels, body(): call(pack_kernel, jax.ShapeDtypeStruct((32, 8 * QUADS, 128), jnp.int32),...  3.43 us
    ppermute x1, starting transfers between devices, body(): near = lax.ppermute(near, SPACE, [(i, i ^ 1) for i in range(tiles)])  3.04 us
    pallas_call x1, Pallas kernels, body(): call(inner_kernel, (f32(6, 6, ROWS, 8, 128), f32(32, 768)), 'inner', [plt...  2.33 us
  transfers between devices with their start and end apart: 2, of which 1 were waited for; matrix products, arithmetic and copies ran while one was open for 0% of the time, Pallas kernels for 2%

profile of v5, /device:TPU:8, one launch (start us, length us, event | category | flops | bytes accessed | tf_op | source)
XLA Modules:
  0.0 112.5 jit_solution(18275949900862553598)
XLA Ops:
  0.6 0.0 copy-start
  0.6 3.4 %pack.1 = s32[32,64,128]{2,1,0:T(8,128)} custom-call(f32[6,24,512]{2,1,0:T(8,128)} %bitcast.6, bf16[18,24,512]{2,1,0:T(8,128)(2,1)} %bitcast.5), custom_call_target="tpu_custom_call" | custom-call | tf_op jit(solution)/shard_map/pack/pallas_call | solution.py:516
  4.1 47.4 %all_to_all.20 = s32[32,64,128]{2,1,0:T(8,128)S(1)} all-to-all(s32[32,64,128]{2,1,0:T(8,128)} %pack.1), channel_id=1, replica_groups=mesh['z_hi'=4,'y'=8,'x'=4,'z_lo'=2,'core'=2] {'z_hi','y'}, dimensions={0} | all-to-all | bytes 2097152 | tf_op jit(solution)/shard_map/all_to_all | solution.py:530
  51.4 0.0 copy-done
  51.4 1.3 %unpack.1 = (f32[6,24,8,128]{3,2,1,0:T(8,128)S(1)}, f32[36,24,128]{2,1,0:T(8,128)S(1)}, f32[416,128]{1,0:T(8,128)S(1)}, f32[416,128]{1,0:T(8,128)S(1)}) custom-call(s32[32]{0:T(128)S(1)} %copy-done, s32[2048,128]{1,0:T(8,128)S(1)} %bitcast.4), custom_call_target="tpu_custom_call" | custom-call | tf_op jit(solution)/shard_map/unpack/pallas_call | solution.py:531
  52.7 2.3 %collective-permute-start = (f32[416,128]{1,0:T(8,128)S(1)}, f32[416,128]{1,0:T(8,128)S(1)}, u32[]{:S(2)}, u32[]{:S(2)}) collective-permute-start(f32[416,128]{1,0:T(8,128)S(1)} %get-tuple-element.14), channel_id=1, source_target_pairs={{0,15},{1,2},{2,1},{3,4},{4,3},{5,6},{6,5},{7,8},{8,7},{9,10},{10,... | collective-permute-start | bytes 638984 | tf_op jit(solution)/shard_map/ppermute | solution.py:538
  55.0 3.0 %collective-permute-start.1 = (f32[416,128]{1,0:T(8,128)S(1)}, f32[416,128]{1,0:T(8,128)S(1)}, u32[]{:S(2)}, u32[]{:S(2)}) collective-permute-start(f32[416,128]{1,0:T(8,128)S(1)} %get-tuple-element.15), channel_id=1, source_target_pairs={{0,1},{1,0},{2,3},{3,2},{4,5},{5,4},{6,7},{7,6},{8,9},{9,8},{10,11... | collective-permute-start | bytes 638984 | tf_op jit(solution)/shard_map/ppermute | solution.py:539
  58.1 2.3 %inner.1 = (f32[6,6,24,8,128]{4,3,2,1,0:T(8,128)S(1)}, f32[32,768]{1,0:T(8,128)S(1)}) custom-call(f32[6,24,8,128]{3,2,1,0:T(8,128)S(1)} %get-tuple-element.12.state_ref, f32[36,24,128]{2,1,0:T(8,128)S(1)} %get-tuple-element.13.base_ref), custom_call_target="tpu_custom_call" | custom-call | flops 20000000 | bytes 8000000 | tf_op jit(solution)/shard_map/inner/pallas_call | solution.py:541
  60.4 3.8 %collective-permute-done.far_ref = f32[416,128]{1,0:T(8,128)S(1)} collective-permute-done((f32[416,128]{1,0:T(8,128)S(1)}, f32[416,128]{1,0:T(8,128)S(1)}, u32[]{:S(2)}, u32[]{:S(2)}) %collective-permute-start) | collective-permute-done | bytes 213024 | tf_op jit(solution)/shard_map/ppermute | solution.py:538
  64.2 0.0 collective-permute-done.1.near_ref
  64.2 2.2 %outer.1 = (f32[32,2304]{1,0:T(8,128)S(1)}, f32[16,8,128]{2,1,0:T(8,128)S(1)}) custom-call(f32[6,24,8,128]{3,2,1,0:T(8,128)S(1)} %get-tuple-element.12.state_ref, f32[36,24,128]{2,1,0:T(8,128)S(1)} %get-tuple-element.13.base_ref, f32[416,128]{1,0:T(8,128)S(1)} %collective-permute-done.far_ref, f32[416,128]{1,0:T(8,128)S(1)} %collective-permute-done.1.near_ref, ...), custom_call_target="tpu_custom_call" | custom-call | tf_op jit(solution)/shard_map/outer/pallas_call | solution.py:548
  66.4 10.4 %all_to_all.21.in_ref = f32[16,8,128]{2,1,0:T(8,128)S(1)} all-to-all(f32[16,8,128]{2,1,0:T(8,128)S(1)} %get-tuple-element.18), channel_id=1, replica_groups=mesh['z_hi'=4,'y'=8,'x'=4,'z_lo'=2,'core'=2] {'z_hi','z_lo','core'}, dimensions={0} | all-to-all | bytes 131072 | tf_op jit(solution)/shard_map/all_to_all | solution.py:558
  76.9 16.4 %all_to_all.22.refs_0_ = f32[32,8,128]{2,1,0:T(8,128)S(1)} all-to-all(f32[32,8,128]{2,1,0:T(8,128)S(1)} %sums.1), channel_id=1, replica_groups=mesh['z_hi'=4,'y'=8,'x'=4,'z_lo'=2,'core'=2] {'x','y'}, dimensions={0} | all-to-all | bytes 262144 | tf_op jit(solution)/shard_map/all_to_all | solution.py:560
  93.3 1.5 %solve.1 = (s32[32,1,1280]{2,1,0:T(1,128)S(1)}, f32[32,32]{1,0:T(8,128)}) custom-call(f32[32,8,128]{2,1,0:T(8,128)S(1)} %all_to_all.22.refs_0_, f32[32,2304]{1,0:T(8,128)S(1)} %get-tuple-element.19.refs_1_), custom_call_target="tpu_custom_call" | custom-call | tf_op jit(solution)/shard_map/solve/pallas_call | solution.py:562
  94.8 16.1 %all_to_all.23.in_ref = s32[32,1,1280]{2,1,0:T(1,128)S(1)} all-to-all(s32[32,1,1280]{2,1,0:T(1,128)S(1)} %get-tuple-element.20), channel_id=1, replica_groups=mesh['z_hi'=4,'y'=8,'x'=4,'z_lo'=2,'core'=2] {'z_hi','y'}, dimensions={0} | all-to-all | bytes 327680 | tf_op jit(solution)/shard_map/all_to_all | solution.py:565
  110.9 1.5 %place.1 = f32[6,24,512]{2,1,0:T(8,128)} custom-call(s32[32,1,1280]{2,1,0:T(1,128)S(1)} %all_to_all.23.in_ref), custom_call_target="tpu_custom_call" | custom-call | tf_op jit(solution)/shard_map/place/pallas_call | solution.py:566
  (1 shorter events, 0.0 us)
Async XLA Ops:
  0.6 50.8 %copy-start = (s32[32]{0:T(128)S(1)}, s32[32]{0:T(128)}, u32[]{:S(2)}) copy-start(s32[32]{0:T(128)} %order_ref.1) | copy-start | bytes 388
  52.7 11.5 %collective-permute-start = (f32[416,128]{1,0:T(8,128)S(1)}, f32[416,128]{1,0:T(8,128)S(1)}, u32[]{:S(2)}, u32[]{:S(2)}) collective-permute-start(f32[416,128]{1,0:T(8,128)S(1)} %get-tuple-element.14), channel_id=1, source_target_pairs={{0,15},{1,2},{2,1},{3,4},{4,3},{5,6},{6,5},{7,8},{8,7},{9,10},{10,... | collective-permute-start | bytes 638984 | tf_op jit(solution)/shard_map/ppermute | solution.py:538
  55.0 9.2 %collective-permute-start.1 = (f32[416,128]{1,0:T(8,128)S(1)}, f32[416,128]{1,0:T(8,128)S(1)}, u32[]{:S(2)}, u32[]{:S(2)}) collective-permute-start(f32[416,128]{1,0:T(8,128)S(1)} %get-tuple-element.15), channel_id=1, source_target_pairs={{0,1},{1,0},{2,3},{3,2},{4,5},{5,4},{6,7},{7,6},{8,9},{9,8},{10,11... | collective-permute-start | bytes 638984 | tf_op jit(solution)/shard_map/ppermute | solution.py:539

commit v6 on v5

--- a/solution.py
+++ b/solution.py
@@ -24,9 +24,8 @@
 TOP_CODE = 32000.0
 BASE_SCALE = 16384.0
 STEP_ROWS = tuple(HALO - section for section in range(6))
-BASE_HALO_ROWS = 6 * sum(STEP_ROWS)
-STATE_HALO_ROWS = 6 * HALO * 8
-HALO_ROWS = STATE_HALO_ROWS + BASE_HALO_ROWS + 2
+STATE_HALO_ROWS = 3 * HALO * 8
+HALO_ROWS = STATE_HALO_ROWS + 3 * sum(STEP_ROWS) + 1
 COEF = 14
 
 
@@ -93,7 +92,13 @@
     return spacing(level) * (1.0 / (TOP_CODE * TOP_CODE))
 
 
-def pack_kernel(pert_hbm, traj_hbm, out_ref, pert_ref, traj_ref, pair_ref, split_ref, sems):
+def spread_level(level):
+    for shift in (1, 2, 4, 8, 16):
+        level = level + roll_lanes(level, shift)
+    return level
+
+
+def pack_kernel(pert_hbm, traj_hbm, out_hbm, out_ref, pert_ref, traj_ref, pair_ref, split_ref, sems):
     copies = [
         pltpu.make_async_copy(pert_hbm, pert_ref, sems.at[0]),
         pltpu.make_async_copy(traj_hbm, traj_ref, sems.at[1]),
@@ -150,6 +155,14 @@
         for (target, at), four in zip(places, quad_transposes(quads)):
             for position, item in enumerate(four):
                 out_ref[target + 2 * position, at : at + 8] = item
+        rows = pl.ds(8 * begin, 16)
+        copy = pltpu.make_async_copy(
+            out_ref.at[:, rows], out_hbm.at[:, rows], sems.at[2 + begin // 2]
+        )
+        copy.start()
+        copies.append(copy)
+    for copy in copies[2:]:
+        copy.wait()
 
 
 def odd_tile():
@@ -174,17 +187,16 @@
                 first, second = halves(both)
                 if scale is None:
                     level = roll_lanes(jnp.where(column == WINDOW, first, 0), -WINDOW)
-                    for shift in (1, 2, 4, 8, 16):
-                        level = level + roll_lanes(level, shift)
+                    level = spread_level(level)
                     scale = code_scale(level)
+                field, line = pair // 3, 8 * (pair % 3) + row
+                if line < HALO or line >= ROWS - HALO:
+                    coded = jnp.where(column >= WINDOW, level, both)
+                    side_ref, at = (up_ref, line) if line < HALO else (down_ref, line - ROWS + HALO)
+                    side_ref[pl.ds(8 * (HALO * field + at), 8)] = coded
                 for layer, item in enumerate((first, second)):
                     item = from_root_code(item, scale)
-                    field, line = pair // 3 + 3 * layer, 8 * (pair % 3) + row
-                    state_ref[field, line] = item
-                    if line < HALO:
-                        up_ref[pl.ds(8 * (HALO * field + line), 8)] = item
-                    if line >= ROWS - HALO:
-                        down_ref[pl.ds(8 * (HALO * field + line - ROWS + HALO), 8)] = item
+                    state_ref[field + 3 * layer, line] = item
     source = lax.broadcasted_iota(jnp.int32, (128, 512), 0)
     target = lax.broadcasted_iota(jnp.int32, (128, 512), 1)
     spread = ((source % 32 == target % 32) & (source // 32 == target // 128)).astype(jnp.float32)
@@ -209,13 +221,20 @@
                 item = wide[8 * (at // 4) : 8 * (at // 4) + 8, 128 * (at % 4) : 128 * (at % 4) + 128]
                 base_ref[18 * step + field, 8 * tile : 8 * tile + 8] = item
     place = STATE_HALO_ROWS
-    for index in range(36):
-        width = STEP_ROWS[index // 6]
-        up_ref[place : place + width] = base_ref[index, 0:width]
-        down_ref[place : place + width] = base_ref[index, ROWS - width : ROWS]
-        place += width
-    up_ref[place : place + 2] = jnp.zeros((2, 128), jnp.float32)
-    down_ref[place : place + 2] = jnp.zeros((2, 128), jnp.float32)
+    for section in range(6):
+        width = STEP_ROWS[section]
+        for field in range(3):
+            for side_ref, rows in ((up_ref, slice(0, 8)), (down_ref, slice(ROWS - 8, ROWS))):
+                codes = [
+                    to_code(base_ref[6 * section + field + 3 * layer, rows] * BASE_SCALE)
+                    for layer in range(2)
+                ]
+                both = join(*codes)
+                both = both[0:width] if side_ref is up_ref else both[8 - width : 8]
+                side_ref[place : place + width] = both
+            place += width
+    for side_ref in (up_ref, down_ref):
+        side_ref[place : place + 1] = jnp.zeros((1, 128), jnp.int32)
     odd = odd_tile()
 
     @pl.when(odd)
@@ -335,20 +354,29 @@
 
 
 def outer_kernel(
-    state_ref, base_ref, far_ref, near_ref, kept_ref, middle_ref, cells_ref, gram_ref, edge_ref, coef_ref, sides_ref
+    state_ref, base_ref, far_ref, near_ref, kept_ref, middle_ref, cells_ref, gram_ref, edge_ref, coef_ref, sides_ref, halo_ref
 ):
     odd = odd_tile()
-    top_ref, bottom_ref = sides_ref.at[0], sides_ref.at[1]
 
     @pl.when(odd)
     def _():
-        top_ref[...] = near_ref[...]
-        bottom_ref[...] = far_ref[...]
+        sides_ref[0] = near_ref[...]
+        sides_ref[1] = far_ref[...]
 
     @pl.when(jnp.logical_not(odd))
     def _():
-        top_ref[...] = far_ref[...]
-        bottom_ref[...] = near_ref[...]
+        sides_ref[0] = far_ref[...]
+        sides_ref[1] = near_ref[...]
+
+    column = lax.broadcasted_iota(jnp.int32, (8, 128), 1) % 32
+    for side in range(2):
+        level = roll_lanes(jnp.where(column == WINDOW, sides_ref[side, 0:8], 0), -WINDOW)
+        scale = code_scale(spread_level(level))
+        for field in range(3):
+            for line in range(HALO):
+                both = sides_ref[side, pl.ds(8 * (HALO * field + line), 8)]
+                for layer, code in enumerate(halves(both)):
+                    halo_ref[field + 3 * layer, HALO * side + line] = from_root_code(code, scale)
 
     def slot(row):
         return row + HALO if row < ROWS // 2 else row - HALO
@@ -357,9 +385,9 @@
         def read(field, row):
             if section < 0:
                 if row < 0:
-                    return top_ref[pl.ds(8 * (HALO * field + row + HALO), 8)]
+                    return halo_ref[field, row + HALO]
                 if row >= ROWS:
-                    return bottom_ref[pl.ds(8 * (HALO * field + row - ROWS), 8)]
+                    return halo_ref[field, row - ROWS + HALO]
                 return state_ref[field, row]
             if inside(section, row):
                 return kept_ref[section, field, row]
@@ -372,14 +400,14 @@
         width = STEP_ROWS[section]
         fields = []
         for field in range(6):
-            pieces = [
-                top_ref[place : place + width],
-                base_ref[6 * section + field],
-                bottom_ref[place : place + width],
-                jnp.zeros((16 - 2 * width, 128), jnp.float32),
+            at = place + width * (field % 3)
+            low, high = [
+                halves(sides_ref[side, at : at + width])[field // 3].astype(jnp.float32) * (1.0 / BASE_SCALE)
+                for side in range(2)
             ]
-            fields.append(jnp.concatenate(pieces, axis=0))
-            place += width
+            gap = jnp.zeros((16 - 2 * width, 128), jnp.float32)
+            fields.append(jnp.concatenate([low, base_ref[6 * section + field], high, gap], axis=0))
+        place += 3 * width
         for index, value in enumerate(coefficients(fields, 0.5 * TIME_STEP)):
             coef_ref[section % 2, index] = value
 
@@ -466,29 +494,38 @@
     ortho_ref[:, 0, half:] = jnp.broadcast_to(level, (32, 128))
 
 
-def place_kernel(in_ref, out_ref):
+def place_kernel(in_ref, out_hbm, out_ref, sems):
     block = lane_group((8, 128), 16)
     line = lax.broadcasted_iota(jnp.int32, (8, 128), 0)
     distance = (block - line) % 8
-    for part in range(4):
-        sources = slice(8 * part, 8 * part + 8)
-        scale = code_scale(in_ref[sources, 0, 1152:1280])
-        for pair in range(9):
-            both = in_ref[sources, 0, 128 * pair : 128 * pair + 128]
-            for unit, code in zip((pair, pair + 9), halves(both)):
-                field, tile = unit // 3, unit % 3
-                value = from_root_code(code, scale)
-                total = value
-                for k in range(1, 8):
-                    moved = roll_rows(roll_lanes(value, 16 * k), -k)
-                    total = jnp.where(distance == k, moved, total)
-                out_ref[field, 8 * tile : 8 * tile + 8, 128 * part : 128 * part + 128] = total
-
-
-def call(kernel, out_shape, name, scratch=(), spaces=None, vmem=40, cost=None):
+    scales = [code_scale(in_ref[8 * part : 8 * part + 8, 0, 1152:1280]) for part in range(4)]
+    copies = []
+    for first in range(3):
+        for tile in range(3):
+            pair = 3 * first + tile
+            for part in range(4):
+                both = in_ref[8 * part : 8 * part + 8, 0, 128 * pair : 128 * pair + 128]
+                for field, code in zip((first, first + 3), halves(both)):
+                    value = from_root_code(code, scales[part])
+                    total = value
+                    for k in range(1, 8):
+                        moved = roll_rows(roll_lanes(value, 16 * k), -k)
+                        total = jnp.where(distance == k, moved, total)
+                    out_ref[field, 8 * tile : 8 * tile + 8, 128 * part : 128 * part + 128] = total
+        for field in (first, first + 3):
+            copy = pltpu.make_async_copy(out_ref.at[field], out_hbm.at[field], sems.at[field])
+            copy.start()
+            copies.append(copy)
+    for copy in copies:
+        copy.wait()
+
+
+def call(kernel, out_shape, name, scratch=(), spaces=None, vmem=40, cost=None, out_space=None):
     specs = {}
     if spaces:
         specs = dict(in_specs=[pl.BlockSpec(memory_space=space) for space in spaces])
+    if out_space is not None:
+        specs["out_specs"] = pl.BlockSpec(memory_space=out_space)
     return pl.pallas_call(
         kernel,
         out_shape=out_shape,
@@ -518,21 +555,24 @@
         jax.ShapeDtypeStruct((32, 8 * QUADS, 128), jnp.int32),
         "pack",
         [
+            pltpu.VMEM((32, 8 * QUADS, 128), jnp.int32),
             pltpu.VMEM((6, ROWS, 512), jnp.float32),
             pltpu.VMEM((18, ROWS, 512), jnp.bfloat16),
             pltpu.VMEM((8 * PAIRS, 512), jnp.int32),
             pltpu.VMEM((2, 8 * (PAIRS - WHOLE), 512), jnp.int32),
-            pltpu.SemaphoreType.DMA((2,)),
+            pltpu.SemaphoreType.DMA((2 + QUADS // 2,)),
         ],
         spaces=(pltpu.HBM, pltpu.HBM),
+        out_space=pltpu.HBM,
         vmem=60,
     )(perturbation[0], trajectory[0].reshape(18, ROWS, 512))
     held = lax.all_to_all(sent, VEC, split_axis=0, concat_axis=0, tiled=True)
+    side = jax.ShapeDtypeStruct((HALO_ROWS, 128), jnp.int32)
     state, base, far, near = call(
         unpack_kernel,
-        (f32(6, ROWS, 8, 128), f32(36, ROWS, 128), f32(HALO_ROWS, 128), f32(HALO_ROWS, 128)),
+        (f32(6, ROWS, 8, 128), f32(36, ROWS, 128), side, side),
         "unpack",
-        [pltpu.VMEM((HALO_ROWS, 128), jnp.float32)] * 2,
+        [pltpu.VMEM((HALO_ROWS, 128), jnp.int32)] * 2,
         spaces=(pltpu.SMEM, pltpu.VMEM),
     )(step_order, held.reshape(32 * 8 * QUADS, 128))
     far = lax.ppermute(far, SPACE, [(i, (i + 1 if i % 2 else i - 1) % tiles) for i in range(tiles)])
@@ -552,7 +592,8 @@
         [
             pltpu.VMEM((6, 6, ROWS, 8, 128), jnp.float32),
             coefs,
-            pltpu.VMEM((2, HALO_ROWS, 128), jnp.float32),
+            pltpu.VMEM((2, HALO_ROWS, 128), jnp.int32),
+            pltpu.VMEM((6, 2 * HALO, 8, 128), jnp.float32),
         ],
     )(state, base, far, near, kept, middle)
     gram = lax.all_to_all(gram, LINE, split_axis=0, concat_axis=0, tiled=True)
@@ -563,7 +604,14 @@
         lambda *refs: solve_kernel(entries, *refs), (jax.ShapeDtypeStruct((32, 1, 1280), jnp.int32), f32(32, 32)), "solve"
     )(gram, cells)
     ortho = lax.all_to_all(ortho, VEC, split_axis=0, concat_axis=0, tiled=True)
-    placed = call(place_kernel, f32(6, ROWS, 512), "place")(ortho)
+    placed = call(
+        place_kernel,
+        f32(6, ROWS, 512),
+        "place",
+        [pltpu.VMEM((6, ROWS, 512), jnp.float32), pltpu.SemaphoreType.DMA((6,))],
+        spaces=(pltpu.VMEM,),
+        out_space=pltpu.HBM,
+    )(ortho)
     return placed[None], upper
 
 

time: 113 us -> 111 us (0.982)
  waiting for transfers between devices: 3.82 us -> 1.46 us
    ppermute x1, waiting for transfers between devices: 3.82 us -> 1.46 us  [body(): lax.ppermute(far, SPACE, [(i, (i + 1 if i % 2 else i - 1) % tiles) for i...]
where the time goes in v6:
time: 111 us
  blocking collectives  90.6 us (82%)
  Pallas kernels  12.6 us (11%)
  starting transfers between devices  5.33 us (5%)
  waiting for transfers between devices  1.46 us (1%)
    all_to_all x1, blocking collectives, body(): held = lax.all_to_all(sent, VEC, split_axis=0, concat_axis=0, tiled=True)  47.4 us
    all_to_all x1, blocking collectives, body(): gram = lax.all_to_all(gram, PLANE, split_axis=0, concat_axis=0, tiled=True)  16.7 us
    all_to_all x1, blocking collectives, body(): ortho = lax.all_to_all(ortho, VEC, split_axis=0, concat_axis=0, tiled=True)  16.1 us
    all_to_all x1, blocking collectives, body(): gram = lax.all_to_all(gram, LINE, split_axis=0, concat_axis=0, tiled=True)  10.4 us
    pallas_call x1, Pallas kernels, body(): call(pack_kernel, jax.ShapeDtypeStruct((32, 8 * QUADS, 128), jnp.int32),...  3.27 us
    ppermute x1, starting transfers between devices, body(): near = lax.ppermute(near, SPACE, [(i, i ^ 1) for i in range(tiles)])  3.04 us
    pallas_call x1, Pallas kernels, body(): call(outer_kernel, (f32(32, 2304), f32(first, 8, 128)), 'outer', [pltpu.V...  2.55 us
    pallas_call x1, Pallas kernels, body(): call(inner_kernel, (f32(6, 6, ROWS, 8, 128), f32(32, 768)), 'inner', [plt...  2.41 us
  transfers between devices with their start and end apart: 2, of which 1 were waited for; matrix products, arithmetic and copies ran while one was open for 0% of the time, Pallas kernels for 2%

profile of v6, /device:TPU:8, one launch (start us, length us, event | category | flops | bytes accessed | tf_op | source)
XLA Modules:
  0.0 110.6 jit_solution(10587028336840652992)
XLA Ops:
  0.6 0.0 copy-start
  0.6 3.3 %pack.1 = s32[32,64,128]{2,1,0:T(8,128)} custom-call(f32[6,24,512]{2,1,0:T(8,128)} %bitcast.6, bf16[18,24,512]{2,1,0:T(8,128)(2,1)} %bitcast.5), custom_call_target="tpu_custom_call" | custom-call | tf_op jit(solution)/shard_map/pack/pallas_call | solution.py:553
  3.9 47.4 %all_to_all.20 = s32[32,64,128]{2,1,0:T(8,128)S(1)} all-to-all(s32[32,64,128]{2,1,0:T(8,128)} %pack.1), channel_id=1, replica_groups=mesh['z_hi'=4,'y'=8,'x'=4,'z_lo'=2,'core'=2] {'z_hi','y'}, dimensions={0} | all-to-all | bytes 2097152 | tf_op jit(solution)/shard_map/all_to_all | solution.py:569
  51.3 0.0 copy-done
  51.3 1.2 %unpack.1 = (f32[6,24,8,128]{3,2,1,0:T(8,128)S(1)}, f32[36,24,128]{2,1,0:T(8,128)S(1)}, s32[208,128]{1,0:T(8,128)S(1)}, s32[208,128]{1,0:T(8,128)S(1)}) custom-call(s32[32]{0:T(128)S(1)} %copy-done, s32[2048,128]{1,0:T(8,128)S(1)} %bitcast.4), custom_call_target="tpu_custom_call" | custom-call | tf_op jit(solution)/shard_map/unpack/pallas_call | solution.py:571
  52.5 2.3 %collective-permute-start = (s32[208,128]{1,0:T(8,128)S(1)}, s32[208,128]{1,0:T(8,128)S(1)}, u32[]{:S(2)}, u32[]{:S(2)}) collective-permute-start(s32[208,128]{1,0:T(8,128)S(1)} %get-tuple-element.14), channel_id=1, source_target_pairs={{0,15},{1,2},{2,1},{3,4},{4,3},{5,6},{6,5},{7,8},{8,7},{9,10},{10,... | collective-permute-start | bytes 319496 | tf_op jit(solution)/shard_map/ppermute | solution.py:578
  54.8 3.0 %collective-permute-start.1 = (s32[208,128]{1,0:T(8,128)S(1)}, s32[208,128]{1,0:T(8,128)S(1)}, u32[]{:S(2)}, u32[]{:S(2)}) collective-permute-start(s32[208,128]{1,0:T(8,128)S(1)} %get-tuple-element.15), channel_id=1, source_target_pairs={{0,1},{1,0},{2,3},{3,2},{4,5},{5,4},{6,7},{7,6},{8,9},{9,8},{10,11... | collective-permute-start | bytes 319496 | tf_op jit(solution)/shard_map/ppermute | solution.py:579
  57.9 2.4 %inner.1 = (f32[6,6,24,8,128]{4,3,2,1,0:T(8,128)S(1)}, f32[32,768]{1,0:T(8,128)S(1)}) custom-call(f32[6,24,8,128]{3,2,1,0:T(8,128)S(1)} %get-tuple-element.12.state_ref, f32[36,24,128]{2,1,0:T(8,128)S(1)} %get-tuple-element.13.base_ref), custom_call_target="tpu_custom_call" | custom-call | flops 20000000 | bytes 8000000 | tf_op jit(solution)/shard_map/inner/pallas_call | solution.py:581
  60.3 1.5 %collective-permute-done.far_ref = s32[208,128]{1,0:T(8,128)S(1)} collective-permute-done((s32[208,128]{1,0:T(8,128)S(1)}, s32[208,128]{1,0:T(8,128)S(1)}, u32[]{:S(2)}, u32[]{:S(2)}) %collective-permute-start) | collective-permute-done | bytes 106528 | tf_op jit(solution)/shard_map/ppermute | solution.py:578
  61.7 0.0 collective-permute-done.1.near_ref
  61.7 2.5 %outer.1 = (f32[32,2304]{1,0:T(8,128)S(1)}, f32[16,8,128]{2,1,0:T(8,128)S(1)}) custom-call(f32[6,24,8,128]{3,2,1,0:T(8,128)S(1)} %get-tuple-element.12.state_ref, f32[36,24,128]{2,1,0:T(8,128)S(1)} %get-tuple-element.13.base_ref, s32[208,128]{1,0:T(8,128)S(1)} %collective-permute-done.far_ref, s32[208,128]{1,0:T(8,128)S(1)} %collective-permute-done.1.near_ref, ...), custom_call_target="tpu_custom_call" | custom-call | tf_op jit(solution)/shard_map/outer/pallas_call | solution.py:588
  64.3 10.4 %all_to_all.21.in_ref = f32[16,8,128]{2,1,0:T(8,128)S(1)} all-to-all(f32[16,8,128]{2,1,0:T(8,128)S(1)} %get-tuple-element.18), channel_id=1, replica_groups=mesh['z_hi'=4,'y'=8,'x'=4,'z_lo'=2,'core'=2] {'z_hi','z_lo','core'}, dimensions={0} | all-to-all | bytes 131072 | tf_op jit(solution)/shard_map/all_to_all | solution.py:599
  74.7 16.7 %all_to_all.22.refs_0_ = f32[32,8,128]{2,1,0:T(8,128)S(1)} all-to-all(f32[32,8,128]{2,1,0:T(8,128)S(1)} %sums.1), channel_id=1, replica_groups=mesh['z_hi'=4,'y'=8,'x'=4,'z_lo'=2,'core'=2] {'x','y'}, dimensions={0} | all-to-all | bytes 262144 | tf_op jit(solution)/shard_map/all_to_all | solution.py:601
  91.4 1.5 %solve.1 = (s32[32,1,1280]{2,1,0:T(1,128)S(1)}, f32[32,32]{1,0:T(8,128)}) custom-call(f32[32,8,128]{2,1,0:T(8,128)S(1)} %all_to_all.22.refs_0_, f32[32,2304]{1,0:T(8,128)S(1)} %get-tuple-element.19.refs_1_), custom_call_target="tpu_custom_call" | custom-call | tf_op jit(solution)/shard_map/solve/pallas_call | solution.py:603
  93.0 16.1 %all_to_all.23.in_ref = s32[32,1,1280]{2,1,0:T(1,128)S(1)} all-to-all(s32[32,1,1280]{2,1,0:T(1,128)S(1)} %get-tuple-element.20), channel_id=1, replica_groups=mesh['z_hi'=4,'y'=8,'x'=4,'z_lo'=2,'core'=2] {'z_hi','y'}, dimensions={0} | all-to-all | bytes 327680 | tf_op jit(solution)/shard_map/all_to_all | solution.py:606
  109.1 1.5 %place.1 = f32[6,24,512]{2,1,0:T(8,128)} custom-call(s32[32,1,1280]{2,1,0:T(1,128)S(1)} %all_to_all.23.in_ref), custom_call_target="tpu_custom_call" | custom-call | tf_op jit(solution)/shard_map/place/pallas_call | solution.py:607
  (1 shorter events, 0.0 us)
Async XLA Ops:
  0.6 50.7 %copy-start = (s32[32]{0:T(128)S(1)}, s32[32]{0:T(128)}, u32[]{:S(2)}) copy-start(s32[32]{0:T(128)} %order_ref.1) | copy-start | bytes 388
  52.5 9.2 %collective-permute-start = (s32[208,128]{1,0:T(8,128)S(1)}, s32[208,128]{1,0:T(8,128)S(1)}, u32[]{:S(2)}, u32[]{:S(2)}) collective-permute-start(s32[208,128]{1,0:T(8,128)S(1)} %get-tuple-element.14), channel_id=1, source_target_pairs={{0,15},{1,2},{2,1},{3,4},{4,3},{5,6},{6,5},{7,8},{8,7},{9,10},{10,... | collective-permute-start | bytes 319496 | tf_op jit(solution)/shard_map/ppermute | solution.py:578
  54.8 6.9 %collective-permute-start.1 = (s32[208,128]{1,0:T(8,128)S(1)}, s32[208,128]{1,0:T(8,128)S(1)}, u32[]{:S(2)}, u32[]{:S(2)}) collective-permute-start(s32[208,128]{1,0:T(8,128)S(1)} %get-tuple-element.15), channel_id=1, source_target_pairs={{0,1},{1,0},{2,3},{3,2},{4,5},{5,4},{6,7},{7,6},{8,9},{9,8},{10,11... | collective-permute-start | bytes 319496 | tf_op jit(solution)/shard_map/ppermute | solution.py:579

commit v7 on v6

--- a/solution.py
+++ b/solution.py
@@ -27,6 +27,7 @@
 STATE_HALO_ROWS = 3 * HALO * 8
 HALO_ROWS = STATE_HALO_ROWS + 3 * sum(STEP_ROWS) + 1
 COEF = 14
+PANEL = 16
 
 
 def roll_lanes(value, shift):
@@ -311,16 +312,16 @@
                 put(field, line, value)
 
 
-def own_cells(lines):
-    block = lane_group((8, 128), 16)
-    results = []
-    for quarter in range(4):
-        total = None
-        for row in range(8):
-            moved = roll_lanes(lines[row], 16 * row - 32 * quarter - HALO)
-            total = moved if total is None else jnp.where(block == row, moved, total)
-        results.append(total)
-    return results
+def own_cells(tiles):
+    first = lane_group((8, 128), 16) % 2 == 0
+    merged = [
+        [
+            jnp.where(first, roll_lanes(lines[-2 * i % 8], -HALO), roll_lanes(lines[(-2 * i - 1) % 8], 16 - HALO))
+            for i in range(4)
+        ]
+        for lines in tiles
+    ]
+    return quad_transposes(merged)
 
 
 def inside(section, row):
@@ -347,8 +348,8 @@
             section + 1,
             ROWS - 2 - 2 * section,
         )
-    for field in range(6):
-        cells = own_cells([kept_ref[5, field, 8 + row] for row in range(8)])
+    tiles = [[kept_ref[5, field, 8 + row] for row in range(8)] for field in range(6)]
+    for field, cells in enumerate(own_cells(tiles)):
         for quarter, item in enumerate(cells):
             middle_ref[8 * quarter : 8 * quarter + 8, 128 * field : 128 * field + 128] = item
 
@@ -425,15 +426,14 @@
                 HALO,
             )
     last = after(5)
-    for unit in range(18):
-        field, tile = unit // 3, unit % 3
-        columns = slice(128 * unit, 128 * unit + 128)
-        if tile == 1:
-            cells_ref[:, columns] = middle_ref[:, 128 * field : 128 * field + 128]
-            continue
-        cells = own_cells([last(field, 8 * tile + row) for row in range(8)])
-        for quarter, item in enumerate(cells):
-            cells_ref[8 * quarter : 8 * quarter + 8, columns] = item
+    for field in range(6):
+        outer = [[last(field, 8 * tile + row) for row in range(8)] for tile in (0, 2)]
+        for tile, cells in zip((0, 2), own_cells(outer)):
+            for quarter, item in enumerate(cells):
+                unit = 3 * field + tile
+                cells_ref[8 * quarter : 8 * quarter + 8, 128 * unit : 128 * unit + 128] = item
+        unit = 3 * field + 1
+        cells_ref[:, 128 * unit : 128 * unit + 128] = middle_ref[:, 128 * field : 128 * field + 128]
     cells = cells_ref[...]
     gram = lax.dot_general(
         cells,
@@ -465,17 +465,17 @@
     wide = jnp.concatenate([roll_lanes(total, -32 * i) for i in range(4)], axis=0)
     work = jnp.where(lane < 32, wide, jnp.where(lane == line + 32, 1.0, 0.0))
     roots = jnp.zeros((32, 128), jnp.float32)
-    for begin in range(0, 32, 8):
-        columns = [jnp.broadcast_to(work[:, k : k + 1], (32, 128)) for k in range(begin, begin + 8)]
-        rows = [work[k : k + 1] for k in range(begin, begin + 8)]
+    for begin in range(0, 32, PANEL):
+        columns = [jnp.broadcast_to(work[:, k : k + 1], (32, 128)) for k in range(begin, begin + PANEL)]
+        rows = [work[k : k + 1] for k in range(begin, begin + PANEL)]
         factors = []
-        for j in range(8):
+        for j in range(PANEL):
             k = begin + j
             pivot = columns[j][k : k + 1]
             roots = jnp.where(line == k, pivot, roots)
             factor = jnp.where(line > k, columns[j] * (1.0 / pivot), 0.0)
             factors.append(factor)
-            for i in range(j + 1, 8):
+            for i in range(j + 1, PANEL):
                 columns[i] = columns[i] - factor * columns[i][k : k + 1]
                 rows[i] = rows[i] - factor[begin + i : begin + i + 1] * rows[j]
         for factor, row in zip(factors, rows):
@@ -494,24 +494,35 @@
     ortho_ref[:, 0, half:] = jnp.broadcast_to(level, (32, 128))
 
 
-def place_kernel(in_ref, out_hbm, out_ref, sems):
+def block_transposes(values):
     block = lane_group((8, 128), 16)
     line = lax.broadcasted_iota(jnp.int32, (8, 128), 0)
-    distance = (block - line) % 8
-    scales = [code_scale(in_ref[8 * part : 8 * part + 8, 0, 1152:1280]) for part in range(4)]
+
+    def shear(values, index, roll, step):
+        for bit in (1, 2, 4):
+            mask = (index & bit) != 0
+            values = [jnp.where(mask, roll(value, step * bit), value) for value in values]
+        return values
+
+    values = shear(values, line, roll_lanes, 16)
+    values = shear(values, block, roll_rows, -1)
+    return shear(values, line, roll_lanes, 16)
+
+
+def place_kernel(in_ref, out_hbm, out_ref, sems):
+    def chunk(part, index):
+        return in_ref[8 * part : 8 * part + 8, 0, 128 * index : 128 * index + 128]
+
+    scales = [code_scale(level) for level in block_transposes([chunk(part, 9) for part in range(4)])]
     copies = []
     for first in range(3):
-        for tile in range(3):
-            pair = 3 * first + tile
-            for part in range(4):
-                both = in_ref[8 * part : 8 * part + 8, 0, 128 * pair : 128 * pair + 128]
-                for field, code in zip((first, first + 3), halves(both)):
-                    value = from_root_code(code, scales[part])
-                    total = value
-                    for k in range(1, 8):
-                        moved = roll_rows(roll_lanes(value, 16 * k), -k)
-                        total = jnp.where(distance == k, moved, total)
-                    out_ref[field, 8 * tile : 8 * tile + 8, 128 * part : 128 * part + 128] = total
+        places = [(tile, part) for tile in range(3) for part in range(4)]
+        items = block_transposes([chunk(part, 3 * first + tile) for tile, part in places])
+        for (tile, part), both in zip(places, items):
+            for field, code in zip((first, first + 3), halves(both)):
+                out_ref[field, 8 * tile : 8 * tile + 8, 128 * part : 128 * part + 128] = from_root_code(
+                    code, scales[part]
+                )
         for field in (first, first + 3):
             copy = pltpu.make_async_copy(out_ref.at[field], out_hbm.at[field], sems.at[field])
             copy.start()

time: 111 us -> 111 us (level)
  no operation moved by 1% of the time
where the time goes in v7:
time: 111 us; the launch traced here: 110 us
  blocking collectives  90.6 us (82%)
  Pallas kernels  12.1 us (11%)
  starting transfers between devices  5.33 us (5%)
  waiting for transfers between devices  1.44 us (1%)
    all_to_all x1, blocking collectives, body(): held = lax.all_to_all(sent, VEC, split_axis=0, concat_axis=0, tiled=True)  47.4 us
    all_to_all x1, blocking collectives, body(): gram = lax.all_to_all(gram, PLANE, split_axis=0, concat_axis=0, tiled=True)  16.7 us
    all_to_all x1, blocking collectives, body(): ortho = lax.all_to_all(ortho, VEC, split_axis=0, concat_axis=0, tiled=True)  16.1 us
    all_to_all x1, blocking collectives, body(): gram = lax.all_to_all(gram, LINE, split_axis=0, concat_axis=0, tiled=True)  10.4 us
    pallas_call x1, Pallas kernels, body(): call(pack_kernel, jax.ShapeDtypeStruct((32, 8 * QUADS, 128), jnp.int32),...  3.27 us
    ppermute x1, starting transfers between devices, body(): near = lax.ppermute(near, SPACE, [(i, i ^ 1) for i in range(tiles)])  3.04 us
    pallas_call x1, Pallas kernels, body(): call(outer_kernel, (f32(32, 2304), f32(first, 8, 128)), 'outer', [pltpu.V...  2.54 us
    pallas_call x1, Pallas kernels, body(): call(inner_kernel, (f32(6, 6, ROWS, 8, 128), f32(32, 768)), 'inner', [plt...  2.43 us
  transfers between devices with their start and end apart: 2, of which 1 were waited for; matrix products, arithmetic and copies ran while one was open for 0% of the time, Pallas kernels for 2%

profile of v7, /device:TPU:8, one launch (start us, length us, event | category | flops | bytes accessed | tf_op | source)
XLA Modules:
  0.0 110.2 jit_solution(15020631430286758609)
XLA Ops:
  0.6 0.0 copy-start
  0.6 3.3 %pack.1 = s32[32,64,128]{2,1,0:T(8,128)} custom-call(f32[6,24,512]{2,1,0:T(8,128)} %bitcast.6, bf16[18,24,512]{2,1,0:T(8,128)(2,1)} %bitcast.5), custom_call_target="tpu_custom_call" | custom-call | tf_op jit(solution)/shard_map/pack/pallas_call | solution.py:564
  3.9 47.4 %all_to_all.20 = s32[32,64,128]{2,1,0:T(8,128)S(1)} all-to-all(s32[32,64,128]{2,1,0:T(8,128)} %pack.1), channel_id=1, replica_groups=mesh['z_hi'=4,'y'=8,'x'=4,'z_lo'=2,'core'=2] {'z_hi','y'}, dimensions={0} | all-to-all | bytes 2097152 | tf_op jit(solution)/shard_map/all_to_all | solution.py:580
  51.3 0.0 copy-done
  51.3 1.2 %unpack.1 = (f32[6,24,8,128]{3,2,1,0:T(8,128)S(1)}, f32[36,24,128]{2,1,0:T(8,128)S(1)}, s32[208,128]{1,0:T(8,128)S(1)}, s32[208,128]{1,0:T(8,128)S(1)}) custom-call(s32[32]{0:T(128)S(1)} %copy-done, s32[2048,128]{1,0:T(8,128)S(1)} %bitcast.4), custom_call_target="tpu_custom_call" | custom-call | tf_op jit(solution)/shard_map/unpack/pallas_call | solution.py:582
  52.5 2.3 %collective-permute-start = (s32[208,128]{1,0:T(8,128)S(1)}, s32[208,128]{1,0:T(8,128)S(1)}, u32[]{:S(2)}, u32[]{:S(2)}) collective-permute-start(s32[208,128]{1,0:T(8,128)S(1)} %get-tuple-element.14), channel_id=1, source_target_pairs={{0,15},{1,2},{2,1},{3,4},{4,3},{5,6},{6,5},{7,8},{8,7},{9,10},{10,... | collective-permute-start | bytes 319496 | tf_op jit(solution)/shard_map/ppermute | solution.py:589
  54.8 3.0 %collective-permute-start.1 = (s32[208,128]{1,0:T(8,128)S(1)}, s32[208,128]{1,0:T(8,128)S(1)}, u32[]{:S(2)}, u32[]{:S(2)}) collective-permute-start(s32[208,128]{1,0:T(8,128)S(1)} %get-tuple-element.15), channel_id=1, source_target_pairs={{0,1},{1,0},{2,3},{3,2},{4,5},{5,4},{6,7},{7,6},{8,9},{9,8},{10,11... | collective-permute-start | bytes 319496 | tf_op jit(solution)/shard_map/ppermute | solution.py:590
  57.9 2.4 %inner.1 = (f32[6,6,24,8,128]{4,3,2,1,0:T(8,128)S(1)}, f32[32,768]{1,0:T(8,128)S(1)}) custom-call(f32[6,24,8,128]{3,2,1,0:T(8,128)S(1)} %get-tuple-element.12.state_ref, f32[36,24,128]{2,1,0:T(8,128)S(1)} %get-tuple-element.13.base_ref), custom_call_target="tpu_custom_call" | custom-call | flops 20000000 | bytes 8000000 | tf_op jit(solution)/shard_map/inner/pallas_call | solution.py:592
  60.3 1.4 %collective-permute-done.far_ref = s32[208,128]{1,0:T(8,128)S(1)} collective-permute-done((s32[208,128]{1,0:T(8,128)S(1)}, s32[208,128]{1,0:T(8,128)S(1)}, u32[]{:S(2)}, u32[]{:S(2)}) %collective-permute-start) | collective-permute-done | bytes 106528 | tf_op jit(solution)/shard_map/ppermute | solution.py:589
  61.7 0.0 collective-permute-done.1.near_ref
  61.7 2.5 %outer.1 = (f32[32,2304]{1,0:T(8,128)S(1)}, f32[16,8,128]{2,1,0:T(8,128)S(1)}) custom-call(f32[6,24,8,128]{3,2,1,0:T(8,128)S(1)} %get-tuple-element.12.state_ref, f32[36,24,128]{2,1,0:T(8,128)S(1)} %get-tuple-element.13.base_ref, s32[208,128]{1,0:T(8,128)S(1)} %collective-permute-done.far_ref, s32[208,128]{1,0:T(8,128)S(1)} %collective-permute-done.1.near_ref, ...), custom_call_target="tpu_custom_call" | custom-call | tf_op jit(solution)/shard_map/outer/pallas_call | solution.py:599
  64.3 10.4 %all_to_all.21.in_ref = f32[16,8,128]{2,1,0:T(8,128)S(1)} all-to-all(f32[16,8,128]{2,1,0:T(8,128)S(1)} %get-tuple-element.18), channel_id=1, replica_groups=mesh['z_hi'=4,'y'=8,'x'=4,'z_lo'=2,'core'=2] {'z_hi','z_lo','core'}, dimensions={0} | all-to-all | bytes 131072 | tf_op jit(solution)/shard_map/all_to_all | solution.py:610
  74.7 16.7 %all_to_all.22.refs_0_ = f32[32,8,128]{2,1,0:T(8,128)S(1)} all-to-all(f32[32,8,128]{2,1,0:T(8,128)S(1)} %sums.1), channel_id=1, replica_groups=mesh['z_hi'=4,'y'=8,'x'=4,'z_lo'=2,'core'=2] {'x','y'}, dimensions={0} | all-to-all | bytes 262144 | tf_op jit(solution)/shard_map/all_to_all | solution.py:612
  91.4 1.4 %solve.1 = (s32[32,1,1280]{2,1,0:T(1,128)S(1)}, f32[32,32]{1,0:T(8,128)}) custom-call(f32[32,8,128]{2,1,0:T(8,128)S(1)} %all_to_all.22.refs_0_, f32[32,2304]{1,0:T(8,128)S(1)} %get-tuple-element.19.refs_1_), custom_call_target="tpu_custom_call" | custom-call | tf_op jit(solution)/shard_map/solve/pallas_call | solution.py:614
  92.9 16.1 %all_to_all.23.in_ref = s32[32,1,1280]{2,1,0:T(1,128)S(1)} all-to-all(s32[32,1,1280]{2,1,0:T(1,128)S(1)} %get-tuple-element.20), channel_id=1, replica_groups=mesh['z_hi'=4,'y'=8,'x'=4,'z_lo'=2,'core'=2] {'z_hi','y'}, dimensions={0} | all-to-all | bytes 327680 | tf_op jit(solution)/shard_map/all_to_all | solution.py:617
  109.0 1.2 %place.1 = f32[6,24,512]{2,1,0:T(8,128)} custom-call(s32[32,1,1280]{2,1,0:T(1,128)S(1)} %all_to_all.23.in_ref), custom_call_target="tpu_custom_call" | custom-call | tf_op jit(solution)/shard_map/place/pallas_call | solution.py:618
  (1 shorter events, 0.0 us)
Async XLA Ops:
  0.6 50.7 %copy-start = (s32[32]{0:T(128)S(1)}, s32[32]{0:T(128)}, u32[]{:S(2)}) copy-start(s32[32]{0:T(128)} %order_ref.1) | copy-start | bytes 388
  52.5 9.2 %collective-permute-start = (s32[208,128]{1,0:T(8,128)S(1)}, s32[208,128]{1,0:T(8,128)S(1)}, u32[]{:S(2)}, u32[]{:S(2)}) collective-permute-start(s32[208,128]{1,0:T(8,128)S(1)} %get-tuple-element.14), channel_id=1, source_target_pairs={{0,15},{1,2},{2,1},{3,4},{4,3},{5,6},{6,5},{7,8},{8,7},{9,10},{10,... | collective-permute-start | bytes 319496 | tf_op jit(solution)/shard_map/ppermute | solution.py:589
  54.8 6.9 %collective-permute-start.1 = (s32[208,128]{1,0:T(8,128)S(1)}, s32[208,128]{1,0:T(8,128)S(1)}, u32[]{:S(2)}, u32[]{:S(2)}) collective-permute-start(s32[208,128]{1,0:T(8,128)S(1)} %get-tuple-element.15), channel_id=1, source_target_pairs={{0,1},{1,0},{2,3},{3,2},{4,5},{5,4},{6,7},{7,6},{8,9},{9,8},{10,11... | collective-permute-start | bytes 319496 | tf_op jit(solution)/shard_map/ppermute | solution.py:590

commit v8 on v7

--- a/solution.py
+++ b/solution.py
@@ -328,6 +328,11 @@
     return section < row < ROWS - 1 - section
 
 
+def split(value):
+    high = value.astype(jnp.bfloat16)
+    return high, (value - high.astype(jnp.float32)).astype(jnp.bfloat16)
+
+
 def inner_kernel(state_ref, base_ref, kept_ref, middle_ref, coef_ref):
     for section in range(6):
         fields = [base_ref[6 * section + field] for field in range(6)]
@@ -355,7 +360,7 @@
 
 
 def outer_kernel(
-    state_ref, base_ref, far_ref, near_ref, kept_ref, middle_ref, cells_ref, gram_ref, edge_ref, coef_ref, sides_ref, halo_ref
+    state_ref, base_ref, far_ref, near_ref, kept_ref, middle_ref, cells_ref, gram_ref, whole_ref, edge_ref, coef_ref, sides_ref, halo_ref
 ):
     odd = odd_tile()
 
@@ -431,17 +436,14 @@
         for tile, cells in zip((0, 2), own_cells(outer)):
             for quarter, item in enumerate(cells):
                 unit = 3 * field + tile
-                cells_ref[8 * quarter : 8 * quarter + 8, 128 * unit : 128 * unit + 128] = item
+                whole_ref[8 * quarter : 8 * quarter + 8, 128 * unit : 128 * unit + 128] = item
         unit = 3 * field + 1
-        cells_ref[:, 128 * unit : 128 * unit + 128] = middle_ref[:, 128 * field : 128 * field + 128]
-    cells = cells_ref[...]
-    gram = lax.dot_general(
-        cells,
-        cells,
-        (((1,), (1,)), ((), ())),
-        precision=lax.Precision.HIGHEST,
-        preferred_element_type=jnp.float32,
-    )
+        whole_ref[:, 128 * unit : 128 * unit + 128] = middle_ref[:, 128 * field : 128 * field + 128]
+    cells = jnp.concatenate(split(whole_ref[...]), axis=0)
+    cells_ref[...] = cells
+    gram = lax.dot_general(cells, cells, (((1,), (1,)), ((), ())), preferred_element_type=jnp.float32)
+    gram = gram[:32] + gram[32:]
+    gram = gram[:, :32] + gram[:, 32:]
     compact = jnp.concatenate([gram[8 * i : 8 * i + 8] for i in range(4)], axis=1)
     for peer in range(gram_ref.shape[0]):
         gram_ref[peer] = compact
@@ -482,10 +484,11 @@
             work = work - factor * row
     work = work / jnp.sqrt(roots)
     upper_ref[...] = jnp.where(lane >= line, work, 0.0)[:, :32]
-    inverse = roll_lanes(work, -32)[:, :32]
-    ortho = jnp.dot(
-        inverse, cells_ref[...], precision=lax.Precision.HIGHEST, preferred_element_type=jnp.float32
-    )
+    inverse = jnp.where(lane < 32, roll_lanes(work, -32), 0.0)
+    high = inverse.astype(jnp.bfloat16).astype(jnp.float32)
+    factors = high + roll_lanes(high, 32) + roll_lanes(inverse - high, 64)
+    cells = jnp.concatenate([cells_ref[...], cells_ref[0:32]], axis=0)
+    ortho = jnp.dot(factors[:, :96].astype(jnp.bfloat16), cells, preferred_element_type=jnp.float32)
     level = level_of(jnp.max(jnp.abs(ortho), axis=1, keepdims=True))
     code = root_code(ortho, 1.0 / spacing(level))
     half = ortho.shape[1] // 2
@@ -554,8 +557,8 @@
 
 VEC = ("z_hi", "y")
 SPACE = ("x", "z_lo", "core")
-LINE = ("z_hi", "z_lo", "core")
-PLANE = ("x", "y")
+LINE = ("y", "core")
+PLANE = ("z_hi", "z_lo", "x")
 
 
 def body(perturbation, trajectory, step_order):
@@ -598,9 +601,10 @@
     )(state, base)
     cells, gram = call(
         outer_kernel,
-        (f32(32, 2304), f32(first, 8, 128)),
+        (jax.ShapeDtypeStruct((64, 2304), jnp.bfloat16), f32(first, 8, 128)),
         "outer",
         [
+            pltpu.VMEM((32, 2304), jnp.float32),
             pltpu.VMEM((6, 6, ROWS, 8, 128), jnp.float32),
             coefs,
             pltpu.VMEM((2, HALO_ROWS, 128), jnp.int32),

time: 111 us -> 110 us (level)
    all_to_all x1, blocking collectives: 16.7 us -> 15.5 us  [body(): gram = lax.all_to_all(gram, PLANE, split_axis=0, concat_axis=0, tiled=True)]
where the time goes in v8:
time: 110 us
  blocking collectives  90.5 us (82%)
  Pallas kernels  12 us (11%)
  starting transfers between devices  5.33 us (5%)
  waiting for transfers between devices  1.44 us (1%)
    all_to_all x1, blocking collectives, body(): held = lax.all_to_all(sent, VEC, split_axis=0, concat_axis=0, tiled=True)  47.4 us
    all_to_all x1, blocking collectives, body(): ortho = lax.all_to_all(ortho, VEC, split_axis=0, concat_axis=0, tiled=True)  16.6 us
    all_to_all x1, blocking collectives, body(): gram = lax.all_to_all(gram, PLANE, split_axis=0, concat_axis=0, tiled=True)  15.5 us
    all_to_all x1, blocking collectives, body(): gram = lax.all_to_all(gram, LINE, split_axis=0, concat_axis=0, tiled=True)  11 us
    pallas_call x1, Pallas kernels, body(): call(pack_kernel, jax.ShapeDtypeStruct((32, 8 * QUADS, 128), jnp.int32),...  3.27 us
    ppermute x1, starting transfers between devices, body(): near = lax.ppermute(near, SPACE, [(i, i ^ 1) for i in range(tiles)])  3.04 us
    pallas_call x1, Pallas kernels, body(): call(outer_kernel, (jax.ShapeDtypeStruct((64, 2304), jnp.bfloat16), f32(f...  2.49 us
    pallas_call x1, Pallas kernels, body(): call(inner_kernel, (f32(6, 6, ROWS, 8, 128), f32(32, 768)), 'inner', [plt...  2.43 us
  transfers between devices with their start and end apart: 2, of which 1 were waited for; matrix products, arithmetic and copies ran while one was open for 0% of the time, Pallas kernels for 2%

profile of v8, /device:TPU:8, one launch (start us, length us, event | category | flops | bytes accessed | tf_op | source)
XLA Modules:
  0.0 110.0 jit_solution(5675819782692641791)
XLA Ops:
  0.6 0.0 copy-start
  0.6 3.3 %pack.1 = s32[32,64,128]{2,1,0:T(8,128)} custom-call(f32[6,24,512]{2,1,0:T(8,128)} %bitcast.6, bf16[18,24,512]{2,1,0:T(8,128)(2,1)} %bitcast.5), custom_call_target="tpu_custom_call" | custom-call | tf_op jit(solution)/shard_map/pack/pallas_call | solution.py:567
  3.9 47.4 %all_to_all.20 = s32[32,64,128]{2,1,0:T(8,128)S(1)} all-to-all(s32[32,64,128]{2,1,0:T(8,128)} %pack.1), channel_id=1, replica_groups=mesh['z_hi'=4,'y'=8,'x'=4,'z_lo'=2,'core'=2] {'z_hi','y'}, dimensions={0} | all-to-all | bytes 2097152 | tf_op jit(solution)/shard_map/all_to_all | solution.py:583
  51.3 0.0 copy-done
  51.3 1.2 %unpack.1 = (f32[6,24,8,128]{3,2,1,0:T(8,128)S(1)}, f32[36,24,128]{2,1,0:T(8,128)S(1)}, s32[208,128]{1,0:T(8,128)S(1)}, s32[208,128]{1,0:T(8,128)S(1)}) custom-call(s32[32]{0:T(128)S(1)} %copy-done, s32[2048,128]{1,0:T(8,128)S(1)} %bitcast.4), custom_call_target="tpu_custom_call" | custom-call | tf_op jit(solution)/shard_map/unpack/pallas_call | solution.py:585
  52.5 2.3 %collective-permute-start = (s32[208,128]{1,0:T(8,128)S(1)}, s32[208,128]{1,0:T(8,128)S(1)}, u32[]{:S(2)}, u32[]{:S(2)}) collective-permute-start(s32[208,128]{1,0:T(8,128)S(1)} %get-tuple-element.14), channel_id=1, source_target_pairs={{0,15},{1,2},{2,1},{3,4},{4,3},{5,6},{6,5},{7,8},{8,7},{9,10},{10,... | collective-permute-start | bytes 319496 | tf_op jit(solution)/shard_map/ppermute | solution.py:592
  54.8 3.0 %collective-permute-start.1 = (s32[208,128]{1,0:T(8,128)S(1)}, s32[208,128]{1,0:T(8,128)S(1)}, u32[]{:S(2)}, u32[]{:S(2)}) collective-permute-start(s32[208,128]{1,0:T(8,128)S(1)} %get-tuple-element.15), channel_id=1, source_target_pairs={{0,1},{1,0},{2,3},{3,2},{4,5},{5,4},{6,7},{7,6},{8,9},{9,8},{10,11... | collective-permute-start | bytes 319496 | tf_op jit(solution)/shard_map/ppermute | solution.py:593
  57.9 2.4 %inner.1 = (f32[6,6,24,8,128]{4,3,2,1,0:T(8,128)S(1)}, f32[32,768]{1,0:T(8,128)S(1)}) custom-call(f32[6,24,8,128]{3,2,1,0:T(8,128)S(1)} %get-tuple-element.12.state_ref, f32[36,24,128]{2,1,0:T(8,128)S(1)} %get-tuple-element.13.base_ref), custom_call_target="tpu_custom_call" | custom-call | flops 20000000 | bytes 8000000 | tf_op jit(solution)/shard_map/inner/pallas_call | solution.py:595
  60.3 1.4 %collective-permute-done.far_ref = s32[208,128]{1,0:T(8,128)S(1)} collective-permute-done((s32[208,128]{1,0:T(8,128)S(1)}, s32[208,128]{1,0:T(8,128)S(1)}, u32[]{:S(2)}, u32[]{:S(2)}) %collective-permute-start) | collective-permute-done | bytes 106528 | tf_op jit(solution)/shard_map/ppermute | solution.py:592
  61.7 0.0 collective-permute-done.1.near_ref
  61.7 2.5 %outer.1 = (bf16[64,2304]{1,0:T(8,128)(2,1)S(1)}, f32[16,8,128]{2,1,0:T(8,128)S(1)}) custom-call(f32[6,24,8,128]{3,2,1,0:T(8,128)S(1)} %get-tuple-element.12.state_ref, f32[36,24,128]{2,1,0:T(8,128)S(1)} %get-tuple-element.13.base_ref, s32[208,128]{1,0:T(8,128)S(1)} %collective-permute-done.far_ref, s32[208,128]{1,0:T(8,128)S(1)} %collective-permute-done.1.near_ref, ...), custom_call_target="tpu_custom_call" | custom-call | tf_op jit(solution)/shard_map/outer/pallas_call | solution.py:602
  64.2 11.0 %all_to_all.21.in_ref = f32[16,8,128]{2,1,0:T(8,128)S(1)} all-to-all(f32[16,8,128]{2,1,0:T(8,128)S(1)} %get-tuple-element.18), channel_id=1, replica_groups=mesh['z_hi'=4,'y'=8,'x'=4,'z_lo'=2,'core'=2] {'y','core'}, dimensions={0} | all-to-all | bytes 131072 | tf_op jit(solution)/shard_map/all_to_all | solution.py:614
  75.3 15.5 %all_to_all.22.refs_0_ = f32[32,8,128]{2,1,0:T(8,128)S(1)} all-to-all(f32[32,8,128]{2,1,0:T(8,128)S(1)} %sums.1), channel_id=1, replica_groups=mesh['z_hi'=4,'y'=8,'x'=4,'z_lo'=2,'core'=2] {'z_hi','z_lo','x'}, dimensions={0} | all-to-all | bytes 262144 | tf_op jit(solution)/shard_map/all_to_all | solution.py:616
  90.8 1.3 %solve.1 = (s32[32,1,1280]{2,1,0:T(1,128)S(1)}, f32[32,32]{1,0:T(8,128)}) custom-call(f32[32,8,128]{2,1,0:T(8,128)S(1)} %all_to_all.22.refs_0_, bf16[64,2304]{1,0:T(8,128)(2,1)S(1)} %get-tuple-element.19.refs_1_), custom_call_target="tpu_custom_call" | custom-call | tf_op jit(solution)/shard_map/solve/pallas_call | solution.py:618
  92.1 16.6 %all_to_all.23.in_ref = s32[32,1,1280]{2,1,0:T(1,128)S(1)} all-to-all(s32[32,1,1280]{2,1,0:T(1,128)S(1)} %get-tuple-element.20), channel_id=1, replica_groups=mesh['z_hi'=4,'y'=8,'x'=4,'z_lo'=2,'core'=2] {'z_hi','y'}, dimensions={0} | all-to-all | bytes 327680 | tf_op jit(solution)/shard_map/all_to_all | solution.py:621
  108.8 1.2 %place.1 = f32[6,24,512]{2,1,0:T(8,128)} custom-call(s32[32,1,1280]{2,1,0:T(1,128)S(1)} %all_to_all.23.in_ref), custom_call_target="tpu_custom_call" | custom-call | tf_op jit(solution)/shard_map/place/pallas_call | solution.py:622
  (1 shorter events, 0.0 us)
Async XLA Ops:
  0.6 50.7 %copy-start = (s32[32]{0:T(128)S(1)}, s32[32]{0:T(128)}, u32[]{:S(2)}) copy-start(s32[32]{0:T(128)} %order_ref.1) | copy-start | bytes 388
  52.5 9.2 %collective-permute-start = (s32[208,128]{1,0:T(8,128)S(1)}, s32[208,128]{1,0:T(8,128)S(1)}, u32[]{:S(2)}, u32[]{:S(2)}) collective-permute-start(s32[208,128]{1,0:T(8,128)S(1)} %get-tuple-element.14), channel_id=1, source_target_pairs={{0,15},{1,2},{2,1},{3,4},{4,3},{5,6},{6,5},{7,8},{8,7},{9,10},{10,... | collective-permute-start | bytes 319496 | tf_op jit(solution)/shard_map/ppermute | solution.py:592
  54.8 6.9 %collective-permute-start.1 = (s32[208,128]{1,0:T(8,128)S(1)}, s32[208,128]{1,0:T(8,128)S(1)}, u32[]{:S(2)}, u32[]{:S(2)}) collective-permute-start(s32[208,128]{1,0:T(8,128)S(1)} %get-tuple-element.15), channel_id=1, source_target_pairs={{0,1},{1,0},{2,3},{3,2},{4,5},{5,4},{6,7},{7,6},{8,9},{9,8},{10,11... | collective-permute-start | bytes 319496 | tf_op jit(solution)/shard_map/ppermute | solution.py:593

commit v9 on v8

--- a/solution.py
+++ b/solution.py
@@ -411,8 +411,8 @@
                 halves(sides_ref[side, at : at + width])[field // 3].astype(jnp.float32) * (1.0 / BASE_SCALE)
                 for side in range(2)
             ]
-            gap = jnp.zeros((16 - 2 * width, 128), jnp.float32)
-            fields.append(jnp.concatenate([low, base_ref[6 * section + field], high, gap], axis=0))
+            value = base_ref[6 * section + field]
+            fields.append(jnp.concatenate([low, value[: 16 - width], value[8 + width :], high], axis=0))
         place += 3 * width
         for index, value in enumerate(coefficients(fields, 0.5 * TIME_STEP)):
             coef_ref[section % 2, index] = value
@@ -425,7 +425,9 @@
                 after(section - 1),
                 after(-1 if section < 3 else 2),
                 put,
-                lambda index, row: coef_ref[section % 2, index, pl.ds(row + width, 8, stride=0), :],
+                lambda index, row: coef_ref[
+                    section % 2, index, pl.ds(row + (width if row < 12 else 8 - width), 8, stride=0), :
+                ],
                 section % 3,
                 begin,
                 HALO,
@@ -591,7 +593,7 @@
     )(step_order, held.reshape(32 * 8 * QUADS, 128))
     far = lax.ppermute(far, SPACE, [(i, (i + 1 if i % 2 else i - 1) % tiles) for i in range(tiles)])
     near = lax.ppermute(near, SPACE, [(i, i ^ 1) for i in range(tiles)])
-    coefs = pltpu.VMEM((2, COEF, ROWS + 16, 128), jnp.float32)
+    coefs = pltpu.VMEM((2, COEF, 32, 128), jnp.float32)
     kept, middle = call(
         inner_kernel,
         (f32(6, 6, ROWS, 8, 128), f32(32, 768)),

time: 110 us -> 110 us (level)
  no operation moved by 1% of the time
where the time goes in v9:
time: 110 us
  blocking collectives  90.5 us (82%)
  Pallas kernels  11.9 us (11%)
  starting transfers between devices  5.33 us (5%)
  waiting for transfers between devices  1.44 us (1%)
    all_to_all x1, blocking collectives, body(): held = lax.all_to_all(sent, VEC, split_axis=0, concat_axis=0, tiled=True)  47.4 us
    all_to_all x1, blocking collectives, body(): ortho = lax.all_to_all(ortho, VEC, split_axis=0, concat_axis=0, tiled=True)  16.6 us
    all_to_all x1, blocking collectives, body(): gram = lax.all_to_all(gram, PLANE, split_axis=0, concat_axis=0, tiled=True)  15.5 us
    all_to_all x1, blocking collectives, body(): gram = lax.all_to_all(gram, LINE, split_axis=0, concat_axis=0, tiled=True)  11 us
    pallas_call x1, Pallas kernels, body(): call(pack_kernel, jax.ShapeDtypeStruct((32, 8 * QUADS, 128), jnp.int32),...  3.27 us
    ppermute x1, starting transfers between devices, body(): near = lax.ppermute(near, SPACE, [(i, i ^ 1) for i in range(tiles)])  3.04 us
    pallas_call x1, Pallas kernels, body(): call(outer_kernel, (jax.ShapeDtypeStruct((64, 2304), jnp.bfloat16), f32(f...  2.47 us
    pallas_call x1, Pallas kernels, body(): call(inner_kernel, (f32(6, 6, ROWS, 8, 128), f32(32, 768)), 'inner', [plt...  2.43 us
  transfers between devices with their start and end apart: 2, of which 1 were waited for; matrix products, arithmetic and copies ran while one was open for 0% of the time, Pallas kernels for 2%

profile of v9, /device:TPU:8, one launch (start us, length us, event | category | flops | bytes accessed | tf_op | source)
XLA Modules:
  0.0 110.0 jit_solution(5903771634007874204)
XLA Ops:
  0.6 0.0 copy-start
  0.6 3.3 %pack.1 = s32[32,64,128]{2,1,0:T(8,128)} custom-call(f32[6,24,512]{2,1,0:T(8,128)} %bitcast.6, bf16[18,24,512]{2,1,0:T(8,128)(2,1)} %bitcast.5), custom_call_target="tpu_custom_call" | custom-call | tf_op jit(solution)/shard_map/pack/pallas_call | solution.py:569
  3.9 47.4 %all_to_all.20 = s32[32,64,128]{2,1,0:T(8,128)S(1)} all-to-all(s32[32,64,128]{2,1,0:T(8,128)} %pack.1), channel_id=1, replica_groups=mesh['z_hi'=4,'y'=8,'x'=4,'z_lo'=2,'core'=2] {'z_hi','y'}, dimensions={0} | all-to-all | bytes 2097152 | tf_op jit(solution)/shard_map/all_to_all | solution.py:585
  51.3 0.0 copy-done
  51.3 1.2 %unpack.1 = (f32[6,24,8,128]{3,2,1,0:T(8,128)S(1)}, f32[36,24,128]{2,1,0:T(8,128)S(1)}, s32[208,128]{1,0:T(8,128)S(1)}, s32[208,128]{1,0:T(8,128)S(1)}) custom-call(s32[32]{0:T(128)S(1)} %copy-done, s32[2048,128]{1,0:T(8,128)S(1)} %bitcast.4), custom_call_target="tpu_custom_call" | custom-call | tf_op jit(solution)/shard_map/unpack/pallas_call | solution.py:587
  52.5 2.3 %collective-permute-start = (s32[208,128]{1,0:T(8,128)S(1)}, s32[208,128]{1,0:T(8,128)S(1)}, u32[]{:S(2)}, u32[]{:S(2)}) collective-permute-start(s32[208,128]{1,0:T(8,128)S(1)} %get-tuple-element.14), channel_id=1, source_target_pairs={{0,15},{1,2},{2,1},{3,4},{4,3},{5,6},{6,5},{7,8},{8,7},{9,10},{10,... | collective-permute-start | bytes 319496 | tf_op jit(solution)/shard_map/ppermute | solution.py:594
  54.8 3.0 %collective-permute-start.1 = (s32[208,128]{1,0:T(8,128)S(1)}, s32[208,128]{1,0:T(8,128)S(1)}, u32[]{:S(2)}, u32[]{:S(2)}) collective-permute-start(s32[208,128]{1,0:T(8,128)S(1)} %get-tuple-element.15), channel_id=1, source_target_pairs={{0,1},{1,0},{2,3},{3,2},{4,5},{5,4},{6,7},{7,6},{8,9},{9,8},{10,11... | collective-permute-start | bytes 319496 | tf_op jit(solution)/shard_map/ppermute | solution.py:595
  57.9 2.4 %inner.1 = (f32[6,6,24,8,128]{4,3,2,1,0:T(8,128)S(1)}, f32[32,768]{1,0:T(8,128)S(1)}) custom-call(f32[6,24,8,128]{3,2,1,0:T(8,128)S(1)} %get-tuple-element.12.state_ref, f32[36,24,128]{2,1,0:T(8,128)S(1)} %get-tuple-element.13.base_ref), custom_call_target="tpu_custom_call" | custom-call | flops 20000000 | bytes 8000000 | tf_op jit(solution)/shard_map/inner/pallas_call | solution.py:597
  60.3 1.4 %collective-permute-done.far_ref = s32[208,128]{1,0:T(8,128)S(1)} collective-permute-done((s32[208,128]{1,0:T(8,128)S(1)}, s32[208,128]{1,0:T(8,128)S(1)}, u32[]{:S(2)}, u32[]{:S(2)}) %collective-permute-start) | collective-permute-done | bytes 106528 | tf_op jit(solution)/shard_map/ppermute | solution.py:594
  61.7 0.0 collective-permute-done.1.near_ref
  61.7 2.5 %outer.1 = (bf16[64,2304]{1,0:T(8,128)(2,1)S(1)}, f32[16,8,128]{2,1,0:T(8,128)S(1)}) custom-call(f32[6,24,8,128]{3,2,1,0:T(8,128)S(1)} %get-tuple-element.12.state_ref, f32[36,24,128]{2,1,0:T(8,128)S(1)} %get-tuple-element.13.base_ref, s32[208,128]{1,0:T(8,128)S(1)} %collective-permute-done.far_ref, s32[208,128]{1,0:T(8,128)S(1)} %collective-permute-done.1.near_ref, ...), custom_call_target="tpu_custom_call" | custom-call | tf_op jit(solution)/shard_map/outer/pallas_call | solution.py:604
  64.2 11.0 %all_to_all.21.in_ref = f32[16,8,128]{2,1,0:T(8,128)S(1)} all-to-all(f32[16,8,128]{2,1,0:T(8,128)S(1)} %get-tuple-element.18), channel_id=1, replica_groups=mesh['z_hi'=4,'y'=8,'x'=4,'z_lo'=2,'core'=2] {'y','core'}, dimensions={0} | all-to-all | bytes 131072 | tf_op jit(solution)/shard_map/all_to_all | solution.py:616
  75.3 15.5 %all_to_all.22.refs_0_ = f32[32,8,128]{2,1,0:T(8,128)S(1)} all-to-all(f32[32,8,128]{2,1,0:T(8,128)S(1)} %sums.1), channel_id=1, replica_groups=mesh['z_hi'=4,'y'=8,'x'=4,'z_lo'=2,'core'=2] {'z_hi','z_lo','x'}, dimensions={0} | all-to-all | bytes 262144 | tf_op jit(solution)/shard_map/all_to_all | solution.py:618
  90.8 1.3 %solve.1 = (s32[32,1,1280]{2,1,0:T(1,128)S(1)}, f32[32,32]{1,0:T(8,128)}) custom-call(f32[32,8,128]{2,1,0:T(8,128)S(1)} %all_to_all.22.refs_0_, bf16[64,2304]{1,0:T(8,128)(2,1)S(1)} %get-tuple-element.19.refs_1_), custom_call_target="tpu_custom_call" | custom-call | tf_op jit(solution)/shard_map/solve/pallas_call | solution.py:620
  92.1 16.6 %all_to_all.23.in_ref = s32[32,1,1280]{2,1,0:T(1,128)S(1)} all-to-all(s32[32,1,1280]{2,1,0:T(1,128)S(1)} %get-tuple-element.20), channel_id=1, replica_groups=mesh['z_hi'=4,'y'=8,'x'=4,'z_lo'=2,'core'=2] {'z_hi','y'}, dimensions={0} | all-to-all | bytes 327680 | tf_op jit(solution)/shard_map/all_to_all | solution.py:623
  108.8 1.2 %place.1 = f32[6,24,512]{2,1,0:T(8,128)} custom-call(s32[32,1,1280]{2,1,0:T(1,128)S(1)} %all_to_all.23.in_ref), custom_call_target="tpu_custom_call" | custom-call | tf_op jit(solution)/shard_map/place/pallas_call | solution.py:624
  (1 shorter events, 0.0 us)
Async XLA Ops:
  0.6 50.7 %copy-start = (s32[32]{0:T(128)S(1)}, s32[32]{0:T(128)}, u32[]{:S(2)}) copy-start(s32[32]{0:T(128)} %order_ref.1) | copy-start | bytes 388
  52.5 9.2 %collective-permute-start = (s32[208,128]{1,0:T(8,128)S(1)}, s32[208,128]{1,0:T(8,128)S(1)}, u32[]{:S(2)}, u32[]{:S(2)}) collective-permute-start(s32[208,128]{1,0:T(8,128)S(1)} %get-tuple-element.14), channel_id=1, source_target_pairs={{0,15},{1,2},{2,1},{3,4},{4,3},{5,6},{6,5},{7,8},{8,7},{9,10},{10,... | collective-permute-start | bytes 319496 | tf_op jit(solution)/shard_map/ppermute | solution.py:594
  54.8 6.9 %collective-permute-start.1 = (s32[208,128]{1,0:T(8,128)S(1)}, s32[208,128]{1,0:T(8,128)S(1)}, u32[]{:S(2)}, u32[]{:S(2)}) collective-permute-start(s32[208,128]{1,0:T(8,128)S(1)} %get-tuple-element.15), channel_id=1, source_target_pairs={{0,1},{1,0},{2,3},{3,2},{4,5},{5,4},{6,7},{7,6},{8,9},{9,8},{10,11... | collective-permute-start | bytes 319496 | tf_op jit(solution)/shard_map/ppermute | solution.py:595
